TPU v7x, 128 devices: a whole 4x4x4 slice. The times are simulated.
128 devices in a mesh: px: 16 (over y, x), py: 8 (over z, core).
Axes of the slice: x: 4, y: 4, z: 4, core: 2. Of those that a mesh axis runs over, the one named last changes fastest.
Arguments:
- block_vectors: float32 [393216, 256], P(('px', 'py')), may hold values from -6 to 6
- stiff_tiles: float32 [3072, 12, 128, 128], P(('px', 'py')), may hold values from -0.15625 to 0.15625
- col_index: int32 [3072, 12], P(('px', 'py')), may hold values from 0 to 39
- send_lists: int32 [128, 4, 4], P(('px', 'py')), may hold values from 0 to 23
- send_counts: int32 [128, 4], P(('px', 'py')), may hold values from 1 to 4, as said below
- part_blocks: int32 [128], P(('px', 'py')), may hold values from 12 to 24, as said below
Outputs:
- basis: float32 [393216, 256], P(('px', 'py'))
- upper_factor: float32 [256, 256], replicated
Inputs may be any that keep to these rules, and one draw needn't show every extreme that they name: `send_counts`: in every draw some partitions send full lists of 4 blocks in some direction. `part_blocks`: in every draw some partitions have all 24 blocks live.
All inputs are finite; a program needn't handle non-finite values.
Results may differ from a plain program's by a relative error of at most 0.000053.
Values sent between devices are 32-bit elements; how exact they have to be, the bound alone decides.
No kernel may reach another device: no remote copies, remote signals or barrier semaphores. Data moves between devices by JAX's collectives and lax.ppermute only.
A program may use at most 192 MiB of HBM per device.

v0:
```python
import jax
import jax.numpy as jnp
from jax import lax
from jax.sharding import PartitionSpec as P


def shifted(block, axis, distance):
    devices = range(lax.axis_size(axis))
    route = [(i - distance, i) for i in devices if i - distance in devices]
    return lax.ppermute(block, axis, route)


def pack_ghosts(own_blocks, send_lists, send_counts, direc):
    chosen = jnp.take(own_blocks, send_lists[0, direc], axis=0)
    slots = jnp.arange(send_lists.shape[2], dtype=jnp.int32)
    alive = (slots < send_counts[0, direc]).astype(jnp.float32)
    return chosen * alive[:, None, None]


def tile_sum(source, columns, valid, stiff_tiles):
    hp = lax.Precision.HIGHEST
    nbd = stiff_tiles.shape[0]
    tiles_row = stiff_tiles.shape[1]
    rows_blk = stiff_tiles.shape[2]
    width = source.shape[2]

    def add_tile(step, total):
        operand = jnp.take(source, columns[:, step], axis=0) * valid[:, step][:, None, None]
        tile = lax.dynamic_index_in_dim(stiff_tiles, step, 1, keepdims=False)
        return total + jnp.einsum("bij,bjk->bik", tile, operand, precision=hp)

    return lax.fori_loop(0, tiles_row, add_tile, jnp.zeros((nbd, rows_blk, width), jnp.float32))


def body(block_vectors, stiff_tiles, col_index, send_lists, send_counts, part_blocks):
    hp = lax.Precision.HIGHEST
    nbd = stiff_tiles.shape[0]
    rows_blk = stiff_tiles.shape[2]
    width = block_vectors.shape[1]
    own_blocks = block_vectors.reshape(nbd, rows_blk, width)
    from_low_px = shifted(pack_ghosts(own_blocks, send_lists, send_counts, 0), "px", 1)
    from_high_px = shifted(pack_ghosts(own_blocks, send_lists, send_counts, 1), "px", -1)
    from_low_py = shifted(pack_ghosts(own_blocks, send_lists, send_counts, 2), "py", 1)
    from_high_py = shifted(pack_ghosts(own_blocks, send_lists, send_counts, 3), "py", -1)
    table = jnp.concatenate(
        [own_blocks, from_low_px, from_high_px, from_low_py, from_high_py], axis=0
    )
    everywhere = jnp.ones(col_index.shape, jnp.float32)
    applied = tile_sum(table, col_index, everywhere, stiff_tiles)
    keep = (jnp.arange(nbd, dtype=jnp.int32) < part_blocks[0]).astype(jnp.float32)
    applied = (applied * keep[:, None, None]).reshape(nbd * rows_blk, width)
    local_gram = jnp.dot(applied.T, applied, precision=hp, preferred_element_type=jnp.float32)
    total_gram = lax.psum(local_gram, ("px", "py"))
    all_rows = nbd * rows_blk * lax.axis_size(("px", "py"))
    gram = total_gram / all_rows
    lower = jnp.linalg.cholesky(gram)
    inverse_lower = lax.linalg.triangular_solve(
        lower, jnp.eye(width, dtype=jnp.float32), left_side=True, lower=True
    )
    inverse_upper = inverse_lower.T
    basis = jnp.dot(applied, inverse_upper, precision=hp, preferred_element_type=jnp.float32)
    return (basis, lower.T)


def solution(mesh):
    placed = (
        P(("px", "py"), None),
        P(("px", "py"), None, None, None),
        P(("px", "py"), None),
        P(("px", "py"), None, None),
        P(("px", "py"), None),
        P(("px", "py")),
    )
    return jax.shard_map(
        body, mesh=mesh, in_specs=placed, out_specs=(P(("px", "py"), None), P()), check_vma=False
    )
```

profile of v0, /device:TPU:1, one launch (start us, length us, event | category | flops | bytes accessed | tf_op | source)
XLA Modules:
  0.0 424.1 jit_solution(267676593862715053)
XLA Ops:
  10.2 3.3 gather_fusion.1
  15.5 4.8 %collective-permute-start = (f32[4,128,256]{2,1,0:T(8,128)}, f32[4,128,256]{2,1,0:T(8,128)}, u32[]{:S(2)}, u32[]{:S(2)}) collective-permute-start(f32[4,128,256]{2,1,0:T(8,128)} %select_multiply_fusion.3), channel_id=1, source_target_pairs={{0,8},{8,16},{16,24},{24,32},{32,40},{40,48},{48,56},{56,64},{64,7... | collective-permute-start | bytes 1572872 | tf_op jit(solution)/shard_map/ppermute | solution.py:10
  20.3 3.3 gather_fusion.2
  31.4 4.4 %collective-permute-start.2 = (f32[4,128,256]{2,1,0:T(8,128)}, f32[4,128,256]{2,1,0:T(8,128)}, u32[]{:S(2)}, u32[]{:S(2)}) collective-permute-start(f32[4,128,256]{2,1,0:T(8,128)} %select_multiply_fusion.1), channel_id=1, source_target_pairs={{0,1},{1,2},{2,3},{3,4},{4,5},{5,6},{6,7},{8,9},{9,10},{10,11},{11... | collective-permute-start | bytes 1572872 | tf_op jit(solution)/shard_map/ppermute | solution.py:10
  52.4 132.9 %while.16 = (s32[]{:T(128)}, f32[24,128,256]{2,1,0:T(8,128)}, f32[24,12,128,128]{3,2,1,0:T(8,128)}, s32[24,12]{0,1:T(8,128)}, f32[40,128,256]{2,1,0:T(8,128)}, /*index=5*/s32[]{:T(128)}, s32[]{:T(128)}) while((s32[]{:T(128)}, f32[24,128,256]{2,1,0:T(8,128)}, f32[24,12,128,128]{3,2,1,0:T(8,128)}, s32[24,12]{0,1:T(8,128)}, ...), condition=%wide.region_1.3_spmd.clone, body=%wide.region_0.0_spmd.clone.sunk | while | flops 1210320000 | bytes 17306636 | solution.py:32
  53.2 3.2 gather_fusion
  56.4 6.3 %select_add_fusion.2 = f32[24,128,256]{2,1,0:T(8,128)} fusion(f32[24,128,256]{2,1,0:T(8,128)} %get-tuple-element.252, f32[24,128,256]{2,1,0:T(8,128)S(1)} %gather_fusion, f32[24,12,128,128]{3,2,1,0:T(8,128)} %get-tuple-element.260, s32[]{:T(128)} %get-tuple-element.251, pred[24]{0:T(512)(128)(4,1)S(1)} %get-tuple-element.243, pred[]{:T(512)S(6)} %compare.26), kind=kOutput, calls=%fused_computation.7.clone.1 | convolution fusion | flops 1210318848 | bytes 11010585 | tf_op jit(solution)/shard_map/while/body/eval_jaxpr/bij,bjk->bik/dot_general | solution.py:30
  63.4 3.2 gather_fusion
  66.6 7.2 %select_add_fusion.2 = f32[24,128,256]{2,1,0:T(8,128)} fusion(f32[24,128,256]{2,1,0:T(8,128)} %get-tuple-element.252, f32[24,128,256]{2,1,0:T(8,128)S(1)} %gather_fusion, f32[24,12,128,128]{3,2,1,0:T(8,128)} %get-tuple-element.260, s32[]{:T(128)} %get-tuple-element.251, pred[24]{0:T(512)(128)(4,1)S(1)} %get-tuple-element.243, pred[]{:T(512)S(6)} %compare.26), kind=kOutput, calls=%fused_computation.7.clone.1 | convolution fusion | flops 1210318848 | bytes 11010585 | tf_op jit(solution)/shard_map/while/body/eval_jaxpr/bij,bjk->bik/dot_general | solution.py:30
  74.5 3.2 gather_fusion
  77.8 7.2 %select_add_fusion.2 = f32[24,128,256]{2,1,0:T(8,128)} fusion(f32[24,128,256]{2,1,0:T(8,128)} %get-tuple-element.252, f32[24,128,256]{2,1,0:T(8,128)S(1)} %gather_fusion, f32[24,12,128,128]{3,2,1,0:T(8,128)} %get-tuple-element.260, s32[]{:T(128)} %get-tuple-element.251, pred[24]{0:T(512)(128)(4,1)S(1)} %get-tuple-element.243, pred[]{:T(512)S(6)} %compare.26), kind=kOutput, calls=%fused_computation.7.clone.1 | convolution fusion | flops 1210318848 | bytes 11010585 | tf_op jit(solution)/shard_map/while/body/eval_jaxpr/bij,bjk->bik/dot_general | solution.py:30
  85.7 3.2 gather_fusion
  88.9 7.2 %select_add_fusion.2 = f32[24,128,256]{2,1,0:T(8,128)} fusion(f32[24,128,256]{2,1,0:T(8,128)} %get-tuple-element.252, f32[24,128,256]{2,1,0:T(8,128)S(1)} %gather_fusion, f32[24,12,128,128]{3,2,1,0:T(8,128)} %get-tuple-element.260, s32[]{:T(128)} %get-tuple-element.251, pred[24]{0:T(512)(128)(4,1)S(1)} %get-tuple-element.243, pred[]{:T(512)S(6)} %compare.26), kind=kOutput, calls=%fused_computation.7.clone.1 | convolution fusion | flops 1210318848 | bytes 11010585 | tf_op jit(solution)/shard_map/while/body/eval_jaxpr/bij,bjk->bik/dot_general | solution.py:30
  96.8 3.2 gather_fusion
  100.1 7.2 %select_add_fusion.2 = f32[24,128,256]{2,1,0:T(8,128)} fusion(f32[24,128,256]{2,1,0:T(8,128)} %get-tuple-element.252, f32[24,128,256]{2,1,0:T(8,128)S(1)} %gather_fusion, f32[24,12,128,128]{3,2,1,0:T(8,128)} %get-tuple-element.260, s32[]{:T(128)} %get-tuple-element.251, pred[24]{0:T(512)(128)(4,1)S(1)} %get-tuple-element.243, pred[]{:T(512)S(6)} %compare.26), kind=kOutput, calls=%fused_computation.7.clone.1 | convolution fusion | flops 1210318848 | bytes 11010585 | tf_op jit(solution)/shard_map/while/body/eval_jaxpr/bij,bjk->bik/dot_general | solution.py:30
  108.0 3.2 gather_fusion
  111.2 7.2 %select_add_fusion.2 = f32[24,128,256]{2,1,0:T(8,128)} fusion(f32[24,128,256]{2,1,0:T(8,128)} %get-tuple-element.252, f32[24,128,256]{2,1,0:T(8,128)S(1)} %gather_fusion, f32[24,12,128,128]{3,2,1,0:T(8,128)} %get-tuple-element.260, s32[]{:T(128)} %get-tuple-element.251, pred[24]{0:T(512)(128)(4,1)S(1)} %get-tuple-element.243, pred[]{:T(512)S(6)} %compare.26), kind=kOutput, calls=%fused_computation.7.clone.1 | convolution fusion | flops 1210318848 | bytes 11010585 | tf_op jit(solution)/shard_map/while/body/eval_jaxpr/bij,bjk->bik/dot_general | solution.py:30
  119.1 3.2 gather_fusion
  122.4 7.2 %select_add_fusion.2 = f32[24,128,256]{2,1,0:T(8,128)} fusion(f32[24,128,256]{2,1,0:T(8,128)} %get-tuple-element.252, f32[24,128,256]{2,1,0:T(8,128)S(1)} %gather_fusion, f32[24,12,128,128]{3,2,1,0:T(8,128)} %get-tuple-element.260, s32[]{:T(128)} %get-tuple-element.251, pred[24]{0:T(512)(128)(4,1)S(1)} %get-tuple-element.243, pred[]{:T(512)S(6)} %compare.26), kind=kOutput, calls=%fused_computation.7.clone.1 | convolution fusion | flops 1210318848 | bytes 11010585 | tf_op jit(solution)/shard_map/while/body/eval_jaxpr/bij,bjk->bik/dot_general | solution.py:30
  133.6 7.2 %select_add_fusion.2 = f32[24,128,256]{2,1,0:T(8,128)} fusion(f32[24,128,256]{2,1,0:T(8,128)} %get-tuple-element.252, f32[24,128,256]{2,1,0:T(8,128)S(1)} %gather_fusion, f32[24,12,128,128]{3,2,1,0:T(8,128)} %get-tuple-element.260, s32[]{:T(128)} %get-tuple-element.251, pred[24]{0:T(512)(128)(4,1)S(1)} %get-tuple-element.243, pred[]{:T(512)S(6)} %compare.26), kind=kOutput, calls=%fused_computation.7.clone.1 | convolution fusion | flops 1210318848 | bytes 11010585 | tf_op jit(solution)/shard_map/while/body/eval_jaxpr/bij,bjk->bik/dot_general | solution.py:30
  144.7 7.2 %select_add_fusion.2 = f32[24,128,256]{2,1,0:T(8,128)} fusion(f32[24,128,256]{2,1,0:T(8,128)} %get-tuple-element.252, f32[24,128,256]{2,1,0:T(8,128)S(1)} %gather_fusion, f32[24,12,128,128]{3,2,1,0:T(8,128)} %get-tuple-element.260, s32[]{:T(128)} %get-tuple-element.251, pred[24]{0:T(512)(128)(4,1)S(1)} %get-tuple-element.243, pred[]{:T(512)S(6)} %compare.26), kind=kOutput, calls=%fused_computation.7.clone.1 | convolution fusion | flops 1210318848 | bytes 11010585 | tf_op jit(solution)/shard_map/while/body/eval_jaxpr/bij,bjk->bik/dot_general | solution.py:30
  155.9 7.2 %select_add_fusion.2 = f32[24,128,256]{2,1,0:T(8,128)} fusion(f32[24,128,256]{2,1,0:T(8,128)} %get-tuple-element.252, f32[24,128,256]{2,1,0:T(8,128)S(1)} %gather_fusion, f32[24,12,128,128]{3,2,1,0:T(8,128)} %get-tuple-element.260, s32[]{:T(128)} %get-tuple-element.251, pred[24]{0:T(512)(128)(4,1)S(1)} %get-tuple-element.243, pred[]{:T(512)S(6)} %compare.26), kind=kOutput, calls=%fused_computation.7.clone.1 | convolution fusion | flops 1210318848 | bytes 11010585 | tf_op jit(solution)/shard_map/while/body/eval_jaxpr/bij,bjk->bik/dot_general | solution.py:30
  167.0 7.2 %select_add_fusion.2 = f32[24,128,256]{2,1,0:T(8,128)} fusion(f32[24,128,256]{2,1,0:T(8,128)} %get-tuple-element.252, f32[24,128,256]{2,1,0:T(8,128)S(1)} %gather_fusion, f32[24,12,128,128]{3,2,1,0:T(8,128)} %get-tuple-element.260, s32[]{:T(128)} %get-tuple-element.251, pred[24]{0:T(512)(128)(4,1)S(1)} %get-tuple-element.243, pred[]{:T(512)S(6)} %compare.26), kind=kOutput, calls=%fused_computation.7.clone.1 | convolution fusion | flops 1210318848 | bytes 11010585 | tf_op jit(solution)/shard_map/while/body/eval_jaxpr/bij,bjk->bik/dot_general | solution.py:30
  178.2 7.2 %select_add_fusion.2 = f32[24,128,256]{2,1,0:T(8,128)} fusion(f32[24,128,256]{2,1,0:T(8,128)} %get-tuple-element.252, f32[24,128,256]{2,1,0:T(8,128)S(1)} %gather_fusion, f32[24,12,128,128]{3,2,1,0:T(8,128)} %get-tuple-element.260, s32[]{:T(128)} %get-tuple-element.251, pred[24]{0:T(512)(128)(4,1)S(1)} %get-tuple-element.243, pred[]{:T(512)S(6)} %compare.26), kind=kOutput, calls=%fused_computation.7.clone.1 | convolution fusion | flops 1210318848 | bytes 11010585 | tf_op jit(solution)/shard_map/while/body/eval_jaxpr/bij,bjk->bik/dot_general | solution.py:30
  187.8 5.8 %convolution_bitcast_fusion = f32[256,256]{0,1:T(8,128)} fusion(f32[24,128,256]{2,1,0:T(8,128)S(1)} %broadcast_multiply_fusion), kind=kOutput, calls=%fused_computation.20 | convolution fusion | flops 2415919104 | bytes 3407872 | tf_op jit(solution)/shard_map/dot_general | solution.py:52
  194.3 143.1 %all-reduce.3.cloned.1.call-done = f32[256,256]{0,1:T(8,128)} async-done(((f32[256,256]{0,1:T(8,128)}), f32[256,256]{0,1:T(8,128)}) %all-reduce.3.cloned.1.call-update) | async-done | bytes 262160 | tf_op jit(solution)/shard_map/psum | solution.py:53
  341.8 11.7 %cholesky.50 = f32[128,128]{1,0:T(8,128)S(1)} custom-call(f32[128,128]{1,0:T(8,128)S(1)} %cholesky.118), custom_call_target="Cholesky" | custom-call | tf_op jit(solution)/shard_map/jit(cholesky)/cholesky | solution.py:56
  353.6 9.8 %custom-call.14 = f32[1,128,128]{1,2,0:T(8,128)S(1)} custom-call(f32[1,128,128]{2,1,0:T(8,128)S(1)} %get-tuple-element.166), custom_call_target="InvertDiagBlocksLowerTriangular" | custom-call | tf_op jit(solution)/shard_map/jit(cholesky)/cholesky | solution.py:56
  365.6 11.9 %cholesky.105 = f32[128,128]{1,0:T(8,128)S(1)} custom-call(f32[128,128]{1,0:T(8,128)S(1)} %convolution_subtract_fusion.1), custom_call_target="Cholesky" | custom-call | tf_op jit(solution)/shard_map/jit(cholesky)/cholesky | solution.py:56
  381.8 5.0 %while.15 = (s32[]{:T(128)}, f32[256,256]{1,0:T(8,128)S(1)}, s32[2,2]{1,0:T(2,128)S(1)}, f32[2,128,128]{2,1,0:T(8,128)}, s32[]{:T(128)}) while((s32[]{:T(128)}, f32[256,256]{1,0:T(8,128)S(1)}, s32[2,2]{1,0:T(2,128)S(1)}, f32[2,128,128]{2,1,0:T(8,128)}, s32[]{:T(128)}) %tuple.77), condition=%wide.while_cond, body=%wide.while_body.sunk | while | flops 2 | bytes 132705 | solution.py:57
  386.8 21.1 %custom-call.15 = f32[2,128,128]{1,2,0:T(8,128)} custom-call(f32[2,128,128]{2,1,0:T(8,128)} %get-tuple-element.105), custom_call_target="InvertDiagBlocksLowerTriangular" | custom-call | tf_op jit(solution)/shard_map/triangular_solve | solution.py:57
  413.0 4.3 %fusion.10 = f32[3072,256]{1,0:T(8,128)} fusion(f32[3072,256]{1,0:T(8,128)S(1)} %bitcast.72, f32[128,256]{1,0:T(8,128)S(1)} %fusion.20, f32[128,256]{1,0:T(8,128)S(1)} %fusion.17), kind=kOutput, calls=%fused_computation.27 | convolution fusion | flops 2415984640 | bytes 6553600 | tf_op jit(solution)/shard_map/dot_general | solution.py:61
  (92 shorter events, 76.3 us)
Async XLA Ops:
  7.2 20.3 %copy-start = (f32[3072,256]{1,0:T(8,128)S(1)}, f32[3072,256]{1,0:T(8,128)}, u32[]{:S(2)}) copy-start(f32[3072,256]{1,0:T(8,128)} %param.10) | copy-start | bytes 9437188
  7.2 330.2 %all-reduce.3.cloned.1.call-start = ((), (), s32[]{:S(2)}) async-start(), calls=%async_computation | async-start | bytes 524288 | tf_op jit(solution)/shard_map/psum | solution.py:53
  15.5 28.8 %collective-permute-start = (f32[4,128,256]{2,1,0:T(8,128)}, f32[4,128,256]{2,1,0:T(8,128)}, u32[]{:S(2)}, u32[]{:S(2)}) collective-permute-start(f32[4,128,256]{2,1,0:T(8,128)} %select_multiply_fusion.3), channel_id=1, source_target_pairs={{0,8},{8,16},{16,24},{24,32},{32,40},{40,48},{48,56},{56,64},{64,7... | collective-permute-start | bytes 1572872 | tf_op jit(solution)/shard_map/ppermute | solution.py:10
  26.1 20.0 %collective-permute-start.1 = (f32[4,128,256]{2,1,0:T(8,128)}, f32[4,128,256]{2,1,0:T(8,128)}, u32[]{:S(2)}, u32[]{:S(2)}) collective-permute-start(f32[4,128,256]{2,1,0:T(8,128)} %select_multiply_fusion.2), channel_id=1, source_target_pairs={{8,0},{16,8},{24,16},{32,24},{40,32},{48,40},{56,48},{64,56},{72,6... | collective-permute-start | bytes 1572872 | tf_op jit(solution)/shard_map/ppermute | solution.py:10
  31.4 16.6 %collective-permute-start.2 = (f32[4,128,256]{2,1,0:T(8,128)}, f32[4,128,256]{2,1,0:T(8,128)}, u32[]{:S(2)}, u32[]{:S(2)}) collective-permute-start(f32[4,128,256]{2,1,0:T(8,128)} %select_multiply_fusion.1), channel_id=1, source_target_pairs={{0,1},{1,2},{2,3},{3,4},{4,5},{5,6},{6,7},{8,9},{9,10},{10,11},{11... | collective-permute-start | bytes 1572872 | tf_op jit(solution)/shard_map/ppermute | solution.py:10
  39.8 10.8 %collective-permute-start.3 = (f32[4,128,256]{2,1,0:T(8,128)}, f32[4,128,256]{2,1,0:T(8,128)}, u32[]{:S(2)}, u32[]{:S(2)}) collective-permute-start(f32[4,128,256]{2,1,0:T(8,128)} %select_multiply_fusion), channel_id=1, source_target_pairs={{1,0},{2,1},{3,2},{4,3},{5,4},{6,5},{7,6},{9,8},{10,9},{11,10},{12... | collective-permute-start | bytes 1572872 | tf_op jit(solution)/shard_map/ppermute | solution.py:10
  341.1 0.7 copy-start.2
  377.5 2.5 copy-start.1
Sparse Core Ops, SparseCore 0:
  193.7 143.6 all-reduce.2
where the time goes:
time: 426 us; the launch traced here: 424 us
  waiting for transfers between devices  144 us (34%)
  matrix products  101 us (24%)
  other arithmetic  82.9 us (19%)
  local copies, waits for them, and re-layouts  67.7 us (16%)
  between operations  16.1 us (4%)
  starting transfers between devices  12.4 us (3%)
    psum x1, waiting for transfers between devices, body(): total_gram = lax.psum(local_gram, ('px', 'py'))  143 us
    dot_general x12, matrix products, add_tile(): return total + jnp.einsum('bij,bjk->bik', tile, operand, precision=hp)  85.5 us
    gather x12, local copies, waits for them, and re-layouts, add_tile(): jnp.take(source, columns[:, step], axis=0) * valid[:, step][:, None, None]  38.8 us
    another operation x7, other arithmetic, body(): lower = jnp.linalg.cholesky(gram)  34.7 us
    another operation x2, other arithmetic, body(): lax.linalg.triangular_solve(lower, jnp.eye(width, dtype=jnp.float32), lef...  21.1 us
    ppermute x4, starting transfers between devices, shifted(): return lax.ppermute(block, axis, route)  12.4 us
    unnamed x11, local copies, waits for them, and re-layouts  10.1 us
    gather x4, local copies, waits for them, and re-layouts, pack_ghosts(): chosen = jnp.take(own_blocks, send_lists[0, direc], axis=0)  9.27 us
  transfers between devices with their start and end apart: 5, of which 2 were waited for; matrix products, arithmetic and copies ran while one was open for 5% of the time, Pallas kernels for 0%

commit v1 on v0

v1 whole, which is shorter than its diff:
```python
import functools
import itertools

import jax
import jax.numpy as jnp
from jax import lax
from jax.experimental import pallas as pl
from jax.experimental.pallas import tpu as pltpu
from jax.sharding import PartitionSpec as P

AXES = ("px", "py")
SIDE = 4
BS = 128
K = 256
NBD = 24
TPR = 12
GMAX = 4
NROWS = 393216
HALF = 136
F32 = jnp.float32
BF16 = jnp.bfloat16
MB = 1 << 20


def device_at(x, y, z, core):
    return (y * SIDE + x) * 8 + z * 2 + core


def route(move):
    places = itertools.product(range(SIDE), range(SIDE), range(SIDE), range(2))
    return [(device_at(*p), device_at(*move(*p))) for p in places]


def pair_route(dim, odd):
    def move(x, y, z, core):
        at = [x, y, z]
        v = at[dim]
        if odd:
            at[dim] = (v - 1) % SIDE if v % 2 == 0 else (v + 1) % SIDE
        else:
            at[dim] = v ^ 1
        return (*at, core)

    return route(move)


CORE_ROUTE = route(lambda x, y, z, core: (x, y, z, 1 - core))


def shifted(block, axis, distance):
    devices = range(lax.axis_size(axis))
    pairs = [(i - distance, i) for i in devices if i - distance in devices]
    return lax.ppermute(block, axis, pairs)


def sum_everywhere(packed):
    core = lax.axis_index("py") % 2
    mine = lax.dynamic_slice_in_dim(packed, core * HALF, HALF, 0)
    other = lax.dynamic_slice_in_dim(packed, (1 - core) * HALF, HALF, 0)
    total = mine + lax.ppermute(other, AXES, CORE_ROUTE)
    for dim in range(3):
        for odd in (False, True):
            total = total + lax.ppermute(total, AXES, pair_route(dim, odd))
    theirs = lax.ppermute(total, AXES, CORE_ROUTE)
    low = jnp.where(core == 0, total, theirs)
    high = jnp.where(core == 0, theirs, total)
    return low, high


def pack_kernel(lists, counts, own, *refs):
    outs, zero, sems = refs[:4], refs[4], refs[5]
    zero[...] = jnp.zeros_like(zero)
    for e in range(4):
        for s in range(GMAX):
            block = lists[e * GMAX + s]

            @pl.when(s < counts[e])
            def _():
                pltpu.make_async_copy(own.at[block], outs[e].at[s], sems.at[e, s]).start()

            @pl.when(s >= counts[e])
            def _():
                pltpu.make_async_copy(zero, outs[e].at[s], sems.at[e, s]).start()

    for e in range(4):
        for s in range(GMAX):
            pltpu.make_async_copy(zero, outs[e].at[s], sems.at[e, s]).wait()


def pack_ghosts(own_blocks, lists, counts):
    smem = pl.BlockSpec(memory_space=pltpu.SMEM)
    anywhere = pl.BlockSpec(memory_space=pl.ANY)
    out = jax.ShapeDtypeStruct((GMAX, BS, K), F32)
    return pl.pallas_call(
        pack_kernel,
        out_shape=[out] * 4,
        in_specs=[smem, smem, anywhere],
        out_specs=[anywhere] * 4,
        scratch_shapes=[pltpu.VMEM((BS, K), F32), pltpu.SemaphoreType.DMA((4, GMAX))],
        cost_estimate=pl.CostEstimate(flops=0, bytes_accessed=4 * MB, transcendentals=0),
        name="pack_ghosts",
    )(lists, counts, own_blocks)


def split(x):
    high = x.astype(BF16)
    return high, (x - high.astype(F32)).astype(BF16)


def dot(a, b):
    return lax.dot_general(a, b, (((1,), (0,)), ((), ())), preferred_element_type=F32)


def gather_row(cols, row, tile_list, col_list, low, high, zero_block):
    n = jnp.int32(0)
    for t in range(TPR):
        c = cols[row * TPR + t]
        tile_list[n] = t
        col_list[n] = c - low
        n = n + jnp.where((c >= low) & (c < high), 1, 0)
    tile_list[n] = 0
    col_list[n] = zero_block
    return (n + 1) // 2


def add_pairs(pairs, tile_list, col_list, tiles, xh, xl, acc):
    def pair(p, _):
        t0, t1 = tile_list[2 * p], tile_list[2 * p + 1]
        c0, c1 = col_list[2 * p], col_list[2 * p + 1]
        th, tl = split(jnp.concatenate([tiles[0, t0], tiles[0, t1]], axis=1))
        r0 = pl.ds(pl.multiple_of(c0 * BS, BS), BS)
        r1 = pl.ds(pl.multiple_of(c1 * BS, BS), BS)
        bh = jnp.concatenate([xh[r0], xh[r1]], axis=0)
        bl = jnp.concatenate([xl[r0], xl[r1]], axis=0)
        acc[...] += dot(th, bh) + dot(tl, bh) + dot(th, bl)
        return 0

    lax.fori_loop(0, pairs, pair, 0)


def own_kernel(cols, live, own, tiles, out, xh, xl, acc, tile_list, col_list):
    row = pl.program_id(0)

    @pl.when(row == 0)
    def _():
        xh[NBD * BS :] = jnp.zeros((BS, K), BF16)
        xl[NBD * BS :] = jnp.zeros((BS, K), BF16)

        def convert(b, _):
            rows = pl.ds(pl.multiple_of(b * BS, BS), BS)
            xh[rows], xl[rows] = split(own[rows])
            return 0

        lax.fori_loop(0, NBD, convert, 0)

    acc[...] = jnp.zeros_like(acc)

    @pl.when(row < live[0])
    def _():
        pairs = gather_row(cols, row, tile_list, col_list, 0, NBD, NBD)
        add_pairs(pairs, tile_list, col_list, tiles, xh, xl, acc)

    out[...] = acc[...]


def apply_own(own, tiles, cols, live):
    smem = pl.BlockSpec(memory_space=pltpu.SMEM)
    return pl.pallas_call(
        own_kernel,
        grid=(NBD,),
        out_shape=jax.ShapeDtypeStruct((NBD * BS, K), F32),
        in_specs=[
            smem,
            smem,
            pl.BlockSpec((NBD * BS, K), lambda b: (0, 0)),
            pl.BlockSpec((1, TPR, BS, BS), lambda b: (b, 0, 0, 0)),
        ],
        out_specs=pl.BlockSpec((BS, K), lambda b: (b, 0)),
        scratch_shapes=[
            pltpu.VMEM(((NBD + 1) * BS, K), BF16),
            pltpu.VMEM(((NBD + 1) * BS, K), BF16),
            pltpu.VMEM((BS, K), F32),
            pltpu.SMEM((TPR + 4,), jnp.int32),
            pltpu.SMEM((TPR + 4,), jnp.int32),
        ],
        compiler_params=pltpu.CompilerParams(vmem_limit_bytes=40 * MB),
        cost_estimate=pl.CostEstimate(flops=4 * 10**9, bytes_accessed=25 * MB, transcendentals=0),
        name="apply_own",
    )(cols, live, own, tiles)


def gram_pack(high, low):
    tn = lambda a, b: lax.dot_general(a, b, (((0,), (0,)), ((), ())), preferred_element_type=F32)
    main = tn(high, high)
    cross = tn(high, low)
    gram = main + cross + cross.T
    i = lax.broadcasted_iota(jnp.int32, (BS, BS), 0)
    j = lax.broadcasted_iota(jnp.int32, (BS, BS), 1)
    first, second = gram[:BS, :BS], gram[BS:, BS:]
    diagonal = jnp.sum(jnp.where(i == j, second, 0.0), axis=0, keepdims=True)
    tail = jnp.broadcast_to(diagonal, (2 * HALF - 2 * BS, BS))
    return jnp.concatenate([jnp.where(i <= j, first, second), gram[:BS, BS:], tail], axis=0)


def ghost_kernel(cols, live, part, g0, g1, g2, g3, tiles, out, gram, xh, xl, ah, al, acc, tile_list, col_list):
    row = pl.program_id(0)

    @pl.when(row == 0)
    def _():
        xh[4 * GMAX * BS :] = jnp.zeros((BS, K), BF16)
        xl[4 * GMAX * BS :] = jnp.zeros((BS, K), BF16)
        for e, g in enumerate((g0, g1, g2, g3)):
            for s in range(GMAX):
                rows = pl.ds((e * GMAX + s) * BS, BS)
                xh[rows], xl[rows] = split(g[s])

    acc[...] = part[...]

    @pl.when(row < live[0])
    def _():
        pairs = gather_row(cols, row, tile_list, col_list, NBD, NBD + 4 * GMAX, 4 * GMAX)
        add_pairs(pairs, tile_list, col_list, tiles, xh, xl, acc)

    total = acc[...]
    out[...] = total
    rows = pl.ds(pl.multiple_of(row * BS, BS), BS)
    ah[rows], al[rows] = split(total)

    @pl.when(row == NBD - 1)
    def _():
        gram[...] = gram_pack(ah[...], al[...])


def apply_ghosts(part, ghosts, tiles, cols, live):
    smem = pl.BlockSpec(memory_space=pltpu.SMEM)
    whole = pl.BlockSpec((GMAX, BS, K), lambda b: (0, 0, 0))
    return pl.pallas_call(
        ghost_kernel,
        grid=(NBD,),
        out_shape=[
            jax.ShapeDtypeStruct((NBD * BS, K), F32),
            jax.ShapeDtypeStruct((2 * HALF, BS), F32),
        ],
        in_specs=[smem, smem, pl.BlockSpec((BS, K), lambda b: (b, 0))]
        + [whole] * 4
        + [pl.BlockSpec((1, TPR, BS, BS), lambda b: (b, 0, 0, 0))],
        out_specs=[
            pl.BlockSpec((BS, K), lambda b: (b, 0)),
            pl.BlockSpec((2 * HALF, BS), lambda b: (0, 0)),
        ],
        scratch_shapes=[
            pltpu.VMEM(((4 * GMAX + 1) * BS, K), BF16),
            pltpu.VMEM(((4 * GMAX + 1) * BS, K), BF16),
            pltpu.VMEM((NBD * BS, K), BF16),
            pltpu.VMEM((NBD * BS, K), BF16),
            pltpu.VMEM((BS, K), F32),
            pltpu.SMEM((TPR + 4,), jnp.int32),
            pltpu.SMEM((TPR + 4,), jnp.int32),
        ],
        compiler_params=pltpu.CompilerParams(vmem_limit_bytes=40 * MB),
        cost_estimate=pl.CostEstimate(flops=4 * 10**9, bytes_accessed=25 * MB, transcendentals=0),
        name="apply_ghosts",
    )(cols, live, part, *ghosts, tiles)


def exact(a, b, ca=1, cb=0):
    return lax.dot_general(
        a, b, (((ca,), (cb,)), ((), ())), precision=lax.Precision.HIGHEST, preferred_element_type=F32
    )


def eliminate(square):
    n = square.shape[0]
    i = lax.broadcasted_iota(jnp.int32, (n, n), 0)
    j = lax.broadcasted_iota(jnp.int32, (n, n), 1)
    unit = jnp.where(i == j, 1.0, 0.0).astype(F32)
    groups = n // 8
    left = [square[8 * g : 8 * g + 8] for g in range(groups)]
    right = [unit[8 * g : 8 * g + 8] for g in range(groups)]
    place = lax.broadcasted_iota(jnp.int32, (8, n), 0)
    for p in range(n):
        at, sub = divmod(p, 8)
        row = left[at][sub : sub + 1]
        row_right = right[at][sub : sub + 1]
        inverse = 1.0 / row[:, p : p + 1]
        for g in range(at, groups):
            if g == at and sub == 7:
                continue
            factor = left[g][:, p : p + 1] * inverse
            if g == at:
                factor = jnp.where(place > sub, factor, 0.0)
            left[g] = left[g] - factor * row
            right[g] = right[g] - factor * row_right
    upper = jnp.concatenate(left, axis=0)
    lower = jnp.concatenate(right, axis=0)
    pivot = jnp.sum(jnp.where(i == j, upper, 0.0), axis=1, keepdims=True)
    scale = lax.rsqrt(pivot)
    return jnp.where(i <= j, upper * scale, 0.0), jnp.where(i >= j, lower * scale, 0.0)


def factor(low, high):
    packed = jnp.concatenate([low, high], axis=0) * (1.0 / NROWS)
    mixed, corner, tail = packed[:BS], packed[BS : 2 * BS], packed[2 * BS : 2 * BS + 1]
    i = lax.broadcasted_iota(jnp.int32, (BS, BS), 0)
    j = lax.broadcasted_iota(jnp.int32, (BS, BS), 1)
    turned = mixed.T
    first = jnp.where(i <= j, mixed, turned)
    second = jnp.where(i > j, mixed, jnp.where(i < j, turned, tail))
    r11, x11 = eliminate(first)
    r12 = exact(x11, corner)
    r22, x22 = eliminate(second - exact(r12, r12, 0, 0))
    x21 = -exact(x22, exact(r12, x11, 0, 0))
    zero = jnp.zeros((BS, BS), F32)
    upper = jnp.concatenate(
        [jnp.concatenate([r11, r12], axis=1), jnp.concatenate([zero, r22], axis=1)], axis=0
    )
    lower = jnp.concatenate(
        [jnp.concatenate([x11, zero], axis=1), jnp.concatenate([x21, x22], axis=1)], axis=0
    )
    return upper, lower


def basis_kernel(low, high, applied, basis, upper, wh, wl):
    @pl.when(pl.program_id(0) == 0)
    def _():
        r, x = factor(low[...], high[...])
        upper[...] = r
        wh[...], wl[...] = split(x.T)

    ah, al = split(applied[...])
    basis[...] = dot(ah, wh[...]) + dot(al, wh[...]) + dot(ah, wl[...])


def orthonormalize(low, high, applied):
    rows = 512
    half = pl.BlockSpec((HALF, BS), lambda b: (0, 0))
    return pl.pallas_call(
        basis_kernel,
        grid=(NBD * BS // rows,),
        out_shape=[
            jax.ShapeDtypeStruct((NBD * BS, K), F32),
            jax.ShapeDtypeStruct((K, K), F32),
        ],
        in_specs=[half, half, pl.BlockSpec((rows, K), lambda b: (b, 0))],
        out_specs=[
            pl.BlockSpec((rows, K), lambda b: (b, 0)),
            pl.BlockSpec((K, K), lambda b: (0, 0)),
        ],
        scratch_shapes=[pltpu.VMEM((K, K), BF16), pltpu.VMEM((K, K), BF16)],
        compiler_params=pltpu.CompilerParams(vmem_limit_bytes=40 * MB),
        cost_estimate=pl.CostEstimate(flops=10**9, bytes_accessed=7 * MB, transcendentals=0),
        name="factor_and_basis",
    )(low, high, applied)


def body(block_vectors, stiff_tiles, col_index, send_lists, send_counts, part_blocks):
    own_blocks = block_vectors.reshape(NBD, BS, K)
    cols = col_index.reshape(NBD * TPR)
    packed = pack_ghosts(own_blocks, send_lists.reshape(4 * GMAX), send_counts.reshape(4))
    ghosts = [
        shifted(packed[0], "px", 1),
        shifted(packed[1], "px", -1),
        shifted(packed[2], "py", 1),
        shifted(packed[3], "py", -1),
    ]
    part = apply_own(block_vectors, stiff_tiles, cols, part_blocks)
    applied, gram = apply_ghosts(part, ghosts, stiff_tiles, cols, part_blocks)
    low, high = sum_everywhere(gram)
    return tuple(orthonormalize(low, high, applied))


def solution(mesh):
    placed = (
        P(AXES, None),
        P(AXES, None, None, None),
        P(AXES, None),
        P(AXES, None, None),
        P(AXES, None),
        P(AXES),
    )
    return jax.shard_map(body, mesh=mesh, in_specs=placed, out_specs=(P(AXES, None), P()), check_vma=False)
```

time: 426 us -> 198 us (0.46)
  waiting for transfers between devices: 144 us -> 14.5 us
  Pallas kernels: 0 us -> 126 us
  matrix products: 101 us -> 0 us
  other arithmetic: 82.9 us -> 0.08 us
  local copies, waits for them, and re-layouts: 67.7 us -> 5.17 us
  starting transfers between devices: 12.4 us -> 50 us
  between operations: 16.1 us -> 1.49 us
    psum x1 -> x0, waiting for transfers between devices: 143 us -> none  [body(): total_gram = lax.psum(local_gram, ('px', 'py'))]
    pallas_call x0 -> x4, Pallas kernels: none -> 126 us  [the longest x1 53.5 us: pack_ghosts(): pl.pallas_call(pack_kernel, out_shape=[out] * 4, in_specs=[smem, smem, an...]
    dot_general x14 -> x0, matrix products: 95.6 us -> none  [the longest x12 85.5 us: add_tile(): return total + jnp.einsum('bij,bjk->bik', tile, operand, precision=hp)]
    another operation x9 -> x0, other arithmetic: 55.8 us -> none  [the longest x7 34.7 us: body(): lower = jnp.linalg.cholesky(gram)]
    gather x16 -> x0, local copies, waits for them, and re-layouts: 48.1 us -> none  [the longest x12 38.8 us: add_tile(): jnp.take(source, columns[:, step], axis=0) * valid[:, step][:, None, None]]
    ppermute x4 -> x12, starting transfers between devices: 12.4 us -> 50 us  [the longest x6 29.4 us: sum_everywhere(): total = total + lax.ppermute(total, AXES, pair_route(dim, odd))]
    ppermute x4 -> x12, waiting for transfers between devices: 0.65 us -> 14.5 us  [the longest x6 12.4 us: sum_everywhere(): total = total + lax.ppermute(total, AXES, pair_route(dim, odd))]
    mul x5 -> x0, other arithmetic: 10.2 us -> none  [the longest x4 7.85 us: pack_ghosts(): return chosen * alive[:, None, None]]
  transfers between devices with their start and end apart: 5 -> 12, of which waited for: 2 -> 8; matrix products, arithmetic and copies ran while one was open for 5% -> 0% of each run, Pallas kernels for 0% -> 12%
where the time goes in v1:
time: 198 us; the launch traced here: 197 us
  Pallas kernels  126 us (64%)
  starting transfers between devices  50 us (25%)
  waiting for transfers between devices  14.5 us (7%)
  local copies, waits for them, and re-layouts  5.17 us (3%)
    pallas_call x1, Pallas kernels, pack_ghosts(): pl.pallas_call(pack_kernel, out_shape=[out] * 4, in_specs=[smem, smem, an...  53.5 us
    ppermute x6, starting transfers between devices, sum_everywhere(): total = total + lax.ppermute(total, AXES, pair_route(dim, odd))  29.4 us
    pallas_call x1, Pallas kernels, orthonormalize(): pl.pallas_call(basis_kernel, grid=(NBD * BS // rows,), out_shape=[jax.Sha...  26.2 us
    pallas_call x1, Pallas kernels, apply_own(): pl.pallas_call(own_kernel, grid=(NBD,), out_shape=jax.ShapeDtypeStruct((N...  23.8 us
    pallas_call x1, Pallas kernels, apply_ghosts(): pl.pallas_call(ghost_kernel, grid=(NBD,), out_shape=[jax.ShapeDtypeStruct...  22.5 us
    ppermute x4, starting transfers between devices, shifted(): return lax.ppermute(block, axis, pairs)  14.2 us
    ppermute x6, waiting for transfers between devices, sum_everywhere(): total = total + lax.ppermute(total, AXES, pair_route(dim, odd))  12.4 us
    ppermute x1, starting transfers between devices, sum_everywhere(): theirs = lax.ppermute(total, AXES, CORE_ROUTE)  6.38 us
  transfers between devices with their start and end apart: 12, of which 8 were waited for; matrix products, arithmetic and copies ran while one was open for 0% of the time, Pallas kernels for 12%

profile of v1, /device:TPU:1, one launch (start us, length us, event | category | flops | bytes accessed | tf_op | source)
XLA Modules:
  0.0 197.3 jit_solution(11578175566653124376)
XLA Ops:
  0.6 0.0 copy-start
  0.7 1.4 reshape.17.lists
  2.1 53.5 %pack_ghosts.1 = (f32[4,128,256]{2,1,0:T(8,128)}, f32[4,128,256]{2,1,0:T(8,128)}, f32[4,128,256]{2,1,0:T(8,128)}, f32[4,128,256]{2,1,0:T(8,128)}) custom-call(s32[16]{0:T(128)} %reshape.17.lists, s32[4]{0:T(128)} %bitcast.3, f32[24,128,256]{2,1,0:T(8,128)} %bitcast.2), custom_call_target="tpu_custom_call" | custom-call | bytes 4194304 | tf_op jit(solution)/shard_map/pack_ghosts/pallas_call | solution.py:94
  55.6 2.1 %collective-permute-start = (f32[4,128,256]{2,1,0:T(8,128)}, f32[4,128,256]{2,1,0:T(8,128)}, u32[]{:S(2)}, u32[]{:S(2)}) collective-permute-start(f32[4,128,256]{2,1,0:T(8,128)} %get-tuple-element.8), channel_id=1, source_target_pairs={{0,8},{8,16},{16,24},{24,32},{32,40},{40,48},{48,56},{56,64},{64,7... | collective-permute-start | bytes 1572872 | tf_op jit(solution)/shard_map/ppermute | solution.py:53
  57.7 1.3 collective-permute-start.1
  59.0 8.9 %collective-permute-start.2 = (f32[4,128,256]{2,1,0:T(8,128)}, f32[4,128,256]{2,1,0:T(8,128)}, u32[]{:S(2)}, u32[]{:S(2)}) collective-permute-start(f32[4,128,256]{2,1,0:T(8,128)} %get-tuple-element.10), channel_id=1, source_target_pairs={{0,1},{1,2},{2,3},{3,4},{4,5},{5,6},{6,7},{8,9},{9,10},{10,11},{11... | collective-permute-start | bytes 1572872 | tf_op jit(solution)/shard_map/ppermute | solution.py:53
  67.9 1.9 collective-permute-start.3
  69.9 0.1 copy.8
  70.0 0.1 reshape.16.cols
  70.8 23.8 %apply_own.1.part = f32[3072,256]{1,0:T(8,128)S(1)} custom-call(s32[288]{0:T(512)S(1)} %reshape.16.cols, s32[1]{0:T(128)S(6)} %copy.9.live, f32[3072,256]{1,0:T(8,128)S(1)} %copy-done, f32[24,12,128,128]{3,2,1,0:T(8,128)} %tiles.3), custom_call_target="tpu_custom_call" | custom-call | flops 4000000000 | bytes 26214400 | tf_op jit(solution)/shard_map/apply_own/pallas_call | solution.py:168
  94.5 0.0 collective-permute-done.1.g1
  94.6 22.5 %apply_ghosts.1 = (f32[3072,256]{1,0:T(8,128)S(1)}, f32[272,128]{1,0:T(8,128)S(1)}) custom-call(s32[288]{0:T(512)S(1)} %reshape.16.cols, s32[1]{0:T(128)S(6)} %copy.9.live, f32[3072,256]{1,0:T(8,128)S(1)} %apply_own.1.part, f32[4,128,256]{2,1,0:T(8,128)} %collective-permute-done.g0, f32[4,128,256]{2,1,0:T(8,128)} %collective-permute-done.1.g1, ...), custom_call_target="tpu_custom_call" | custom-call | flops 4000000000 | bytes 26214400 | tf_op jit(solution)/shard_map/apply_ghosts/pallas_call | solution.py:237
  117.1 0.0 copy-start.1
  117.1 1.7 copy-done.1
  118.8 1.2 collective-permute-done.4
  120.1 9.4 %collective-permute-start.5 = (f32[136,128]{1,0:T(8,128)S(1)}, f32[136,128]{1,0:T(8,128)S(1)}, u32[]{:S(2)}, u32[]{:S(2)}) collective-permute-start(f32[136,128]{1,0:T(8,128)S(1)} %dynamic-slice_add_fusion), channel_id=1, source_target_pairs={{0,8},{1,9},{2,10},{3,11},{4,12},{5,13},{6,14},{7,15},{32,40},{33,... | collective-permute-start | bytes 208904 | tf_op jit(solution)/shard_map/ppermute | solution.py:63
  129.5 2.4 %collective-permute-done.5 = f32[136,128]{1,0:T(8,128)S(1)} collective-permute-done((f32[136,128]{1,0:T(8,128)S(1)}, f32[136,128]{1,0:T(8,128)S(1)}, u32[]{:S(2)}, u32[]{:S(2)}) %collective-permute-start.5) | collective-permute-done | bytes 69664 | tf_op jit(solution)/shard_map/ppermute | solution.py:63
  131.9 2.6 %collective-permute-start.6 = (f32[136,128]{1,0:T(8,128)S(1)}, f32[136,128]{1,0:T(8,128)S(1)}, u32[]{:S(2)}, u32[]{:S(2)}) collective-permute-start(f32[136,128]{1,0:T(8,128)S(1)} %add.35), channel_id=1, source_target_pairs={{0,24},{1,25},{2,26},{3,27},{4,28},{5,29},{6,30},{7,31},{32,56},{3... | collective-permute-start | bytes 208904 | tf_op jit(solution)/shard_map/ppermute | solution.py:63
  134.5 1.8 collective-permute-done.6
  136.4 0.2 collective-permute-start.7
  136.6 3.0 %collective-permute-done.7 = f32[136,128]{1,0:T(8,128)S(1)} collective-permute-done((f32[136,128]{1,0:T(8,128)S(1)}, f32[136,128]{1,0:T(8,128)S(1)}, u32[]{:S(2)}, u32[]{:S(2)}) %collective-permute-start.7) | collective-permute-done | bytes 69664 | tf_op jit(solution)/shard_map/ppermute | solution.py:63
  139.6 3.3 %collective-permute-start.8 = (f32[136,128]{1,0:T(8,128)S(1)}, f32[136,128]{1,0:T(8,128)S(1)}, u32[]{:S(2)}, u32[]{:S(2)}) collective-permute-start(f32[136,128]{1,0:T(8,128)S(1)} %add.37), channel_id=1, source_target_pairs={{0,96},{1,97},{2,98},{3,99},{4,100},{5,101},{6,102},{7,103},{32,64... | collective-permute-start | bytes 208904 | tf_op jit(solution)/shard_map/ppermute | solution.py:63
  142.9 1.7 collective-permute-done.8
  144.6 7.2 %collective-permute-start.9 = (f32[136,128]{1,0:T(8,128)S(1)}, f32[136,128]{1,0:T(8,128)S(1)}, u32[]{:S(2)}, u32[]{:S(2)}) collective-permute-start(f32[136,128]{1,0:T(8,128)S(1)} %add.38), channel_id=1, source_target_pairs={{0,2},{1,3},{2,0},{3,1},{4,6},{5,7},{6,4},{7,5},{32,34},{33,35},{3... | collective-permute-start | bytes 208904 | tf_op jit(solution)/shard_map/ppermute | solution.py:63
  151.8 1.7 collective-permute-done.9
  153.5 6.7 %collective-permute-start.10 = (f32[136,128]{1,0:T(8,128)S(1)}, f32[136,128]{1,0:T(8,128)S(1)}, u32[]{:S(2)}, u32[]{:S(2)}) collective-permute-start(f32[136,128]{1,0:T(8,128)S(1)} %add.39), channel_id=1, source_target_pairs={{0,6},{1,7},{2,4},{3,5},{4,2},{5,3},{6,0},{7,1},{32,38},{33,39},{3... | collective-permute-start | bytes 208904 | tf_op jit(solution)/shard_map/ppermute | solution.py:63
  160.2 1.7 collective-permute-done.10
  161.9 6.4 %collective-permute-start.11 = (f32[136,128]{1,0:T(8,128)S(1)}, f32[136,128]{1,0:T(8,128)S(1)}, u32[]{:S(2)}, u32[]{:S(2)}) collective-permute-start(f32[136,128]{1,0:T(8,128)S(1)} %add.40), channel_id=1, source_target_pairs={{0,1},{1,0},{2,3},{3,2},{4,5},{5,4},{6,7},{7,6},{32,33},{33,32},{3... | collective-permute-start | bytes 208904 | tf_op jit(solution)/shard_map/ppermute | solution.py:64
  168.3 0.9 collective-permute-done.11
  169.2 0.0 copy-start.2
  169.2 1.9 copy-done.2
  171.1 26.2 %factor_and_basis.1 = (f32[3072,256]{1,0:T(8,128)}, f32[256,256]{1,0:T(8,128)}) custom-call(f32[136,128]{1,0:T(8,128)S(1)} %get-tuple-element.15.low, f32[136,128]{1,0:T(8,128)S(1)} %get-tuple-element.14.high, f32[3072,256]{1,0:T(8,128)S(1)} %copy-done.2), custom_call_target="tpu_custom_call" | custom-call | flops 1000000000 | bytes 7340032 | tf_op jit(solution)/shard_map/factor_and_basis/pallas_call | solution.py:337
  (16 shorter events, 0.1 us)
Async XLA Ops:
  0.6 70.1 %copy-start = (f32[3072,256]{1,0:T(8,128)S(1)}, f32[3072,256]{1,0:T(8,128)}, u32[]{:S(2)}) copy-start(f32[3072,256]{1,0:T(8,128)} %own.1) | copy-start | bytes 9437188
  0.6 69.2 %copy-start.3 = (s32[24,12]{0,1:T(8,128)S(1)}, s32[24,12]{0,1:T(8,128)}, u32[]{:S(2)}) copy-start(s32[24,12]{0,1:T(8,128)} %param.8) | copy-start | bytes 3460
  55.6 38.9 %collective-permute-start = (f32[4,128,256]{2,1,0:T(8,128)}, f32[4,128,256]{2,1,0:T(8,128)}, u32[]{:S(2)}, u32[]{:S(2)}) collective-permute-start(f32[4,128,256]{2,1,0:T(8,128)} %get-tuple-element.8), channel_id=1, source_target_pairs={{0,8},{8,16},{16,24},{24,32},{32,40},{40,48},{48,56},{56,64},{64,7... | collective-permute-start | bytes 1572872 | tf_op jit(solution)/shard_map/ppermute | solution.py:53
  57.7 36.8 %collective-permute-start.1 = (f32[4,128,256]{2,1,0:T(8,128)}, f32[4,128,256]{2,1,0:T(8,128)}, u32[]{:S(2)}, u32[]{:S(2)}) collective-permute-start(f32[4,128,256]{2,1,0:T(8,128)} %get-tuple-element.9), channel_id=1, source_target_pairs={{8,0},{16,8},{24,16},{32,24},{40,32},{48,40},{56,48},{64,56},{72,6... | collective-permute-start | bytes 1572872 | tf_op jit(solution)/shard_map/ppermute | solution.py:53
  59.0 35.5 %collective-permute-start.2 = (f32[4,128,256]{2,1,0:T(8,128)}, f32[4,128,256]{2,1,0:T(8,128)}, u32[]{:S(2)}, u32[]{:S(2)}) collective-permute-start(f32[4,128,256]{2,1,0:T(8,128)} %get-tuple-element.10), channel_id=1, source_target_pairs={{0,1},{1,2},{2,3},{3,4},{4,5},{5,6},{6,7},{8,9},{9,10},{10,11},{11... | collective-permute-start | bytes 1572872 | tf_op jit(solution)/shard_map/ppermute | solution.py:53
  67.9 26.6 %collective-permute-start.3 = (f32[4,128,256]{2,1,0:T(8,128)}, f32[4,128,256]{2,1,0:T(8,128)}, u32[]{:S(2)}, u32[]{:S(2)}) collective-permute-start(f32[4,128,256]{2,1,0:T(8,128)} %get-tuple-element.11), channel_id=1, source_target_pairs={{1,0},{2,1},{3,2},{4,3},{5,4},{6,5},{7,6},{9,8},{10,9},{11,10},{12... | collective-permute-start | bytes 1572872 | tf_op jit(solution)/shard_map/ppermute | solution.py:53
  117.1 1.7 copy-start.1
  118.8 1.3 collective-permute-start.4
  120.1 11.8 %collective-permute-start.5 = (f32[136,128]{1,0:T(8,128)S(1)}, f32[136,128]{1,0:T(8,128)S(1)}, u32[]{:S(2)}, u32[]{:S(2)}) collective-permute-start(f32[136,128]{1,0:T(8,128)S(1)} %dynamic-slice_add_fusion), channel_id=1, source_target_pairs={{0,8},{1,9},{2,10},{3,11},{4,12},{5,13},{6,14},{7,15},{32,40},{33,... | collective-permute-start | bytes 208904 | tf_op jit(solution)/shard_map/ppermute | solution.py:63
  131.9 4.5 %collective-permute-start.6 = (f32[136,128]{1,0:T(8,128)S(1)}, f32[136,128]{1,0:T(8,128)S(1)}, u32[]{:S(2)}, u32[]{:S(2)}) collective-permute-start(f32[136,128]{1,0:T(8,128)S(1)} %add.35), channel_id=1, source_target_pairs={{0,24},{1,25},{2,26},{3,27},{4,28},{5,29},{6,30},{7,31},{32,56},{3... | collective-permute-start | bytes 208904 | tf_op jit(solution)/shard_map/ppermute | solution.py:63
  136.4 3.2 %collective-permute-start.7 = (f32[136,128]{1,0:T(8,128)S(1)}, f32[136,128]{1,0:T(8,128)S(1)}, u32[]{:S(2)}, u32[]{:S(2)}) collective-permute-start(f32[136,128]{1,0:T(8,128)S(1)} %add.36), channel_id=1, source_target_pairs={{0,32},{1,33},{2,34},{3,35},{4,36},{5,37},{6,38},{7,39},{32,0},{33... | collective-permute-start | bytes 208904 | tf_op jit(solution)/shard_map/ppermute | solution.py:63
  139.6 5.0 %collective-permute-start.8 = (f32[136,128]{1,0:T(8,128)S(1)}, f32[136,128]{1,0:T(8,128)S(1)}, u32[]{:S(2)}, u32[]{:S(2)}) collective-permute-start(f32[136,128]{1,0:T(8,128)S(1)} %add.37), channel_id=1, source_target_pairs={{0,96},{1,97},{2,98},{3,99},{4,100},{5,101},{6,102},{7,103},{32,64... | collective-permute-start | bytes 208904 | tf_op jit(solution)/shard_map/ppermute | solution.py:63
  144.6 8.9 %collective-permute-start.9 = (f32[136,128]{1,0:T(8,128)S(1)}, f32[136,128]{1,0:T(8,128)S(1)}, u32[]{:S(2)}, u32[]{:S(2)}) collective-permute-start(f32[136,128]{1,0:T(8,128)S(1)} %add.38), channel_id=1, source_target_pairs={{0,2},{1,3},{2,0},{3,1},{4,6},{5,7},{6,4},{7,5},{32,34},{33,35},{3... | collective-permute-start | bytes 208904 | tf_op jit(solution)/shard_map/ppermute | solution.py:63
  153.5 8.4 %collective-permute-start.10 = (f32[136,128]{1,0:T(8,128)S(1)}, f32[136,128]{1,0:T(8,128)S(1)}, u32[]{:S(2)}, u32[]{:S(2)}) collective-permute-start(f32[136,128]{1,0:T(8,128)S(1)} %add.39), channel_id=1, source_target_pairs={{0,6},{1,7},{2,4},{3,5},{4,2},{5,3},{6,0},{7,1},{32,38},{33,39},{3... | collective-permute-start | bytes 208904 | tf_op jit(solution)/shard_map/ppermute | solution.py:63
  161.9 7.3 %collective-permute-start.11 = (f32[136,128]{1,0:T(8,128)S(1)}, f32[136,128]{1,0:T(8,128)S(1)}, u32[]{:S(2)}, u32[]{:S(2)}) collective-permute-start(f32[136,128]{1,0:T(8,128)S(1)} %add.40), channel_id=1, source_target_pairs={{0,1},{1,0},{2,3},{3,2},{4,5},{5,4},{6,7},{7,6},{32,33},{33,32},{3... | collective-permute-start | bytes 208904 | tf_op jit(solution)/shard_map/ppermute | solution.py:64
  169.2 1.9 copy-start.2

commit v2 on v1

v2 whole, which is shorter than its diff:
```python
import functools
import itertools

import jax
import jax.numpy as jnp
from jax import lax
from jax.experimental import pallas as pl
from jax.experimental.pallas import tpu as pltpu
from jax.sharding import PartitionSpec as P

AXES = ("px", "py")
SIDE = 4
BS = 128
K = 256
NBD = 24
TPR = 12
GMAX = 4
NROWS = 393216
HALF = 136
F32 = jnp.float32
BF16 = jnp.bfloat16
MB = 1 << 20
CHUNK = 4
AHEAD = 4
NEAR = 2
STORE = 512


def device_at(x, y, z, core):
    return (y * SIDE + x) * 8 + z * 2 + core


def route(move):
    places = itertools.product(range(SIDE), range(SIDE), range(SIDE), range(2))
    return [(device_at(*p), device_at(*move(*p))) for p in places]


def pair_route(dim, odd):
    def move(x, y, z, core):
        at = [x, y, z]
        v = at[dim]
        if odd:
            at[dim] = (v - 1) % SIDE if v % 2 == 0 else (v + 1) % SIDE
        else:
            at[dim] = v ^ 1
        return (*at, core)

    return route(move)


CORE_ROUTE = route(lambda x, y, z, core: (x, y, z, 1 - core))


def shifted(block, axis, distance):
    devices = range(lax.axis_size(axis))
    pairs = [(i - distance, i) for i in devices if i - distance in devices]
    return lax.ppermute(block, axis, pairs)


def sum_everywhere(packed):
    core = lax.axis_index("py") % 2
    mine = lax.dynamic_slice_in_dim(packed, core * HALF, HALF, 0)
    other = lax.dynamic_slice_in_dim(packed, (1 - core) * HALF, HALF, 0)
    total = mine + lax.ppermute(other, AXES, CORE_ROUTE)
    for dim in range(3):
        for odd in (False, True):
            total = total + lax.ppermute(total, AXES, pair_route(dim, odd))
    theirs = lax.ppermute(total, AXES, CORE_ROUTE)
    low = jnp.where(core == 0, total, theirs)
    high = jnp.where(core == 0, theirs, total)
    return low, high


def on_vmem(x):
    return pltpu.with_memory_space_constraint(x, pltpu.VMEM)


def pack_kernel(lists, counts, own, *refs):
    outs, sems = refs[:4], refs[4]

    def copy(e, s, block):
        return pltpu.make_async_copy(own.at[block], outs[e].at[s], sems.at[e, s])

    for e in range(4):
        for s in range(GMAX):
            alive = s < counts[e]

            @pl.when(alive)
            def _():
                copy(e, s, lists[e * GMAX + s]).start()

            @pl.when(jnp.logical_not(alive))
            def _():
                outs[e][s] = jnp.zeros((BS, K), F32)

    for e in range(4):
        for s in range(GMAX):

            @pl.when(s < counts[e])
            def _():
                copy(e, s, 0).wait()


def pack_ghosts(own_blocks, lists, counts):
    smem = pl.BlockSpec(memory_space=pltpu.SMEM)
    vmem = pl.BlockSpec(memory_space=pltpu.VMEM)
    return pl.pallas_call(
        pack_kernel,
        out_shape=[pltpu.VMEM((GMAX, BS, K), F32)] * 4,
        in_specs=[smem, smem, pl.BlockSpec(memory_space=pltpu.HBM)],
        out_specs=[vmem] * 4,
        scratch_shapes=[pltpu.SemaphoreType.DMA((4, GMAX))],
        compiler_params=pltpu.CompilerParams(vmem_limit_bytes=4 * MB),
        cost_estimate=pl.CostEstimate(flops=0, bytes_accessed=4 * MB, transcendentals=0),
        name="pack_ghosts",
    )(lists, counts, own_blocks)


def split(x):
    high = x.astype(BF16)
    return high, (x - high.astype(F32)).astype(BF16)


def dot(a, b):
    return lax.dot_general(a, b, (((1,), (0,)), ((), ())), preferred_element_type=F32)


def pair_lists(cols, live, own_list, ghost_list):
    def row_pairs(row, counts):
        starts = counts
        for t in range(TPR):
            c = cols[row * TPR + t]
            ghost = jnp.where(c >= NBD, 1, 0)
            for (tile, block, _, _), n, first, mine in (
                (own_list, counts[0], 0, 1 - ghost),
                (ghost_list, counts[1], NBD, ghost),
            ):
                tile[n] = row * TPR + t
                block[n] = c - first
            counts = (counts[0] + 1 - ghost, counts[1] + ghost)
        ends = []
        for (tile, block, rows, _), n, start, zero in (
            (own_list, counts[0], starts[0], NBD),
            (ghost_list, counts[1], starts[1], 4 * GMAX),
        ):
            tile[n] = 0
            block[n] = zero
            end = n + (n & 1)
            for k in range(TPR // 2):
                rows[start // 2 + k] = row
            ends.append(end)
        return tuple(ends)

    zero = jnp.int32(0)
    own_n, ghost_n = lax.fori_loop(0, live[0], row_pairs, (zero, zero))
    for (tile, block, rows, count), n, blank in (
        (own_list, own_n, NBD),
        (ghost_list, ghost_n, 4 * GMAX),
    ):
        for k in range(2 * CHUNK):
            tile[n + k] = 0
            block[n + k] = blank
        for k in range(CHUNK):
            rows[n // 2 + k] = 0
        count[0] = n // 2


def add_chunk(start, lists, tiles, xh, xl, acc):
    tile, block, rows, _ = lists
    for k in range(CHUNK):
        p = start + k
        t0, t1, c0, c1 = tile[2 * p], tile[2 * p + 1], block[2 * p], block[2 * p + 1]
        th, tl = split(jnp.concatenate([tiles[t0], tiles[t1]], axis=1))
        r0 = pl.ds(pl.multiple_of(c0 * BS, BS), BS)
        r1 = pl.ds(pl.multiple_of(c1 * BS, BS), BS)
        bh = jnp.concatenate([xh[r0], xh[r1]], axis=0)
        bl = jnp.concatenate([xl[r0], xl[r1]], axis=0)
        at = pl.ds(pl.multiple_of(rows[p] * BS, BS), BS)
        acc[at] += dot(th, bh) + dot(tl, bh) + dot(th, bl)


def own_kernel(cols, live, own, tiles, part, held, gt, gb, gr, gn, xv, xh, xl, ot, ob, orow, on, xsem, tsem):
    x_copies = [
        pltpu.make_async_copy(own.at[pl.ds(i * BS * 6, BS * 6)], xv.at[pl.ds(i * BS * 6, BS * 6)], xsem.at[i])
        for i in range(4)
    ]

    def fetch(row):
        rows = pl.ds(row * TPR, TPR)
        return pltpu.make_async_copy(tiles.at[rows], held.at[rows], tsem.at[row])

    for c in x_copies:
        c.start()
    for row in range(AHEAD):
        fetch(row).start()
    own_list, ghost_list = (ot, ob, orow, on), (gt, gb, gr, gn)
    pair_lists(cols, live, own_list, ghost_list)
    part[...] = jnp.zeros_like(part)
    xh[NBD * BS :] = jnp.zeros((BS, K), BF16)
    xl[NBD * BS :] = jnp.zeros((BS, K), BF16)
    for i, c in enumerate(x_copies):
        c.wait()

        def convert(b, _):
            rows = pl.ds(pl.multiple_of((i * 6 + b) * BS, BS), BS)
            xh[rows], xl[rows] = split(xv[rows])
            return 0

        lax.fori_loop(0, 6, convert, 0)

    def arrive(row, _):
        fetch(row).wait()

        @pl.when(row + AHEAD < NBD)
        def _():
            fetch(row + AHEAD).start()

        return 0

    pairs = on[0]

    def chunk(i, ready):
        last = jnp.minimum(i * CHUNK + CHUNK, pairs) - 1
        need = jnp.maximum(orow[last] + 1, ready)
        lax.fori_loop(ready, need, arrive, 0)
        add_chunk(i * CHUNK, own_list, held, xh, xl, part)
        return need

    ready = lax.fori_loop(0, (pairs + CHUNK - 1) // CHUNK, chunk, jnp.int32(0))
    lax.fori_loop(ready, NBD, arrive, 0)


def list_shapes(kind):
    return [
        kind((NBD * (TPR + 2) + 4 * CHUNK,), jnp.int32),
        kind((NBD * (TPR + 2) + 4 * CHUNK,), jnp.int32),
        kind((NBD * (TPR + 2) // 2 + 4 * CHUNK,), jnp.int32),
        kind((1,), jnp.int32),
    ]


def apply_own(own, tiles, cols, live):
    smem = pl.BlockSpec(memory_space=pltpu.SMEM)
    vmem = pl.BlockSpec(memory_space=pltpu.VMEM)
    hbm = pl.BlockSpec(memory_space=pltpu.HBM)
    return pl.pallas_call(
        own_kernel,
        out_shape=[
            pltpu.VMEM((NBD * BS, K), F32),
            pltpu.VMEM((NBD * TPR, BS, BS), F32),
            *list_shapes(jax.ShapeDtypeStruct),
        ],
        in_specs=[smem, smem, hbm, hbm],
        out_specs=[vmem, vmem] + [smem] * 4,
        scratch_shapes=[
            pltpu.VMEM((NBD * BS, K), F32),
            pltpu.VMEM(((NBD + 1) * BS, K), BF16),
            pltpu.VMEM(((NBD + 1) * BS, K), BF16),
            *list_shapes(pltpu.SMEM),
            pltpu.SemaphoreType.DMA((4,)),
            pltpu.SemaphoreType.DMA((NBD,)),
        ],
        compiler_params=pltpu.CompilerParams(vmem_limit_bytes=12 * MB),
        cost_estimate=pl.CostEstimate(flops=4 * 10**9, bytes_accessed=25 * MB, transcendentals=0),
        name="apply_own",
    )(cols, live, own, tiles)


def gram_pack(high, low):
    tn = lambda a, b: lax.dot_general(a, b, (((0,), (0,)), ((), ())), preferred_element_type=F32)
    main = tn(high, high)
    cross = tn(high, low)
    gram = main + cross + cross.T
    i = lax.broadcasted_iota(jnp.int32, (BS, BS), 0)
    j = lax.broadcasted_iota(jnp.int32, (BS, BS), 1)
    first, second = gram[:BS, :BS], gram[BS:, BS:]
    diagonal = jnp.sum(jnp.where(i == j, second, 0.0), axis=0, keepdims=True)
    tail = jnp.broadcast_to(diagonal, (2 * HALF - 2 * BS, BS))
    return jnp.concatenate([jnp.where(i <= j, first, second), gram[:BS, BS:], tail], axis=0)


def ghost_kernel(gt, gb, gr, gn, part, held, g0, g1, g2, g3, total, ah, al, gram, xh, xl):
    xh[4 * GMAX * BS :] = jnp.zeros((BS, K), BF16)
    xl[4 * GMAX * BS :] = jnp.zeros((BS, K), BF16)
    for e, g in enumerate((g0, g1, g2, g3)):

        def convert(s, _):
            rows = pl.ds(pl.multiple_of((e * GMAX + s) * BS, BS), BS)
            xh[rows], xl[rows] = split(g[s])
            return 0

        lax.fori_loop(0, GMAX, convert, 0)

    def chunk(i, _):
        add_chunk(i * CHUNK, (gt, gb, gr, gn), held, xh, xl, total)
        return 0

    lax.fori_loop(0, (gn[0] + CHUNK - 1) // CHUNK, chunk, 0)

    def finish(row, _):
        rows = pl.ds(pl.multiple_of(row * BS, BS), BS)
        ah[rows], al[rows] = split(total[rows])
        return 0

    lax.fori_loop(0, NBD, finish, 0)
    gram[...] = gram_pack(ah[...], al[...])


def apply_ghosts(part, held, lists, ghosts):
    smem = pl.BlockSpec(memory_space=pltpu.SMEM)
    vmem = pl.BlockSpec(memory_space=pltpu.VMEM)
    _, ah, al, gram = pl.pallas_call(
        ghost_kernel,
        out_shape=[
            pltpu.VMEM((NBD * BS, K), F32),
            pltpu.VMEM((NBD * BS, K), BF16),
            pltpu.VMEM((NBD * BS, K), BF16),
            jax.ShapeDtypeStruct((2 * HALF, BS), F32),
        ],
        in_specs=[smem] * 4 + [vmem] * 6,
        out_specs=[vmem] * 4,
        scratch_shapes=[
            pltpu.VMEM(((4 * GMAX + 1) * BS, K), BF16),
            pltpu.VMEM(((4 * GMAX + 1) * BS, K), BF16),
        ],
        input_output_aliases={4: 0},
        compiler_params=pltpu.CompilerParams(vmem_limit_bytes=16 * MB),
        cost_estimate=pl.CostEstimate(flops=3 * 10**9, bytes_accessed=25 * MB, transcendentals=0),
        name="apply_ghosts",
    )(*lists, on_vmem(part), on_vmem(held), *[on_vmem(g) for g in ghosts])
    return ah, al, gram


def exact(a, b, ca=1, cb=0):
    return lax.dot_general(
        a, b, (((ca,), (cb,)), ((), ())), precision=lax.Precision.HIGHEST, preferred_element_type=F32
    )


def spread(x):
    return jnp.broadcast_to(x, (8, BS))


def tree_sum(terms):
    while len(terms) > 1:
        pairs = [terms[i] + terms[i + 1] for i in range(0, len(terms) - 1, 2)]
        terms = pairs + terms[len(terms) - len(terms) % 2 :]
    return terms[0]


def eliminate(columns):
    groups, wide = BS // 8, range(len(columns))
    state = [[c[8 * g : 8 * g + 8] for c in columns] for g in range(groups)]
    outs = [[] for _ in columns]
    place = lax.broadcasted_iota(jnp.int32, (8, BS), 0)
    for at in range(groups):
        near = range(at + 1, min(groups, at + 1 + NEAR))
        first = {g: [spread(state[g][0][:, 8 * at + k : 8 * at + k + 1]) for k in range(8)] for g in (at, *near)}
        a = {(i, j): spread(first[at][j][i : i + 1]) for i in range(8) for j in range(i, 8)}
        w = [[spread(state[at][c][k : k + 1]) for c in wide] for k in range(8)]
        inverse, lower = [], {}
        for k in range(8):
            inverse.append(1.0 / a[k, k])
            for i in range(k + 1, 8):
                m = lower[i, k] = a[k, i] * inverse[k]
                for j in range(i, 8):
                    a[i, j] = a[i, j] - m * a[k, j]
                for c in wide:
                    w[i][c] = w[i][c] - m * w[k][c]
        for k in range(8):
            scale = lax.rsqrt(a[k, k])
            for c in wide:
                outs[c].append((w[k][c] * scale)[:1])
        if at + 1 == groups:
            break
        q = [[w[k][c] * inverse[k] for c in wide] for k in range(8)]
        for k in range(6, -1, -1):
            for m in range(k + 1, 8):
                for c in wide:
                    q[k][c] = q[k][c] - lower[m, k] * q[m][c]
        for g in near:
            for c in wide:
                state[g][c] = state[g][c] - tree_sum([first[g][k] * q[k][c] for k in range(8)])
        far = at + 1 + NEAR
        if far < groups:
            rows = []
            for c in wide:
                block = q[0][c]
                for k in range(1, 8):
                    block = jnp.where(place == k, q[k][c], block)
                rows.append(block)
            parts = [jnp.concatenate(rows, axis=1)]
            if at:
                parts.insert(0, jnp.zeros((8 * at, BS * len(columns)), F32))
            parts.append(jnp.zeros((BS - 8 * at - 8, BS * len(columns)), F32))
            update = exact(
                jnp.concatenate([state[g][0] for g in range(far, groups)], axis=0),
                jnp.concatenate(parts, axis=0),
            )
            for n, g in enumerate(range(far, groups)):
                for c in wide:
                    state[g][c] = state[g][c] - update[8 * n : 8 * n + 8, c * BS : c * BS + BS]
    return [jnp.concatenate(rows, axis=0) for rows in outs]


def factor(low, high):
    packed = jnp.concatenate([low, high], axis=0) * (1.0 / NROWS)
    mixed, corner, tail = packed[:BS], packed[BS : 2 * BS], packed[2 * BS : 2 * BS + 1]
    i = lax.broadcasted_iota(jnp.int32, (BS, BS), 0)
    j = lax.broadcasted_iota(jnp.int32, (BS, BS), 1)
    unit = jnp.where(i == j, 1.0, 0.0).astype(F32)
    turned = mixed.T
    first = jnp.where(i <= j, mixed, turned)
    second = jnp.where(i > j, mixed, jnp.where(i < j, turned, tail))
    r11, r12, x11 = eliminate([first, corner, unit])
    x11 = jnp.where(i >= j, x11, 0.0)
    r22, x22 = eliminate([second - exact(r12, r12, 0, 0), unit])
    x22 = jnp.where(i >= j, x22, 0.0)
    x21 = -exact(x22, exact(r12, x11, 0, 0))
    r11, r22 = jnp.where(i <= j, r11, 0.0), jnp.where(i <= j, r22, 0.0)
    zero = jnp.zeros((BS, BS), F32)
    upper = jnp.concatenate(
        [jnp.concatenate([r11, r12], axis=1), jnp.concatenate([zero, r22], axis=1)], axis=0
    )
    lower = jnp.concatenate(
        [jnp.concatenate([x11, zero], axis=1), jnp.concatenate([x21, x22], axis=1)], axis=0
    )
    return upper, lower


def basis_kernel(low, high, ah, al, basis, upper, wh, wl, staged, sems):
    r, x = factor(low[...], high[...])
    upper[...] = r
    wh[...], wl[...] = split(x.T)

    def store(n):
        rows = pl.ds(pl.multiple_of(n * STORE, STORE), STORE)
        return pltpu.make_async_copy(staged.at[rows], basis.at[rows], sems.at[n])

    def chunk(n, _):
        rows = pl.ds(pl.multiple_of(n * STORE, STORE), STORE)
        h, l = ah[rows], al[rows]
        staged[rows] = dot(h, wh[...]) + dot(l, wh[...]) + dot(h, wl[...])
        store(n).start()
        return 0

    lax.fori_loop(0, NBD * BS // STORE, chunk, 0)
    for n in range(NBD * BS // STORE):
        store(n).wait()


def orthonormalize(low, high, ah, al):
    vmem = pl.BlockSpec(memory_space=pltpu.VMEM)
    return pl.pallas_call(
        basis_kernel,
        out_shape=[
            jax.ShapeDtypeStruct((NBD * BS, K), F32),
            jax.ShapeDtypeStruct((K, K), F32),
        ],
        in_specs=[vmem] * 4,
        out_specs=[pl.BlockSpec(memory_space=pltpu.HBM), vmem],
        scratch_shapes=[
            pltpu.VMEM((K, K), BF16),
            pltpu.VMEM((K, K), BF16),
            pltpu.VMEM((NBD * BS, K), F32),
            pltpu.SemaphoreType.DMA((NBD * BS // STORE,)),
        ],
        compiler_params=pltpu.CompilerParams(vmem_limit_bytes=16 * MB),
        cost_estimate=pl.CostEstimate(flops=10**9, bytes_accessed=7 * MB, transcendentals=0),
        name="factor_and_basis",
    )(low, high, on_vmem(ah), on_vmem(al))


def body(block_vectors, stiff_tiles, col_index, send_lists, send_counts, part_blocks):
    own_blocks = block_vectors.reshape(NBD, BS, K)
    cols = col_index.reshape(NBD * TPR)
    packed = pack_ghosts(own_blocks, send_lists.reshape(4 * GMAX), send_counts.reshape(4))
    ghosts = [
        shifted(packed[0], "px", 1),
        shifted(packed[1], "px", -1),
        shifted(packed[2], "py", 1),
        shifted(packed[3], "py", -1),
    ]
    part, held, *lists = apply_own(block_vectors, stiff_tiles.reshape(NBD * TPR, BS, BS), cols, part_blocks)
    ah, al, gram = apply_ghosts(part, held, lists, ghosts)
    low, high = sum_everywhere(gram)
    return tuple(orthonormalize(low, high, ah, al))


def solution(mesh):
    placed = (
        P(AXES, None),
        P(AXES, None, None, None),
        P(AXES, None),
        P(AXES, None, None),
        P(AXES, None),
        P(AXES),
    )
    return jax.shard_map(body, mesh=mesh, in_specs=placed, out_specs=(P(AXES, None), P()), check_vma=False)
```

time: 198 us -> 94 us (0.47)
  Pallas kernels: 126 us -> 35.7 us
  starting transfers between devices: 50 us -> 41 us
  waiting for transfers between devices: 14.5 us -> 12.3 us
    pallas_call x4, Pallas kernels: 126 us -> 35.7 us  [the longest x1 12.2 us: orthonormalize(): pl.pallas_call(basis_kernel, out_shape=[jax.ShapeDtypeStruct((NBD * BS, K...]
    ppermute x6, starting transfers between devices: 29.4 us -> 18.7 us  [sum_everywhere(): total = total + lax.ppermute(total, AXES, pair_route(dim, odd))]
    ppermute x1, starting transfers between devices: 0.01 us -> 3.42 us  [sum_everywhere(): total = mine + lax.ppermute(other, AXES, CORE_ROUTE)]
where the time goes in v2:
time: 94 us; the launch traced here: 94.2 us
  starting transfers between devices  41 us (44%)
  Pallas kernels  35.7 us (38%)
  waiting for transfers between devices  12.3 us (13%)
  local copies, waits for them, and re-layouts  3.51 us (4%)
  between operations  1.61 us (2%)
    ppermute x6, starting transfers between devices, sum_everywhere(): total = total + lax.ppermute(total, AXES, pair_route(dim, odd))  18.7 us
    ppermute x4, starting transfers between devices, shifted(): return lax.ppermute(block, axis, pairs)  12.7 us
    pallas_call x1, Pallas kernels, orthonormalize(): pl.pallas_call(basis_kernel, out_shape=[jax.ShapeDtypeStruct((NBD * BS, K...  12.2 us
    pallas_call x1, Pallas kernels, apply_own(): pl.pallas_call(own_kernel, out_shape=[pltpu.VMEM((NBD * BS, K), F32), plt...  11.6 us
    ppermute x6, waiting for transfers between devices, sum_everywhere(): total = total + lax.ppermute(total, AXES, pair_route(dim, odd))  10.5 us
    pallas_call x1, Pallas kernels, apply_ghosts(): pl.pallas_call(ghost_kernel, out_shape=[pltpu.VMEM((NBD * BS, K), F32), p...  7.74 us
    ppermute x1, starting transfers between devices, sum_everywhere(): theirs = lax.ppermute(total, AXES, CORE_ROUTE)  6.11 us
    pallas_call x1, Pallas kernels, pack_ghosts(): pl.pallas_call(pack_kernel, out_shape=[pltpu.VMEM((GMAX, BS, K), F32)] *...  4.17 us
  transfers between devices with their start and end apart: 12, of which 8 were waited for; matrix products, arithmetic and copies ran while one was open for 0% of the time, Pallas kernels for 12%

profile of v2, /device:TPU:1, one launch (start us, length us, event | category | flops | bytes accessed | tf_op | source)
XLA Modules:
  0.0 94.2 jit_solution(1285058636631105726)
XLA Ops:
  0.6 0.8 reshape.21.lists
  1.4 1.9 %copy-done = f32[3072,256]{1,0:T(8,128)S(1)} copy-done((f32[3072,256]{1,0:T(8,128)S(1)}, f32[3072,256]{1,0:T(8,128)}, u32[]{:S(2)}) %copy-start) | copy-done | bytes 3145752
  3.3 0.7 copy-done.2
  3.9 4.2 %pack_ghosts.1 = (f32[4,128,256]{2,1,0:T(8,128)}, f32[4,128,256]{2,1,0:T(8,128)}, f32[4,128,256]{2,1,0:T(8,128)}, f32[4,128,256]{2,1,0:T(8,128)}) custom-call(s32[16]{0:T(128)S(1)} %reshape.21.lists, s32[4]{0:T(128)S(1)} %bitcast.4, f32[24,128,256]{2,1,0:T(8,128)S(1)} %bitcast.3), custom_call_target="tpu_custom_call" | custom-call | bytes 4194304 | tf_op jit(solution)/shard_map/pack_ghosts/pallas_call | solution.py:107
  8.1 5.1 %collective-permute-start = (f32[4,128,256]{2,1,0:T(8,128)}, f32[4,128,256]{2,1,0:T(8,128)}, u32[]{:S(2)}, u32[]{:S(2)}) collective-permute-start(f32[4,128,256]{2,1,0:T(8,128)} %get-tuple-element.21), channel_id=1, source_target_pairs={{0,8},{8,16},{16,24},{24,32},{32,40},{40,48},{48,56},{56,64},{64,7... | collective-permute-start | bytes 1572872 | tf_op jit(solution)/shard_map/ppermute | solution.py:57
  13.2 1.3 %collective-permute-start.1 = (f32[4,128,256]{2,1,0:T(8,128)}, f32[4,128,256]{2,1,0:T(8,128)}, u32[]{:S(2)}, u32[]{:S(2)}) collective-permute-start(f32[4,128,256]{2,1,0:T(8,128)} %get-tuple-element.22), channel_id=1, source_target_pairs={{8,0},{16,8},{24,16},{32,24},{40,32},{48,40},{56,48},{64,56},{72,6... | collective-permute-start | bytes 1572872 | tf_op jit(solution)/shard_map/ppermute | solution.py:57
  14.5 4.4 %collective-permute-start.2 = (f32[4,128,256]{2,1,0:T(8,128)}, f32[4,128,256]{2,1,0:T(8,128)}, u32[]{:S(2)}, u32[]{:S(2)}) collective-permute-start(f32[4,128,256]{2,1,0:T(8,128)} %get-tuple-element.23), channel_id=1, source_target_pairs={{0,1},{1,2},{2,3},{3,4},{4,5},{5,6},{6,7},{8,9},{9,10},{10,11},{11... | collective-permute-start | bytes 1572872 | tf_op jit(solution)/shard_map/ppermute | solution.py:57
  18.9 1.9 %collective-permute-start.3 = (f32[4,128,256]{2,1,0:T(8,128)}, f32[4,128,256]{2,1,0:T(8,128)}, u32[]{:S(2)}, u32[]{:S(2)}) collective-permute-start(f32[4,128,256]{2,1,0:T(8,128)} %get-tuple-element.24), channel_id=1, source_target_pairs={{1,0},{2,1},{3,2},{4,3},{5,4},{6,5},{7,6},{9,8},{10,9},{11,10},{12... | collective-permute-start | bytes 1572872 | tf_op jit(solution)/shard_map/ppermute | solution.py:57
  20.9 0.1 copy.9
  20.9 0.1 reshape.19.cols
  21.7 11.6 %apply_own.1 = (f32[3072,256]{1,0:T(8,128)S(1)}, f32[288,128,128]{2,1,0:T(8,128)S(1)}, s32[352]{0:T(512)S(1)}, s32[352]{0:T(512)S(1)}, s32[184]{0:T(256)S(1)}, /*index=5*/s32[1]{0:T(128)}) custom-call(s32[288]{0:T(512)S(1)} %reshape.19.cols, s32[1]{0:T(128)S(6)} %copy.11.live, f32[3072,256]{1,0:T(8,128)S(1)} %copy-done.1, f32[288,128,128]{2,1,0:T(8,128)} %bitcast.5), custom_call_target="tpu_custom_call" | custom-call | flops 4000000000 | bytes 26214400 | tf_op jit(solution)/shard_map/apply_own/pallas_call | solution.py:246
  33.3 0.0 collective-permute-done.g0
  33.3 0.0 collective-permute-done.1.g1
  33.3 0.0 collective-permute-done.2.g2
  33.4 7.7 %apply_ghosts.1 = (f32[3072,256]{1,0:T(8,128)S(1)}, bf16[3072,256]{1,0:T(8,128)(2,1)S(1)}, bf16[3072,256]{1,0:T(8,128)(2,1)S(1)}, f32[272,128]{1,0:T(8,128)S(1)}) custom-call(s32[352]{0:T(512)S(1)} %get-tuple-element.15.gt, s32[352]{0:T(512)S(1)} %get-tuple-element.16.gb, s32[184]{0:T(256)S(1)} %get-tuple-element.17.gr, ...), custom_call_target="tpu_custom_call", output_to_operand_aliasing={{0}: (4, {})} | custom-call | flops 3000000000 | bytes 26214400 | tf_op jit(solution)/shard_map/apply_ghosts/pallas_call | solution.py:312
  41.1 3.4 %collective-permute-start.4 = (f32[136,128]{1,0:T(8,128)S(1)}, f32[136,128]{1,0:T(8,128)S(1)}, u32[]{:S(2)}, u32[]{:S(2)}) collective-permute-start(f32[136,128]{1,0:T(8,128)S(1)} %constant_dynamic-slice_fusion), channel_id=1, source_target_pairs={{0,1},{1,0},{2,3},{3,2},{4,5},{5,4},{6,7},{7,6},{32,33},{33,32},{3... | collective-permute-start | bytes 208904 | tf_op jit(solution)/shard_map/ppermute | solution.py:64
  44.5 0.9 collective-permute-done.4
  45.5 1.3 %collective-permute-start.5 = (f32[136,128]{1,0:T(8,128)S(1)}, f32[136,128]{1,0:T(8,128)S(1)}, u32[]{:S(2)}, u32[]{:S(2)}) collective-permute-start(f32[136,128]{1,0:T(8,128)S(1)} %dynamic-slice_add_fusion), channel_id=1, source_target_pairs={{0,8},{1,9},{2,10},{3,11},{4,12},{5,13},{6,14},{7,15},{32,40},{33,... | collective-permute-start | bytes 208904 | tf_op jit(solution)/shard_map/ppermute | solution.py:67
  46.7 2.0 %collective-permute-done.5 = f32[136,128]{1,0:T(8,128)S(1)} collective-permute-done((f32[136,128]{1,0:T(8,128)S(1)}, f32[136,128]{1,0:T(8,128)S(1)}, u32[]{:S(2)}, u32[]{:S(2)}) %collective-permute-start.5) | collective-permute-done | bytes 69664 | tf_op jit(solution)/shard_map/ppermute | solution.py:67
  48.7 5.5 %collective-permute-start.6 = (f32[136,128]{1,0:T(8,128)S(1)}, f32[136,128]{1,0:T(8,128)S(1)}, u32[]{:S(2)}, u32[]{:S(2)}) collective-permute-start(f32[136,128]{1,0:T(8,128)S(1)} %add.35), channel_id=1, source_target_pairs={{0,24},{1,25},{2,26},{3,27},{4,28},{5,29},{6,30},{7,31},{32,56},{3... | collective-permute-start | bytes 208904 | tf_op jit(solution)/shard_map/ppermute | solution.py:67
  54.3 1.7 %collective-permute-done.6 = f32[136,128]{1,0:T(8,128)S(1)} collective-permute-done((f32[136,128]{1,0:T(8,128)S(1)}, f32[136,128]{1,0:T(8,128)S(1)}, u32[]{:S(2)}, u32[]{:S(2)}) %collective-permute-start.6) | collective-permute-done | bytes 69664 | tf_op jit(solution)/shard_map/ppermute | solution.py:67
  56.0 2.9 %collective-permute-start.7 = (f32[136,128]{1,0:T(8,128)S(1)}, f32[136,128]{1,0:T(8,128)S(1)}, u32[]{:S(2)}, u32[]{:S(2)}) collective-permute-start(f32[136,128]{1,0:T(8,128)S(1)} %add.36), channel_id=1, source_target_pairs={{0,32},{1,33},{2,34},{3,35},{4,36},{5,37},{6,38},{7,39},{32,0},{33... | collective-permute-start | bytes 208904 | tf_op jit(solution)/shard_map/ppermute | solution.py:67
  58.8 1.7 %collective-permute-done.7 = f32[136,128]{1,0:T(8,128)S(1)} collective-permute-done((f32[136,128]{1,0:T(8,128)S(1)}, f32[136,128]{1,0:T(8,128)S(1)}, u32[]{:S(2)}, u32[]{:S(2)}) %collective-permute-start.7) | collective-permute-done | bytes 69664 | tf_op jit(solution)/shard_map/ppermute | solution.py:67
  60.6 3.2 %collective-permute-start.8 = (f32[136,128]{1,0:T(8,128)S(1)}, f32[136,128]{1,0:T(8,128)S(1)}, u32[]{:S(2)}, u32[]{:S(2)}) collective-permute-start(f32[136,128]{1,0:T(8,128)S(1)} %add.37), channel_id=1, source_target_pairs={{0,96},{1,97},{2,98},{3,99},{4,100},{5,101},{6,102},{7,103},{32,64... | collective-permute-start | bytes 208904 | tf_op jit(solution)/shard_map/ppermute | solution.py:67
  63.8 1.7 %collective-permute-done.8 = f32[136,128]{1,0:T(8,128)S(1)} collective-permute-done((f32[136,128]{1,0:T(8,128)S(1)}, f32[136,128]{1,0:T(8,128)S(1)}, u32[]{:S(2)}, u32[]{:S(2)}) %collective-permute-start.8) | collective-permute-done | bytes 69664 | tf_op jit(solution)/shard_map/ppermute | solution.py:67
  65.5 2.0 %collective-permute-start.9 = (f32[136,128]{1,0:T(8,128)S(1)}, f32[136,128]{1,0:T(8,128)S(1)}, u32[]{:S(2)}, u32[]{:S(2)}) collective-permute-start(f32[136,128]{1,0:T(8,128)S(1)} %add.38), channel_id=1, source_target_pairs={{0,2},{1,3},{2,0},{3,1},{4,6},{5,7},{6,4},{7,5},{32,34},{33,35},{3... | collective-permute-start | bytes 208904 | tf_op jit(solution)/shard_map/ppermute | solution.py:67
  67.5 1.7 %collective-permute-done.9 = f32[136,128]{1,0:T(8,128)S(1)} collective-permute-done((f32[136,128]{1,0:T(8,128)S(1)}, f32[136,128]{1,0:T(8,128)S(1)}, u32[]{:S(2)}, u32[]{:S(2)}) %collective-permute-start.9) | collective-permute-done | bytes 69664 | tf_op jit(solution)/shard_map/ppermute | solution.py:67
  69.2 3.8 %collective-permute-start.10 = (f32[136,128]{1,0:T(8,128)S(1)}, f32[136,128]{1,0:T(8,128)S(1)}, u32[]{:S(2)}, u32[]{:S(2)}) collective-permute-start(f32[136,128]{1,0:T(8,128)S(1)} %add.39), channel_id=1, source_target_pairs={{0,6},{1,7},{2,4},{3,5},{4,2},{5,3},{6,0},{7,1},{32,38},{33,39},{3... | collective-permute-start | bytes 208904 | tf_op jit(solution)/shard_map/ppermute | solution.py:67
  73.0 1.7 %collective-permute-done.10 = f32[136,128]{1,0:T(8,128)S(1)} collective-permute-done((f32[136,128]{1,0:T(8,128)S(1)}, f32[136,128]{1,0:T(8,128)S(1)}, u32[]{:S(2)}, u32[]{:S(2)}) %collective-permute-start.10) | collective-permute-done | bytes 69664 | tf_op jit(solution)/shard_map/ppermute | solution.py:67
  74.7 6.1 %collective-permute-start.11 = (f32[136,128]{1,0:T(8,128)S(1)}, f32[136,128]{1,0:T(8,128)S(1)}, u32[]{:S(2)}, u32[]{:S(2)}) collective-permute-start(f32[136,128]{1,0:T(8,128)S(1)} %add.40), channel_id=1, source_target_pairs={{0,1},{1,0},{2,3},{3,2},{4,5},{5,4},{6,7},{7,6},{32,33},{33,32},{3... | collective-permute-start | bytes 208904 | tf_op jit(solution)/shard_map/ppermute | solution.py:68
  80.9 0.9 collective-permute-done.11
  81.8 12.2 %factor_and_basis.1 = (f32[3072,256]{1,0:T(8,128)}, f32[256,256]{1,0:T(8,128)}) custom-call(f32[136,128]{1,0:T(8,128)S(1)} %get-tuple-element.29.low, f32[136,128]{1,0:T(8,128)S(1)} %get-tuple-element.28.high, bf16[3072,256]{1,0:T(8,128)(2,1)S(1)} %get-tuple-element.26.ah, bf16[3072,256]{1,0:T(8,128)(2,1)S(1)} %get-tuple-element.27.al), custom_call_target="tpu_custom_call" | custom-call | flops 1000000000 | bytes 7340032 | tf_op jit(solution)/shard_map/factor_and_basis/pallas_call | solution.py:454
  (16 shorter events, 0.1 us)
Async XLA Ops:
  1.4 1.9 %copy-start = (f32[3072,256]{1,0:T(8,128)S(1)}, f32[3072,256]{1,0:T(8,128)}, u32[]{:S(2)}) copy-start(f32[3072,256]{1,0:T(8,128)} %own.1) | copy-start | bytes 9437188
  3.3 0.7 copy-start.2
  3.9 16.9 %copy-start.3 = (s32[24,12]{0,1:T(8,128)S(1)}, s32[24,12]{0,1:T(8,128)}, u32[]{:S(2)}) copy-start(s32[24,12]{0,1:T(8,128)} %param.8) | copy-start | bytes 3460
  3.9 17.8 %copy-start.1 = (f32[3072,256]{1,0:T(8,128)S(1)}, f32[3072,256]{1,0:T(8,128)}, u32[]{:S(2)}) copy-start(f32[3072,256]{1,0:T(8,128)} %own.1) | copy-start | bytes 9437188
  8.1 25.2 %collective-permute-start = (f32[4,128,256]{2,1,0:T(8,128)}, f32[4,128,256]{2,1,0:T(8,128)}, u32[]{:S(2)}, u32[]{:S(2)}) collective-permute-start(f32[4,128,256]{2,1,0:T(8,128)} %get-tuple-element.21), channel_id=1, source_target_pairs={{0,8},{8,16},{16,24},{24,32},{32,40},{40,48},{48,56},{56,64},{64,7... | collective-permute-start | bytes 1572872 | tf_op jit(solution)/shard_map/ppermute | solution.py:57
  13.2 20.1 %collective-permute-start.1 = (f32[4,128,256]{2,1,0:T(8,128)}, f32[4,128,256]{2,1,0:T(8,128)}, u32[]{:S(2)}, u32[]{:S(2)}) collective-permute-start(f32[4,128,256]{2,1,0:T(8,128)} %get-tuple-element.22), channel_id=1, source_target_pairs={{8,0},{16,8},{24,16},{32,24},{40,32},{48,40},{56,48},{64,56},{72,6... | collective-permute-start | bytes 1572872 | tf_op jit(solution)/shard_map/ppermute | solution.py:57
  14.5 18.8 %collective-permute-start.2 = (f32[4,128,256]{2,1,0:T(8,128)}, f32[4,128,256]{2,1,0:T(8,128)}, u32[]{:S(2)}, u32[]{:S(2)}) collective-permute-start(f32[4,128,256]{2,1,0:T(8,128)} %get-tuple-element.23), channel_id=1, source_target_pairs={{0,1},{1,2},{2,3},{3,4},{4,5},{5,6},{6,7},{8,9},{9,10},{10,11},{11... | collective-permute-start | bytes 1572872 | tf_op jit(solution)/shard_map/ppermute | solution.py:57
  18.9 14.4 %collective-permute-start.3 = (f32[4,128,256]{2,1,0:T(8,128)}, f32[4,128,256]{2,1,0:T(8,128)}, u32[]{:S(2)}, u32[]{:S(2)}) collective-permute-start(f32[4,128,256]{2,1,0:T(8,128)} %get-tuple-element.24), channel_id=1, source_target_pairs={{1,0},{2,1},{3,2},{4,3},{5,4},{6,5},{7,6},{9,8},{10,9},{11,10},{12... | collective-permute-start | bytes 1572872 | tf_op jit(solution)/shard_map/ppermute | solution.py:57
  41.1 4.3 %collective-permute-start.4 = (f32[136,128]{1,0:T(8,128)S(1)}, f32[136,128]{1,0:T(8,128)S(1)}, u32[]{:S(2)}, u32[]{:S(2)}) collective-permute-start(f32[136,128]{1,0:T(8,128)S(1)} %constant_dynamic-slice_fusion), channel_id=1, source_target_pairs={{0,1},{1,0},{2,3},{3,2},{4,5},{5,4},{6,7},{7,6},{32,33},{33,32},{3... | collective-permute-start | bytes 208904 | tf_op jit(solution)/shard_map/ppermute | solution.py:64
  45.5 3.2 %collective-permute-start.5 = (f32[136,128]{1,0:T(8,128)S(1)}, f32[136,128]{1,0:T(8,128)S(1)}, u32[]{:S(2)}, u32[]{:S(2)}) collective-permute-start(f32[136,128]{1,0:T(8,128)S(1)} %dynamic-slice_add_fusion), channel_id=1, source_target_pairs={{0,8},{1,9},{2,10},{3,11},{4,12},{5,13},{6,14},{7,15},{32,40},{33,... | collective-permute-start | bytes 208904 | tf_op jit(solution)/shard_map/ppermute | solution.py:67
  48.7 7.2 %collective-permute-start.6 = (f32[136,128]{1,0:T(8,128)S(1)}, f32[136,128]{1,0:T(8,128)S(1)}, u32[]{:S(2)}, u32[]{:S(2)}) collective-permute-start(f32[136,128]{1,0:T(8,128)S(1)} %add.35), channel_id=1, source_target_pairs={{0,24},{1,25},{2,26},{3,27},{4,28},{5,29},{6,30},{7,31},{32,56},{3... | collective-permute-start | bytes 208904 | tf_op jit(solution)/shard_map/ppermute | solution.py:67
  56.0 4.6 %collective-permute-start.7 = (f32[136,128]{1,0:T(8,128)S(1)}, f32[136,128]{1,0:T(8,128)S(1)}, u32[]{:S(2)}, u32[]{:S(2)}) collective-permute-start(f32[136,128]{1,0:T(8,128)S(1)} %add.36), channel_id=1, source_target_pairs={{0,32},{1,33},{2,34},{3,35},{4,36},{5,37},{6,38},{7,39},{32,0},{33... | collective-permute-start | bytes 208904 | tf_op jit(solution)/shard_map/ppermute | solution.py:67
  60.6 4.9 %collective-permute-start.8 = (f32[136,128]{1,0:T(8,128)S(1)}, f32[136,128]{1,0:T(8,128)S(1)}, u32[]{:S(2)}, u32[]{:S(2)}) collective-permute-start(f32[136,128]{1,0:T(8,128)S(1)} %add.37), channel_id=1, source_target_pairs={{0,96},{1,97},{2,98},{3,99},{4,100},{5,101},{6,102},{7,103},{32,64... | collective-permute-start | bytes 208904 | tf_op jit(solution)/shard_map/ppermute | solution.py:67
  65.5 3.7 %collective-permute-start.9 = (f32[136,128]{1,0:T(8,128)S(1)}, f32[136,128]{1,0:T(8,128)S(1)}, u32[]{:S(2)}, u32[]{:S(2)}) collective-permute-start(f32[136,128]{1,0:T(8,128)S(1)} %add.38), channel_id=1, source_target_pairs={{0,2},{1,3},{2,0},{3,1},{4,6},{5,7},{6,4},{7,5},{32,34},{33,35},{3... | collective-permute-start | bytes 208904 | tf_op jit(solution)/shard_map/ppermute | solution.py:67
  69.2 5.5 %collective-permute-start.10 = (f32[136,128]{1,0:T(8,128)S(1)}, f32[136,128]{1,0:T(8,128)S(1)}, u32[]{:S(2)}, u32[]{:S(2)}) collective-permute-start(f32[136,128]{1,0:T(8,128)S(1)} %add.39), channel_id=1, source_target_pairs={{0,6},{1,7},{2,4},{3,5},{4,2},{5,3},{6,0},{7,1},{32,38},{33,39},{3... | collective-permute-start | bytes 208904 | tf_op jit(solution)/shard_map/ppermute | solution.py:67
  74.7 7.0 %collective-permute-start.11 = (f32[136,128]{1,0:T(8,128)S(1)}, f32[136,128]{1,0:T(8,128)S(1)}, u32[]{:S(2)}, u32[]{:S(2)}) collective-permute-start(f32[136,128]{1,0:T(8,128)S(1)} %add.40), channel_id=1, source_target_pairs={{0,1},{1,0},{2,3},{3,2},{4,5},{5,4},{6,7},{7,6},{32,33},{33,32},{3... | collective-permute-start | bytes 208904 | tf_op jit(solution)/shard_map/ppermute | solution.py:68

commit v3 on v2

--- a/solution.py
+++ b/solution.py
@@ -20,8 +20,8 @@
 F32 = jnp.float32
 BF16 = jnp.bfloat16
 MB = 1 << 20
-CHUNK = 4
-AHEAD = 4
+CHUNK = 8
+AHEAD = 6
 NEAR = 2
 STORE = 512
 
@@ -51,10 +51,19 @@
 CORE_ROUTE = route(lambda x, y, z, core: (x, y, z, 1 - core))
 
 
-def shifted(block, axis, distance):
-    devices = range(lax.axis_size(axis))
-    pairs = [(i - distance, i) for i in devices if i - distance in devices]
-    return lax.ppermute(block, axis, pairs)
+def far_route(dim):
+    def move(x, y, z, core):
+        at = [x, y, z]
+        at[dim] ^= 2
+        return (*at, core)
+
+    return route(move)
+
+
+def swapped(block, axis, odd):
+    n = lax.axis_size(axis)
+    pairs = [(i, i + 1) for i in range(1 if odd else 0, n - 1, 2)]
+    return lax.ppermute(block, axis, pairs + [(j, i) for i, j in pairs])
 
 
 def sum_everywhere(packed):
@@ -63,8 +72,9 @@
     other = lax.dynamic_slice_in_dim(packed, (1 - core) * HALF, HALF, 0)
     total = mine + lax.ppermute(other, AXES, CORE_ROUTE)
     for dim in range(3):
-        for odd in (False, True):
-            total = total + lax.ppermute(total, AXES, pair_route(dim, odd))
+        routes = (pair_route(dim, False), pair_route(dim, True), far_route(dim))
+        near, wrap, far = [lax.ppermute(total, AXES, r) for r in routes]
+        total = (total + near) + (wrap + far)
     theirs = lax.ppermute(total, AXES, CORE_ROUTE)
     low = jnp.where(core == 0, total, theirs)
     high = jnp.where(core == 0, theirs, total)
@@ -75,45 +85,54 @@
     return pltpu.with_memory_space_constraint(x, pltpu.VMEM)
 
 
-def pack_kernel(lists, counts, own, *refs):
-    outs, sems = refs[:4], refs[4]
-
-    def copy(e, s, block):
-        return pltpu.make_async_copy(own.at[block], outs[e].at[s], sems.at[e, s])
-
-    for e in range(4):
+def pack_kernel(parity, lists, counts, own, *refs):
+    outs, held, in_sems, out_sems = refs[:4], refs[4], refs[5], refs[6]
+    odd_px, odd_py = parity[0], parity[1]
+    directions = (odd_px, 1 - odd_px, 2 + odd_py, 3 - odd_py)
+
+    def fetch(n, s):
+        block = lists[0, directions[n], s]
+        rows = pl.ds(pl.multiple_of(block * BS, BS), BS)
+        return pltpu.make_async_copy(own.at[rows], held.at[n, s], in_sems.at[n, s])
+
+    def store(n, s):
+        return pltpu.make_async_copy(held.at[n, s], outs[n].at[s], out_sems.at[n, s])
+
+    for n in range(4):
         for s in range(GMAX):
-            alive = s < counts[e]
-
-            @pl.when(alive)
+            fetch(n, s).start()
+    for n in range(4):
+        for s in range(GMAX):
+            fetch(n, s).wait()
+
+            @pl.when(s >= counts[0, directions[n]])
             def _():
-                copy(e, s, lists[e * GMAX + s]).start()
-
-            @pl.when(jnp.logical_not(alive))
-            def _():
-                outs[e][s] = jnp.zeros((BS, K), F32)
-
-    for e in range(4):
+                held[n, s] = jnp.zeros((BS, K), F32)
+
+            store(n, s).start()
+    for n in range(4):
         for s in range(GMAX):
-
-            @pl.when(s < counts[e])
-            def _():
-                copy(e, s, 0).wait()
-
-
-def pack_ghosts(own_blocks, lists, counts):
+            store(n, s).wait()
+
+
+def pack_ghosts(parity, lists, counts, own):
     smem = pl.BlockSpec(memory_space=pltpu.SMEM)
-    vmem = pl.BlockSpec(memory_space=pltpu.VMEM)
+    hbm = pl.BlockSpec(memory_space=pltpu.HBM)
+    anywhere = pl.BlockSpec(memory_space=pl.ANY)
     return pl.pallas_call(
         pack_kernel,
-        out_shape=[pltpu.VMEM((GMAX, BS, K), F32)] * 4,
-        in_specs=[smem, smem, pl.BlockSpec(memory_space=pltpu.HBM)],
-        out_specs=[vmem] * 4,
-        scratch_shapes=[pltpu.SemaphoreType.DMA((4, GMAX))],
+        out_shape=[jax.ShapeDtypeStruct((GMAX, BS, K), F32)] * 4,
+        in_specs=[smem, smem, smem, hbm],
+        out_specs=[anywhere] * 4,
+        scratch_shapes=[
+            pltpu.VMEM((4, GMAX, BS, K), F32),
+            pltpu.SemaphoreType.DMA((4, GMAX)),
+            pltpu.SemaphoreType.DMA((4, GMAX)),
+        ],
         compiler_params=pltpu.CompilerParams(vmem_limit_bytes=4 * MB),
         cost_estimate=pl.CostEstimate(flops=0, bytes_accessed=4 * MB, transcendentals=0),
         name="pack_ghosts",
-    )(lists, counts, own_blocks)
+    )(parity, lists, counts, pltpu.with_memory_space_constraint(own, pltpu.HBM))
 
 
 def split(x):
@@ -125,18 +144,21 @@
     return lax.dot_general(a, b, (((1,), (0,)), ((), ())), preferred_element_type=F32)
 
 
-def pair_lists(cols, live, own_list, ghost_list):
+def pair_lists(parity, cols, live, own_list, ghost_list):
+    turn_px, turn_py = GMAX * (1 - parity[0]), GMAX * (1 - parity[1])
+
     def row_pairs(row, counts):
         starts = counts
         for t in range(TPR):
-            c = cols[row * TPR + t]
+            c = cols[row, t]
             ghost = jnp.where(c >= NBD, 1, 0)
-            for (tile, block, _, _), n, first, mine in (
-                (own_list, counts[0], 0, 1 - ghost),
-                (ghost_list, counts[1], NBD, ghost),
+            g = c - NBD
+            for (tile, block, _, _), n, at in (
+                (own_list, counts[0], c),
+                (ghost_list, counts[1], g ^ jnp.where(g < 2 * GMAX, turn_px, turn_py)),
             ):
                 tile[n] = row * TPR + t
-                block[n] = c - first
+                block[n] = at
             counts = (counts[0] + 1 - ghost, counts[1] + ghost)
         ends = []
         for (tile, block, rows, _), n, start, zero in (
@@ -179,34 +201,25 @@
         acc[at] += dot(th, bh) + dot(tl, bh) + dot(th, bl)
 
 
-def own_kernel(cols, live, own, tiles, part, held, gt, gb, gr, gn, xv, xh, xl, ot, ob, orow, on, xsem, tsem):
-    x_copies = [
-        pltpu.make_async_copy(own.at[pl.ds(i * BS * 6, BS * 6)], xv.at[pl.ds(i * BS * 6, BS * 6)], xsem.at[i])
-        for i in range(4)
-    ]
-
+def own_kernel(parity, cols, live, own, tiles, part, held, gt, gb, gr, gn, xh, xl, ot, ob, orow, on, sems):
     def fetch(row):
         rows = pl.ds(row * TPR, TPR)
-        return pltpu.make_async_copy(tiles.at[rows], held.at[rows], tsem.at[row])
-
-    for c in x_copies:
-        c.start()
+        return pltpu.make_async_copy(tiles.at[rows], held.at[rows], sems.at[row])
+
     for row in range(AHEAD):
         fetch(row).start()
     own_list, ghost_list = (ot, ob, orow, on), (gt, gb, gr, gn)
-    pair_lists(cols, live, own_list, ghost_list)
+    pair_lists(parity, cols, live, own_list, ghost_list)
     part[...] = jnp.zeros_like(part)
     xh[NBD * BS :] = jnp.zeros((BS, K), BF16)
     xl[NBD * BS :] = jnp.zeros((BS, K), BF16)
-    for i, c in enumerate(x_copies):
-        c.wait()
-
-        def convert(b, _):
-            rows = pl.ds(pl.multiple_of((i * 6 + b) * BS, BS), BS)
-            xh[rows], xl[rows] = split(xv[rows])
-            return 0
-
-        lax.fori_loop(0, 6, convert, 0)
+
+    def convert(b, _):
+        rows = pl.ds(pl.multiple_of(b * BS, BS), BS)
+        xh[rows], xl[rows] = split(own[rows])
+        return 0
+
+    lax.fori_loop(0, NBD, convert, 0)
 
     def arrive(row, _):
         fetch(row).wait()
@@ -239,10 +252,9 @@
     ]
 
 
-def apply_own(own, tiles, cols, live):
+def apply_own(parity, cols, live, own, tiles):
     smem = pl.BlockSpec(memory_space=pltpu.SMEM)
     vmem = pl.BlockSpec(memory_space=pltpu.VMEM)
-    hbm = pl.BlockSpec(memory_space=pltpu.HBM)
     return pl.pallas_call(
         own_kernel,
         out_shape=[
@@ -250,20 +262,18 @@
             pltpu.VMEM((NBD * TPR, BS, BS), F32),
             *list_shapes(jax.ShapeDtypeStruct),
         ],
-        in_specs=[smem, smem, hbm, hbm],
-        out_specs=[vmem, vmem] + [smem] * 4,
+        in_specs=[smem, smem, smem, vmem, pl.BlockSpec(memory_space=pltpu.HBM)],
+        out_specs=[vmem] * 2 + [smem] * 4,
         scratch_shapes=[
-            pltpu.VMEM((NBD * BS, K), F32),
             pltpu.VMEM(((NBD + 1) * BS, K), BF16),
             pltpu.VMEM(((NBD + 1) * BS, K), BF16),
             *list_shapes(pltpu.SMEM),
-            pltpu.SemaphoreType.DMA((4,)),
             pltpu.SemaphoreType.DMA((NBD,)),
         ],
-        compiler_params=pltpu.CompilerParams(vmem_limit_bytes=12 * MB),
+        compiler_params=pltpu.CompilerParams(vmem_limit_bytes=8 * MB),
         cost_estimate=pl.CostEstimate(flops=4 * 10**9, bytes_accessed=25 * MB, transcendentals=0),
         name="apply_own",
-    )(cols, live, own, tiles)
+    )(parity, cols, live, on_vmem(own), pltpu.with_memory_space_constraint(tiles, pltpu.HBM))
 
 
 def gram_pack(high, low):
@@ -279,14 +289,18 @@
     return jnp.concatenate([jnp.where(i <= j, first, second), gram[:BS, BS:], tail], axis=0)
 
 
-def ghost_kernel(gt, gb, gr, gn, part, held, g0, g1, g2, g3, total, ah, al, gram, xh, xl):
+def ghost_kernel(gt, gb, gr, gn, part, held, g0, g1, g2, g3, total, ah, al, gram, xh, xl, xv, sems):
+    arrivals = [pltpu.make_async_copy(g, xv.at[e], sems.at[e]) for e, g in enumerate((g0, g1, g2, g3))]
+    for c in arrivals:
+        c.start()
     xh[4 * GMAX * BS :] = jnp.zeros((BS, K), BF16)
     xl[4 * GMAX * BS :] = jnp.zeros((BS, K), BF16)
-    for e, g in enumerate((g0, g1, g2, g3)):
+    for e, c in enumerate(arrivals):
+        c.wait()
 
         def convert(s, _):
             rows = pl.ds(pl.multiple_of((e * GMAX + s) * BS, BS), BS)
-            xh[rows], xl[rows] = split(g[s])
+            xh[rows], xl[rows] = split(xv[e, s])
             return 0
 
         lax.fori_loop(0, GMAX, convert, 0)
@@ -309,6 +323,7 @@
 def apply_ghosts(part, held, lists, ghosts):
     smem = pl.BlockSpec(memory_space=pltpu.SMEM)
     vmem = pl.BlockSpec(memory_space=pltpu.VMEM)
+    anywhere = pl.BlockSpec(memory_space=pl.ANY)
     _, ah, al, gram = pl.pallas_call(
         ghost_kernel,
         out_shape=[
@@ -317,17 +332,19 @@
             pltpu.VMEM((NBD * BS, K), BF16),
             jax.ShapeDtypeStruct((2 * HALF, BS), F32),
         ],
-        in_specs=[smem] * 4 + [vmem] * 6,
+        in_specs=[smem] * 4 + [vmem] * 2 + [anywhere] * 4,
         out_specs=[vmem] * 4,
         scratch_shapes=[
             pltpu.VMEM(((4 * GMAX + 1) * BS, K), BF16),
             pltpu.VMEM(((4 * GMAX + 1) * BS, K), BF16),
+            pltpu.VMEM((4, GMAX, BS, K), F32),
+            pltpu.SemaphoreType.DMA((4,)),
         ],
         input_output_aliases={4: 0},
         compiler_params=pltpu.CompilerParams(vmem_limit_bytes=16 * MB),
         cost_estimate=pl.CostEstimate(flops=3 * 10**9, bytes_accessed=25 * MB, transcendentals=0),
         name="apply_ghosts",
-    )(*lists, on_vmem(part), on_vmem(held), *[on_vmem(g) for g in ghosts])
+    )(*lists, on_vmem(part), on_vmem(held), *ghosts)
     return ah, al, gram
 
 
@@ -472,16 +489,16 @@
 
 
 def body(block_vectors, stiff_tiles, col_index, send_lists, send_counts, part_blocks):
-    own_blocks = block_vectors.reshape(NBD, BS, K)
-    cols = col_index.reshape(NBD * TPR)
-    packed = pack_ghosts(own_blocks, send_lists.reshape(4 * GMAX), send_counts.reshape(4))
+    parity = jnp.stack([lax.axis_index("px") % 2, lax.axis_index("py") % 2]).astype(jnp.int32)
+    tiles = stiff_tiles.reshape(NBD * TPR, BS, BS)
+    packed = pack_ghosts(parity, send_lists, send_counts, block_vectors)
     ghosts = [
-        shifted(packed[0], "px", 1),
-        shifted(packed[1], "px", -1),
-        shifted(packed[2], "py", 1),
-        shifted(packed[3], "py", -1),
+        swapped(packed[0], "px", False),
+        swapped(packed[1], "px", True),
+        swapped(packed[2], "py", False),
+        swapped(packed[3], "py", True),
     ]
-    part, held, *lists = apply_own(block_vectors, stiff_tiles.reshape(NBD * TPR, BS, BS), cols, part_blocks)
+    part, held, *lists = apply_own(parity, col_index, part_blocks, block_vectors, tiles)
     ah, al, gram = apply_ghosts(part, held, lists, ghosts)
     low, high = sum_everywhere(gram)
     return tuple(orthonormalize(low, high, ah, al))

time: 94 us -> 81.4 us (0.87)
  starting transfers between devices: 41 us -> 31.5 us
  Pallas kernels: 35.7 us -> 33.4 us
  local copies, waits for them, and re-layouts: 3.51 us -> 1.62 us
  waiting for transfers between devices: 12.3 us -> 13.3 us
    ppermute x10 -> x13, starting transfers between devices: 31.4 us -> 23.3 us  [the longest x9 15.5 us: sum_everywhere(): near, wrap, far = [lax.ppermute(total, AXES, r) for r in routes]]
    pallas_call x1, Pallas kernels: 11.6 us -> 9.79 us  [apply_own(): pl.pallas_call(own_kernel, out_shape=[pltpu.VMEM((NBD * BS, K), F32), plt...]
    ppermute x1, starting transfers between devices: 6.11 us -> 4.98 us  [sum_everywhere(): theirs = lax.ppermute(total, AXES, CORE_ROUTE)]
    ppermute x10 -> x13, waiting for transfers between devices: 10.5 us -> 11.5 us  [the longest x9 11.5 us: sum_everywhere(): near, wrap, far = [lax.ppermute(total, AXES, r) for r in routes]]
    unnamed x9, local copies, waits for them, and re-layouts: 2.64 us -> 1.61 us
  transfers between devices with their start and end apart: 12 -> 15, of which waited for: 8 -> 9; matrix products, arithmetic and copies ran while one was open for 0% -> 0% of each run, Pallas kernels for 12% -> 12%
where the time goes in v3:
time: 81.4 us; the launch traced here: 81.6 us
  Pallas kernels  33.4 us (41%)
  starting transfers between devices  31.5 us (39%)
  waiting for transfers between devices  13.3 us (16%)
  local copies, waits for them, and re-layouts  1.62 us (2%)
  between operations  1.6 us (2%)
    ppermute x9, starting transfers between devices, sum_everywhere(): near, wrap, far = [lax.ppermute(total, AXES, r) for r in routes]  15.5 us
    pallas_call x1, Pallas kernels, orthonormalize(): pl.pallas_call(basis_kernel, out_shape=[jax.ShapeDtypeStruct((NBD * BS, K...  12.2 us
    ppermute x9, waiting for transfers between devices, sum_everywhere(): near, wrap, far = [lax.ppermute(total, AXES, r) for r in routes]  11.5 us
    pallas_call x1, Pallas kernels, apply_own(): pl.pallas_call(own_kernel, out_shape=[pltpu.VMEM((NBD * BS, K), F32), plt...  9.79 us
    ppermute x4, starting transfers between devices, swapped(): return lax.ppermute(block, axis, pairs + [(j, i) for i, j in pairs])  7.83 us
    pallas_call x1, Pallas kernels, apply_ghosts(): pl.pallas_call(ghost_kernel, out_shape=[pltpu.VMEM((NBD * BS, K), F32), p...  7.62 us
    ppermute x1, starting transfers between devices, sum_everywhere(): theirs = lax.ppermute(total, AXES, CORE_ROUTE)  4.98 us
    pallas_call x1, Pallas kernels, pack_ghosts(): pl.pallas_call(pack_kernel, out_shape=[jax.ShapeDtypeStruct((GMAX, BS, K)...  3.74 us
  transfers between devices with their start and end apart: 15, of which 9 were waited for; matrix products, arithmetic and copies ran while one was open for 0% of the time, Pallas kernels for 12%

profile of v3, /device:TPU:1, one launch (start us, length us, event | category | flops | bytes accessed | tf_op | source)
XLA Modules:
  0.0 81.6 jit_solution(16799501770049551880)
XLA Ops:
  0.6 0.0 copy-start
  0.7 0.1 pad_add_fusion.parity
  0.7 0.8 %copy-done.1 = s32[1,4,4]{2,1,0:T(4,128)S(1)} copy-done((s32[1,4,4]{2,1,0:T(4,128)S(1)}, s32[1,4,4]{2,1,0:T(4,128)}, u32[]{:S(2)}) %copy-start.1) | copy-done | bytes 88
  1.6 0.7 copy-done.2
  2.3 3.7 %pack_ghosts.1 = (f32[4,128,256]{2,1,0:T(8,128)}, f32[4,128,256]{2,1,0:T(8,128)}, f32[4,128,256]{2,1,0:T(8,128)}, f32[4,128,256]{2,1,0:T(8,128)}) custom-call(s32[2]{0:T(128)S(1)} %pad_add_fusion.parity, s32[1,4,4]{2,1,0:T(4,128)S(1)} %copy-done.1, s32[1,4]{1,0:T(1,128)S(1)} %copy-done.2, f32[3072,256]{1,0:T(8,128)} %own.3), custom_call_target="tpu_custom_call" | custom-call | bytes 4194304 | tf_op jit(solution)/shard_map/pack_ghosts/pallas_call | solution.py:122
  6.0 1.5 %collective-permute-start = (f32[4,128,256]{2,1,0:T(8,128)}, f32[4,128,256]{2,1,0:T(8,128)}, u32[]{:S(2)}, u32[]{:S(2)}) collective-permute-start(f32[4,128,256]{2,1,0:T(8,128)} %get-tuple-element.21), channel_id=1, source_target_pairs={{0,8},{16,24},{32,40},{48,56},{64,72},{80,88},{96,104},{112,120},{... | collective-permute-start | bytes 1572872 | tf_op jit(solution)/shard_map/ppermute | solution.py:66
  7.5 1.4 %collective-permute-start.1 = (f32[4,128,256]{2,1,0:T(8,128)}, f32[4,128,256]{2,1,0:T(8,128)}, u32[]{:S(2)}, u32[]{:S(2)}) collective-permute-start(f32[4,128,256]{2,1,0:T(8,128)} %get-tuple-element.22), channel_id=1, source_target_pairs={{8,16},{24,32},{40,48},{56,64},{72,80},{88,96},{104,112},{16,8},{3... | collective-permute-start | bytes 1572872 | tf_op jit(solution)/shard_map/ppermute | solution.py:66
  9.0 1.2 %collective-permute-start.2 = (f32[4,128,256]{2,1,0:T(8,128)}, f32[4,128,256]{2,1,0:T(8,128)}, u32[]{:S(2)}, u32[]{:S(2)}) collective-permute-start(f32[4,128,256]{2,1,0:T(8,128)} %get-tuple-element.23), channel_id=1, source_target_pairs={{0,1},{2,3},{4,5},{6,7},{1,0},{3,2},{5,4},{7,6},{8,9},{10,11},{12,... | collective-permute-start | bytes 1572872 | tf_op jit(solution)/shard_map/ppermute | solution.py:66
  10.2 3.6 %collective-permute-start.3 = (f32[4,128,256]{2,1,0:T(8,128)}, f32[4,128,256]{2,1,0:T(8,128)}, u32[]{:S(2)}, u32[]{:S(2)}) collective-permute-start(f32[4,128,256]{2,1,0:T(8,128)} %get-tuple-element.24), channel_id=1, source_target_pairs={{1,2},{3,4},{5,6},{2,1},{4,3},{6,5},{9,10},{11,12},{13,14},{10,9},... | collective-permute-start | bytes 1572872 | tf_op jit(solution)/shard_map/ppermute | solution.py:66
  13.8 0.1 copy.9.cols
  14.6 9.8 %apply_own.1 = (f32[3072,256]{1,0:T(8,128)S(1)}, f32[288,128,128]{2,1,0:T(8,128)S(1)}, s32[368]{0:T(512)S(1)}, s32[368]{0:T(512)S(1)}, s32[200]{0:T(256)S(1)}, /*index=5*/s32[1]{0:T(128)}) custom-call(s32[2]{0:T(128)S(1)} %pad_add_fusion.parity, s32[24,12]{1,0:T(8,128)S(1)} %copy.9.cols, s32[1]{0:T(128)S(6)} %copy.11.live, f32[3072,256]{1,0:T(8,128)S(1)} %copy-done, ...), custom_call_target="tpu_custom_call" | custom-call | flops 4000000000 | bytes 26214400 | tf_op jit(solution)/shard_map/apply_own/pallas_call | solution.py:258
  24.4 7.6 %apply_ghosts.1 = (f32[3072,256]{1,0:T(8,128)S(1)}, bf16[3072,256]{1,0:T(8,128)(2,1)S(1)}, bf16[3072,256]{1,0:T(8,128)(2,1)S(1)}, f32[272,128]{1,0:T(8,128)S(1)}) custom-call(s32[368]{0:T(512)S(1)} %get-tuple-element.15.gt, s32[368]{0:T(512)S(1)} %get-tuple-element.16.gb, s32[200]{0:T(256)S(1)} %get-tuple-element.17.gr, ...), custom_call_target="tpu_custom_call", output_to_operand_aliasing={{0}: (4, {})} | custom-call | flops 3000000000 | bytes 26214400 | tf_op jit(solution)/shard_map/apply_ghosts/pallas_call | solution.py:327
  32.1 3.2 %collective-permute-start.4 = (f32[136,128]{1,0:T(8,128)S(1)}, f32[136,128]{1,0:T(8,128)S(1)}, u32[]{:S(2)}, u32[]{:S(2)}) collective-permute-start(f32[136,128]{1,0:T(8,128)S(1)} %constant_dynamic-slice_fusion), channel_id=1, source_target_pairs={{0,1},{1,0},{2,3},{3,2},{4,5},{5,4},{6,7},{7,6},{32,33},{33,32},{3... | collective-permute-start | bytes 208904 | tf_op jit(solution)/shard_map/ppermute | solution.py:73
  35.3 0.9 %collective-permute-done.4 = f32[136,128]{1,0:T(8,128)S(1)} collective-permute-done((f32[136,128]{1,0:T(8,128)S(1)}, f32[136,128]{1,0:T(8,128)S(1)}, u32[]{:S(2)}, u32[]{:S(2)}) %collective-permute-start.4) | collective-permute-done | bytes 69664 | tf_op jit(solution)/shard_map/ppermute | solution.py:73
  36.2 2.4 %collective-permute-start.5 = (f32[136,128]{1,0:T(8,128)S(1)}, f32[136,128]{1,0:T(8,128)S(1)}, u32[]{:S(2)}, u32[]{:S(2)}) collective-permute-start(f32[136,128]{1,0:T(8,128)S(1)} %dynamic-slice_add_fusion), channel_id=1, source_target_pairs={{0,8},{1,9},{2,10},{3,11},{4,12},{5,13},{6,14},{7,15},{32,40},{33,... | collective-permute-start | bytes 208904 | tf_op jit(solution)/shard_map/ppermute | solution.py:76
  38.6 4.9 %collective-permute-start.6 = (f32[136,128]{1,0:T(8,128)S(1)}, f32[136,128]{1,0:T(8,128)S(1)}, u32[]{:S(2)}, u32[]{:S(2)}) collective-permute-start(f32[136,128]{1,0:T(8,128)S(1)} %dynamic-slice_add_fusion), channel_id=1, source_target_pairs={{0,24},{1,25},{2,26},{3,27},{4,28},{5,29},{6,30},{7,31},{32,56},{3... | collective-permute-start | bytes 208904 | tf_op jit(solution)/shard_map/ppermute | solution.py:76
  43.4 1.1 %collective-permute-start.7 = (f32[136,128]{1,0:T(8,128)S(1)}, f32[136,128]{1,0:T(8,128)S(1)}, u32[]{:S(2)}, u32[]{:S(2)}) collective-permute-start(f32[136,128]{1,0:T(8,128)S(1)} %dynamic-slice_add_fusion), channel_id=1, source_target_pairs={{0,16},{1,17},{2,18},{3,19},{4,20},{5,21},{6,22},{7,23},{32,48},{3... | collective-permute-start | bytes 208904 | tf_op jit(solution)/shard_map/ppermute | solution.py:76
  44.5 1.3 %collective-permute-done.6 = f32[136,128]{1,0:T(8,128)S(1)} collective-permute-done((f32[136,128]{1,0:T(8,128)S(1)}, f32[136,128]{1,0:T(8,128)S(1)}, u32[]{:S(2)}, u32[]{:S(2)}) %collective-permute-start.6) | collective-permute-done | bytes 69664 | tf_op jit(solution)/shard_map/ppermute | solution.py:76
  45.8 2.3 %collective-permute-done.7 = f32[136,128]{1,0:T(8,128)S(1)} collective-permute-done((f32[136,128]{1,0:T(8,128)S(1)}, f32[136,128]{1,0:T(8,128)S(1)}, u32[]{:S(2)}, u32[]{:S(2)}) %collective-permute-start.7) | collective-permute-done | bytes 69664 | tf_op jit(solution)/shard_map/ppermute | solution.py:76
  48.1 1.4 %collective-permute-start.10 = (f32[136,128]{1,0:T(8,128)S(1)}, f32[136,128]{1,0:T(8,128)S(1)}, u32[]{:S(2)}, u32[]{:S(2)}) collective-permute-start(f32[136,128]{1,0:T(8,128)S(1)} %add_add_fusion.2), channel_id=1, source_target_pairs={{0,64},{1,65},{2,66},{3,67},{4,68},{5,69},{6,70},{7,71},{32,96},{3... | collective-permute-start | bytes 208904 | tf_op jit(solution)/shard_map/ppermute | solution.py:76
  49.5 2.2 %collective-permute-start.8 = (f32[136,128]{1,0:T(8,128)S(1)}, f32[136,128]{1,0:T(8,128)S(1)}, u32[]{:S(2)}, u32[]{:S(2)}) collective-permute-start(f32[136,128]{1,0:T(8,128)S(1)} %add_add_fusion.2), channel_id=1, source_target_pairs={{0,32},{1,33},{2,34},{3,35},{4,36},{5,37},{6,38},{7,39},{32,0},{33... | collective-permute-start | bytes 208904 | tf_op jit(solution)/shard_map/ppermute | solution.py:76
  51.7 1.1 %collective-permute-done.10 = f32[136,128]{1,0:T(8,128)S(1)} collective-permute-done((f32[136,128]{1,0:T(8,128)S(1)}, f32[136,128]{1,0:T(8,128)S(1)}, u32[]{:S(2)}, u32[]{:S(2)}) %collective-permute-start.10) | collective-permute-done | bytes 69664 | tf_op jit(solution)/shard_map/ppermute | solution.py:76
  52.9 1.8 %collective-permute-done.8 = f32[136,128]{1,0:T(8,128)S(1)} collective-permute-done((f32[136,128]{1,0:T(8,128)S(1)}, f32[136,128]{1,0:T(8,128)S(1)}, u32[]{:S(2)}, u32[]{:S(2)}) %collective-permute-start.8) | collective-permute-done | bytes 69664 | tf_op jit(solution)/shard_map/ppermute | solution.py:76
  54.7 1.4 %collective-permute-done.9 = f32[136,128]{1,0:T(8,128)S(1)} collective-permute-done((f32[136,128]{1,0:T(8,128)S(1)}, f32[136,128]{1,0:T(8,128)S(1)}, u32[]{:S(2)}, u32[]{:S(2)}) %collective-permute-start.9) | collective-permute-done | bytes 69664 | tf_op jit(solution)/shard_map/ppermute | solution.py:76
  56.1 0.1 collective-permute-start.11
  56.2 2.4 %collective-permute-start.12 = (f32[136,128]{1,0:T(8,128)S(1)}, f32[136,128]{1,0:T(8,128)S(1)}, u32[]{:S(2)}, u32[]{:S(2)}) collective-permute-start(f32[136,128]{1,0:T(8,128)S(1)} %add_add_fusion.1), channel_id=1, source_target_pairs={{0,6},{1,7},{2,4},{3,5},{4,2},{5,3},{6,0},{7,1},{32,38},{33,39},{3... | collective-permute-start | bytes 208904 | tf_op jit(solution)/shard_map/ppermute | solution.py:76
  58.6 1.1 %collective-permute-start.13 = (f32[136,128]{1,0:T(8,128)S(1)}, f32[136,128]{1,0:T(8,128)S(1)}, u32[]{:S(2)}, u32[]{:S(2)}) collective-permute-start(f32[136,128]{1,0:T(8,128)S(1)} %add_add_fusion.1), channel_id=1, source_target_pairs={{0,4},{1,5},{2,6},{3,7},{4,0},{5,1},{6,2},{7,3},{32,36},{33,37},{3... | collective-permute-start | bytes 208904 | tf_op jit(solution)/shard_map/ppermute | solution.py:76
  59.7 1.0 %collective-permute-done.12 = f32[136,128]{1,0:T(8,128)S(1)} collective-permute-done((f32[136,128]{1,0:T(8,128)S(1)}, f32[136,128]{1,0:T(8,128)S(1)}, u32[]{:S(2)}, u32[]{:S(2)}) %collective-permute-start.12) | collective-permute-done | bytes 69664 | tf_op jit(solution)/shard_map/ppermute | solution.py:76
  60.7 2.6 %collective-permute-done.13 = f32[136,128]{1,0:T(8,128)S(1)} collective-permute-done((f32[136,128]{1,0:T(8,128)S(1)}, f32[136,128]{1,0:T(8,128)S(1)}, u32[]{:S(2)}, u32[]{:S(2)}) %collective-permute-start.13) | collective-permute-done | bytes 69664 | tf_op jit(solution)/shard_map/ppermute | solution.py:76
  63.3 5.0 %collective-permute-start.14 = (f32[136,128]{1,0:T(8,128)S(1)}, f32[136,128]{1,0:T(8,128)S(1)}, u32[]{:S(2)}, u32[]{:S(2)}) collective-permute-start(f32[136,128]{1,0:T(8,128)S(1)} %add_add_fusion), channel_id=1, source_target_pairs={{0,1},{1,0},{2,3},{3,2},{4,5},{5,4},{6,7},{7,6},{32,33},{33,32},{3... | collective-permute-start | bytes 208904 | tf_op jit(solution)/shard_map/ppermute | solution.py:78
  68.3 0.9 %collective-permute-done.14 = f32[136,128]{1,0:T(8,128)S(1)} collective-permute-done((f32[136,128]{1,0:T(8,128)S(1)}, f32[136,128]{1,0:T(8,128)S(1)}, u32[]{:S(2)}, u32[]{:S(2)}) %collective-permute-start.14) | collective-permute-done | bytes 69664 | tf_op jit(solution)/shard_map/ppermute | solution.py:78
  69.2 12.2 %factor_and_basis.1 = (f32[3072,256]{1,0:T(8,128)}, f32[256,256]{1,0:T(8,128)}) custom-call(f32[136,128]{1,0:T(8,128)S(1)} %get-tuple-element.29.low, f32[136,128]{1,0:T(8,128)S(1)} %get-tuple-element.28.high, bf16[3072,256]{1,0:T(8,128)(2,1)S(1)} %get-tuple-element.26.ah, bf16[3072,256]{1,0:T(8,128)(2,1)S(1)} %get-tuple-element.27.al), custom_call_target="tpu_custom_call" | custom-call | flops 1000000000 | bytes 7340032 | tf_op jit(solution)/shard_map/factor_and_basis/pallas_call | solution.py:471
  (18 shorter events, 0.1 us)
Async XLA Ops:
  0.6 14.0 %copy-start = (f32[3072,256]{1,0:T(8,128)S(1)}, f32[3072,256]{1,0:T(8,128)}, u32[]{:S(2)}) copy-start(f32[3072,256]{1,0:T(8,128)} %own.3) | copy-start | bytes 9437188
  0.7 0.8 %copy-start.1 = (s32[1,4,4]{2,1,0:T(4,128)S(1)}, s32[1,4,4]{2,1,0:T(4,128)}, u32[]{:S(2)}) copy-start(s32[1,4,4]{2,1,0:T(4,128)} %lists.1) | copy-start | bytes 196
  1.6 0.7 copy-start.2
  2.2 11.6 %copy-start.3 = (s32[24,12]{0,1:T(8,128)S(1)}, s32[24,12]{0,1:T(8,128)}, u32[]{:S(2)}) copy-start(s32[24,12]{0,1:T(8,128)} %param.8) | copy-start | bytes 3460
  6.0 18.4 %collective-permute-start = (f32[4,128,256]{2,1,0:T(8,128)}, f32[4,128,256]{2,1,0:T(8,128)}, u32[]{:S(2)}, u32[]{:S(2)}) collective-permute-start(f32[4,128,256]{2,1,0:T(8,128)} %get-tuple-element.21), channel_id=1, source_target_pairs={{0,8},{16,24},{32,40},{48,56},{64,72},{80,88},{96,104},{112,120},{... | collective-permute-start | bytes 1572872 | tf_op jit(solution)/shard_map/ppermute | solution.py:66
  7.5 16.9 %collective-permute-start.1 = (f32[4,128,256]{2,1,0:T(8,128)}, f32[4,128,256]{2,1,0:T(8,128)}, u32[]{:S(2)}, u32[]{:S(2)}) collective-permute-start(f32[4,128,256]{2,1,0:T(8,128)} %get-tuple-element.22), channel_id=1, source_target_pairs={{8,16},{24,32},{40,48},{56,64},{72,80},{88,96},{104,112},{16,8},{3... | collective-permute-start | bytes 1572872 | tf_op jit(solution)/shard_map/ppermute | solution.py:66
  9.0 15.5 %collective-permute-start.2 = (f32[4,128,256]{2,1,0:T(8,128)}, f32[4,128,256]{2,1,0:T(8,128)}, u32[]{:S(2)}, u32[]{:S(2)}) collective-permute-start(f32[4,128,256]{2,1,0:T(8,128)} %get-tuple-element.23), channel_id=1, source_target_pairs={{0,1},{2,3},{4,5},{6,7},{1,0},{3,2},{5,4},{7,6},{8,9},{10,11},{12,... | collective-permute-start | bytes 1572872 | tf_op jit(solution)/shard_map/ppermute | solution.py:66
  10.2 14.2 %collective-permute-start.3 = (f32[4,128,256]{2,1,0:T(8,128)}, f32[4,128,256]{2,1,0:T(8,128)}, u32[]{:S(2)}, u32[]{:S(2)}) collective-permute-start(f32[4,128,256]{2,1,0:T(8,128)} %get-tuple-element.24), channel_id=1, source_target_pairs={{1,2},{3,4},{5,6},{2,1},{4,3},{6,5},{9,10},{11,12},{13,14},{10,9},... | collective-permute-start | bytes 1572872 | tf_op jit(solution)/shard_map/ppermute | solution.py:66
  32.1 4.1 %collective-permute-start.4 = (f32[136,128]{1,0:T(8,128)S(1)}, f32[136,128]{1,0:T(8,128)S(1)}, u32[]{:S(2)}, u32[]{:S(2)}) collective-permute-start(f32[136,128]{1,0:T(8,128)S(1)} %constant_dynamic-slice_fusion), channel_id=1, source_target_pairs={{0,1},{1,0},{2,3},{3,2},{4,5},{5,4},{6,7},{7,6},{32,33},{33,32},{3... | collective-permute-start | bytes 208904 | tf_op jit(solution)/shard_map/ppermute | solution.py:73
  36.2 8.3 %collective-permute-start.5 = (f32[136,128]{1,0:T(8,128)S(1)}, f32[136,128]{1,0:T(8,128)S(1)}, u32[]{:S(2)}, u32[]{:S(2)}) collective-permute-start(f32[136,128]{1,0:T(8,128)S(1)} %dynamic-slice_add_fusion), channel_id=1, source_target_pairs={{0,8},{1,9},{2,10},{3,11},{4,12},{5,13},{6,14},{7,15},{32,40},{33,... | collective-permute-start | bytes 208904 | tf_op jit(solution)/shard_map/ppermute | solution.py:76
  38.6 7.3 %collective-permute-start.6 = (f32[136,128]{1,0:T(8,128)S(1)}, f32[136,128]{1,0:T(8,128)S(1)}, u32[]{:S(2)}, u32[]{:S(2)}) collective-permute-start(f32[136,128]{1,0:T(8,128)S(1)} %dynamic-slice_add_fusion), channel_id=1, source_target_pairs={{0,24},{1,25},{2,26},{3,27},{4,28},{5,29},{6,30},{7,31},{32,56},{3... | collective-permute-start | bytes 208904 | tf_op jit(solution)/shard_map/ppermute | solution.py:76
  43.4 4.7 %collective-permute-start.7 = (f32[136,128]{1,0:T(8,128)S(1)}, f32[136,128]{1,0:T(8,128)S(1)}, u32[]{:S(2)}, u32[]{:S(2)}) collective-permute-start(f32[136,128]{1,0:T(8,128)S(1)} %dynamic-slice_add_fusion), channel_id=1, source_target_pairs={{0,16},{1,17},{2,18},{3,19},{4,20},{5,21},{6,22},{7,23},{32,48},{3... | collective-permute-start | bytes 208904 | tf_op jit(solution)/shard_map/ppermute | solution.py:76
  48.1 4.7 %collective-permute-start.10 = (f32[136,128]{1,0:T(8,128)S(1)}, f32[136,128]{1,0:T(8,128)S(1)}, u32[]{:S(2)}, u32[]{:S(2)}) collective-permute-start(f32[136,128]{1,0:T(8,128)S(1)} %add_add_fusion.2), channel_id=1, source_target_pairs={{0,64},{1,65},{2,66},{3,67},{4,68},{5,69},{6,70},{7,71},{32,96},{3... | collective-permute-start | bytes 208904 | tf_op jit(solution)/shard_map/ppermute | solution.py:76
  49.5 5.2 %collective-permute-start.8 = (f32[136,128]{1,0:T(8,128)S(1)}, f32[136,128]{1,0:T(8,128)S(1)}, u32[]{:S(2)}, u32[]{:S(2)}) collective-permute-start(f32[136,128]{1,0:T(8,128)S(1)} %add_add_fusion.2), channel_id=1, source_target_pairs={{0,32},{1,33},{2,34},{3,35},{4,36},{5,37},{6,38},{7,39},{32,0},{33... | collective-permute-start | bytes 208904 | tf_op jit(solution)/shard_map/ppermute | solution.py:76
  51.7 4.4 %collective-permute-start.9 = (f32[136,128]{1,0:T(8,128)S(1)}, f32[136,128]{1,0:T(8,128)S(1)}, u32[]{:S(2)}, u32[]{:S(2)}) collective-permute-start(f32[136,128]{1,0:T(8,128)S(1)} %add_add_fusion.2), channel_id=1, source_target_pairs={{0,96},{1,97},{2,98},{3,99},{4,100},{5,101},{6,102},{7,103},{32,64... | collective-permute-start | bytes 208904 | tf_op jit(solution)/shard_map/ppermute | solution.py:76
  56.1 3.6 %collective-permute-start.11 = (f32[136,128]{1,0:T(8,128)S(1)}, f32[136,128]{1,0:T(8,128)S(1)}, u32[]{:S(2)}, u32[]{:S(2)}) collective-permute-start(f32[136,128]{1,0:T(8,128)S(1)} %add_add_fusion.1), channel_id=1, source_target_pairs={{0,2},{1,3},{2,0},{3,1},{4,6},{5,7},{6,4},{7,5},{32,34},{33,35},{3... | collective-permute-start | bytes 208904 | tf_op jit(solution)/shard_map/ppermute | solution.py:76
  56.2 4.5 %collective-permute-start.12 = (f32[136,128]{1,0:T(8,128)S(1)}, f32[136,128]{1,0:T(8,128)S(1)}, u32[]{:S(2)}, u32[]{:S(2)}) collective-permute-start(f32[136,128]{1,0:T(8,128)S(1)} %add_add_fusion.1), channel_id=1, source_target_pairs={{0,6},{1,7},{2,4},{3,5},{4,2},{5,3},{6,0},{7,1},{32,38},{33,39},{3... | collective-permute-start | bytes 208904 | tf_op jit(solution)/shard_map/ppermute | solution.py:76
  58.6 4.7 %collective-permute-start.13 = (f32[136,128]{1,0:T(8,128)S(1)}, f32[136,128]{1,0:T(8,128)S(1)}, u32[]{:S(2)}, u32[]{:S(2)}) collective-permute-start(f32[136,128]{1,0:T(8,128)S(1)} %add_add_fusion.1), channel_id=1, source_target_pairs={{0,4},{1,5},{2,6},{3,7},{4,0},{5,1},{6,2},{7,3},{32,36},{33,37},{3... | collective-permute-start | bytes 208904 | tf_op jit(solution)/shard_map/ppermute | solution.py:76
  63.3 5.9 %collective-permute-start.14 = (f32[136,128]{1,0:T(8,128)S(1)}, f32[136,128]{1,0:T(8,128)S(1)}, u32[]{:S(2)}, u32[]{:S(2)}) collective-permute-start(f32[136,128]{1,0:T(8,128)S(1)} %add_add_fusion), channel_id=1, source_target_pairs={{0,1},{1,0},{2,3},{3,2},{4,5},{5,4},{6,7},{7,6},{32,33},{33,32},{3... | collective-permute-start | bytes 208904 | tf_op jit(solution)/shard_map/ppermute | solution.py:78

commit v4 on v3

--- a/solution.py
+++ b/solution.py
@@ -20,10 +20,17 @@
 F32 = jnp.float32
 BF16 = jnp.bfloat16
 MB = 1 << 20
-CHUNK = 8
-AHEAD = 6
+OWN_CHUNK = 8
+GHOST_CHUNK = 12
+LIST_AT = 8
+LIST_SIZE = LIST_AT + NBD * TPR + 2 * NBD + 32
+TILE_SHIFT = 6
+ROW_SHIFT = 16
+TILE_UNIT = 1 << TILE_SHIFT
+ROW_UNIT = 1 << ROW_SHIFT
+AHEAD = 9
 NEAR = 2
-STORE = 512
+STORE = 1024
 
 
 def device_at(x, y, z, core):
@@ -85,10 +92,55 @@
     return pltpu.with_memory_space_constraint(x, pltpu.VMEM)
 
 
-def pack_kernel(parity, lists, counts, own, *refs):
-    outs, held, in_sems, out_sems = refs[:4], refs[4], refs[5], refs[6]
+def split(x):
+    high = x.astype(BF16)
+    return high, (x - high.astype(F32)).astype(BF16)
+
+
+def dot(a, b):
+    return lax.dot_general(a, b, (((1,), (0,)), ((), ())), preferred_element_type=F32)
+
+
+def pair_lists(parity, cols, live, own_list, ghost_list):
+    turn_px, turn_py = GMAX * (1 - parity[0]), GMAX * (1 - parity[1])
+
+    def row_pairs(row, counts):
+        own_n, ghost_n = counts
+        base = row * (ROW_UNIT + TPR * TILE_UNIT)
+        for t in range(TPR):
+            c = cols[t, row]
+            ghost = jnp.where(c >= NBD, 1, 0)
+            g = c - NBD
+            entry = base + t * TILE_UNIT
+            own_list[LIST_AT + own_n] = entry + c
+            ghost_list[LIST_AT + ghost_n] = entry + (g ^ jnp.where(g < 2 * GMAX, turn_px, turn_py))
+            own_n, ghost_n = own_n + 1 - ghost, ghost_n + ghost
+        own_list[LIST_AT + own_n] = NBD
+        ghost_list[LIST_AT + ghost_n] = 4 * GMAX
+        return own_n + (own_n & 1), ghost_n + (ghost_n & 1)
+
+    zero = jnp.int32(0)
+    ends = lax.fori_loop(0, live[0], row_pairs, (zero, zero))
+    for out, n, blank, chunk in (
+        (own_list, ends[0], NBD, OWN_CHUNK),
+        (ghost_list, ends[1], 4 * GMAX, GHOST_CHUNK),
+    ):
+        for k in range(2 * chunk):
+            out[LIST_AT + n + k] = blank
+        out[0] = n >> 1
+
+
+def prepare_kernel(parity, live, lists_in, counts_in, cols_in, own, *refs):
+    outs, (own_list, ghost_list, lists, counts, cols, held) = refs[:4], refs[4:10]
+    small_sems, in_sems, out_sems = refs[10:]
+    small = [
+        pltpu.make_async_copy(a, b, small_sems.at[n])
+        for n, (a, b) in enumerate(((lists_in, lists), (counts_in, counts), (cols_in, cols)))
+    ]
+    for c in small:
+        c.start()
     odd_px, odd_py = parity[0], parity[1]
-    directions = (odd_px, 1 - odd_px, 2 + odd_py, 3 - odd_py)
+    directions = (1 - odd_px, odd_px, 3 - odd_py, 2 + odd_py)
 
     def fetch(n, s):
         block = lists[0, directions[n], s]
@@ -98,9 +150,13 @@
     def store(n, s):
         return pltpu.make_async_copy(held.at[n, s], outs[n].at[s], out_sems.at[n, s])
 
+    small[0].wait()
     for n in range(4):
         for s in range(GMAX):
             fetch(n, s).start()
+    for c in small[1:]:
+        c.wait()
+    pair_lists(parity, cols, live, own_list, ghost_list)
     for n in range(4):
         for s in range(GMAX):
             fetch(n, s).wait()
@@ -115,108 +171,60 @@
             store(n, s).wait()
 
 
-def pack_ghosts(parity, lists, counts, own):
+def prepare(parity, lists, counts, cols, live, own):
     smem = pl.BlockSpec(memory_space=pltpu.SMEM)
     hbm = pl.BlockSpec(memory_space=pltpu.HBM)
     anywhere = pl.BlockSpec(memory_space=pl.ANY)
-    return pl.pallas_call(
-        pack_kernel,
-        out_shape=[jax.ShapeDtypeStruct((GMAX, BS, K), F32)] * 4,
-        in_specs=[smem, smem, smem, hbm],
-        out_specs=[anywhere] * 4,
+    arrays = (lists, counts, cols, own)
+    outs = pl.pallas_call(
+        prepare_kernel,
+        out_shape=[jax.ShapeDtypeStruct((GMAX, BS, K), F32)] * 4
+        + [jax.ShapeDtypeStruct((LIST_SIZE,), jnp.int32)] * 2,
+        in_specs=[smem] * 2 + [hbm] * 4,
+        out_specs=[anywhere] * 4 + [smem] * 2,
         scratch_shapes=[
+            *[pltpu.SMEM(a.shape, jnp.int32) for a in arrays[:3]],
             pltpu.VMEM((4, GMAX, BS, K), F32),
+            pltpu.SemaphoreType.DMA((3,)),
             pltpu.SemaphoreType.DMA((4, GMAX)),
             pltpu.SemaphoreType.DMA((4, GMAX)),
         ],
         compiler_params=pltpu.CompilerParams(vmem_limit_bytes=4 * MB),
         cost_estimate=pl.CostEstimate(flops=0, bytes_accessed=4 * MB, transcendentals=0),
-        name="pack_ghosts",
-    )(parity, lists, counts, pltpu.with_memory_space_constraint(own, pltpu.HBM))
-
-
-def split(x):
-    high = x.astype(BF16)
-    return high, (x - high.astype(F32)).astype(BF16)
-
-
-def dot(a, b):
-    return lax.dot_general(a, b, (((1,), (0,)), ((), ())), preferred_element_type=F32)
-
-
-def pair_lists(parity, cols, live, own_list, ghost_list):
-    turn_px, turn_py = GMAX * (1 - parity[0]), GMAX * (1 - parity[1])
-
-    def row_pairs(row, counts):
-        starts = counts
-        for t in range(TPR):
-            c = cols[row, t]
-            ghost = jnp.where(c >= NBD, 1, 0)
-            g = c - NBD
-            for (tile, block, _, _), n, at in (
-                (own_list, counts[0], c),
-                (ghost_list, counts[1], g ^ jnp.where(g < 2 * GMAX, turn_px, turn_py)),
-            ):
-                tile[n] = row * TPR + t
-                block[n] = at
-            counts = (counts[0] + 1 - ghost, counts[1] + ghost)
-        ends = []
-        for (tile, block, rows, _), n, start, zero in (
-            (own_list, counts[0], starts[0], NBD),
-            (ghost_list, counts[1], starts[1], 4 * GMAX),
-        ):
-            tile[n] = 0
-            block[n] = zero
-            end = n + (n & 1)
-            for k in range(TPR // 2):
-                rows[start // 2 + k] = row
-            ends.append(end)
-        return tuple(ends)
-
-    zero = jnp.int32(0)
-    own_n, ghost_n = lax.fori_loop(0, live[0], row_pairs, (zero, zero))
-    for (tile, block, rows, count), n, blank in (
-        (own_list, own_n, NBD),
-        (ghost_list, ghost_n, 4 * GMAX),
-    ):
-        for k in range(2 * CHUNK):
-            tile[n + k] = 0
-            block[n + k] = blank
-        for k in range(CHUNK):
-            rows[n // 2 + k] = 0
-        count[0] = n // 2
-
-
-def add_chunk(start, lists, tiles, xh, xl, acc):
-    tile, block, rows, _ = lists
-    for k in range(CHUNK):
-        p = start + k
-        t0, t1, c0, c1 = tile[2 * p], tile[2 * p + 1], block[2 * p], block[2 * p + 1]
+        name="prepare",
+    )(parity, live, *[pltpu.with_memory_space_constraint(a, pltpu.HBM) for a in arrays])
+    return outs[:4], outs[4:]
+
+
+def add_chunk(start, size, pairs, tiles, xh, xl, acc):
+    for k in range(size):
+        first = pairs[LIST_AT + 2 * (start + k)]
+        second = pairs[LIST_AT + 2 * (start + k) + 1]
+        t0, t1 = (first >> TILE_SHIFT) & 1023, (second >> TILE_SHIFT) & 1023
+        c0, c1 = first & 63, second & 63
         th, tl = split(jnp.concatenate([tiles[t0], tiles[t1]], axis=1))
         r0 = pl.ds(pl.multiple_of(c0 * BS, BS), BS)
         r1 = pl.ds(pl.multiple_of(c1 * BS, BS), BS)
         bh = jnp.concatenate([xh[r0], xh[r1]], axis=0)
         bl = jnp.concatenate([xl[r0], xl[r1]], axis=0)
-        at = pl.ds(pl.multiple_of(rows[p] * BS, BS), BS)
+        at = pl.ds(pl.multiple_of((first >> ROW_SHIFT) * BS, BS), BS)
         acc[at] += dot(th, bh) + dot(tl, bh) + dot(th, bl)
 
 
-def own_kernel(parity, cols, live, own, tiles, part, held, gt, gb, gr, gn, xh, xl, ot, ob, orow, on, sems):
+def own_kernel(pairs, own, tiles, part, held, xh, xl, sems):
     def fetch(row):
         rows = pl.ds(row * TPR, TPR)
         return pltpu.make_async_copy(tiles.at[rows], held.at[rows], sems.at[row])
 
     for row in range(AHEAD):
         fetch(row).start()
-    own_list, ghost_list = (ot, ob, orow, on), (gt, gb, gr, gn)
-    pair_lists(parity, cols, live, own_list, ghost_list)
-    part[...] = jnp.zeros_like(part)
     xh[NBD * BS :] = jnp.zeros((BS, K), BF16)
     xl[NBD * BS :] = jnp.zeros((BS, K), BF16)
 
     def convert(b, _):
         rows = pl.ds(pl.multiple_of(b * BS, BS), BS)
         xh[rows], xl[rows] = split(own[rows])
+        part[rows] = jnp.zeros((BS, K), F32)
         return 0
 
     lax.fori_loop(0, NBD, convert, 0)
@@ -230,50 +238,35 @@
 
         return 0
 
-    pairs = on[0]
+    count = pairs[0]
 
     def chunk(i, ready):
-        last = jnp.minimum(i * CHUNK + CHUNK, pairs) - 1
-        need = jnp.maximum(orow[last] + 1, ready)
+        last = jnp.minimum(i * OWN_CHUNK + OWN_CHUNK, count) - 1
+        need = jnp.maximum((pairs[LIST_AT + 2 * last] >> ROW_SHIFT) + 1, ready)
         lax.fori_loop(ready, need, arrive, 0)
-        add_chunk(i * CHUNK, own_list, held, xh, xl, part)
+        add_chunk(i * OWN_CHUNK, OWN_CHUNK, pairs, held, xh, xl, part)
         return need
 
-    ready = lax.fori_loop(0, (pairs + CHUNK - 1) // CHUNK, chunk, jnp.int32(0))
+    ready = lax.fori_loop(0, (count + OWN_CHUNK - 1) // OWN_CHUNK, chunk, jnp.int32(0))
     lax.fori_loop(ready, NBD, arrive, 0)
 
 
-def list_shapes(kind):
-    return [
-        kind((NBD * (TPR + 2) + 4 * CHUNK,), jnp.int32),
-        kind((NBD * (TPR + 2) + 4 * CHUNK,), jnp.int32),
-        kind((NBD * (TPR + 2) // 2 + 4 * CHUNK,), jnp.int32),
-        kind((1,), jnp.int32),
-    ]
-
-
-def apply_own(parity, cols, live, own, tiles):
-    smem = pl.BlockSpec(memory_space=pltpu.SMEM)
+def apply_own(pairs, own, tiles):
     vmem = pl.BlockSpec(memory_space=pltpu.VMEM)
     return pl.pallas_call(
         own_kernel,
-        out_shape=[
-            pltpu.VMEM((NBD * BS, K), F32),
-            pltpu.VMEM((NBD * TPR, BS, BS), F32),
-            *list_shapes(jax.ShapeDtypeStruct),
-        ],
-        in_specs=[smem, smem, smem, vmem, pl.BlockSpec(memory_space=pltpu.HBM)],
-        out_specs=[vmem] * 2 + [smem] * 4,
+        out_shape=[pltpu.VMEM((NBD * BS, K), F32), pltpu.VMEM((NBD * TPR, BS, BS), F32)],
+        in_specs=[pl.BlockSpec(memory_space=pltpu.SMEM), vmem, pl.BlockSpec(memory_space=pltpu.HBM)],
+        out_specs=[vmem] * 2,
         scratch_shapes=[
             pltpu.VMEM(((NBD + 1) * BS, K), BF16),
             pltpu.VMEM(((NBD + 1) * BS, K), BF16),
-            *list_shapes(pltpu.SMEM),
             pltpu.SemaphoreType.DMA((NBD,)),
         ],
         compiler_params=pltpu.CompilerParams(vmem_limit_bytes=8 * MB),
         cost_estimate=pl.CostEstimate(flops=4 * 10**9, bytes_accessed=25 * MB, transcendentals=0),
         name="apply_own",
-    )(parity, cols, live, on_vmem(own), pltpu.with_memory_space_constraint(tiles, pltpu.HBM))
+    )(pairs, on_vmem(own), pltpu.with_memory_space_constraint(tiles, pltpu.HBM))
 
 
 def gram_pack(high, low):
@@ -289,7 +282,7 @@
     return jnp.concatenate([jnp.where(i <= j, first, second), gram[:BS, BS:], tail], axis=0)
 
 
-def ghost_kernel(gt, gb, gr, gn, part, held, g0, g1, g2, g3, total, ah, al, gram, xh, xl, xv, sems):
+def ghost_kernel(pairs, _, held, g0, g1, g2, g3, total, high, low, gram, xh, xl, xv, ah, al, sems, out_sems):
     arrivals = [pltpu.make_async_copy(g, xv.at[e], sems.at[e]) for e, g in enumerate((g0, g1, g2, g3))]
     for c in arrivals:
         c.start()
@@ -306,10 +299,10 @@
         lax.fori_loop(0, GMAX, convert, 0)
 
     def chunk(i, _):
-        add_chunk(i * CHUNK, (gt, gb, gr, gn), held, xh, xl, total)
+        add_chunk(i * GHOST_CHUNK, GHOST_CHUNK, pairs, held, xh, xl, total)
         return 0
 
-    lax.fori_loop(0, (gn[0] + CHUNK - 1) // CHUNK, chunk, 0)
+    lax.fori_loop(0, (pairs[0] + GHOST_CHUNK - 1) // GHOST_CHUNK, chunk, 0)
 
     def finish(row, _):
         rows = pl.ds(pl.multiple_of(row * BS, BS), BS)
@@ -317,34 +310,43 @@
         return 0
 
     lax.fori_loop(0, NBD, finish, 0)
+    stores = [pltpu.make_async_copy(a, b, out_sems.at[n]) for n, (a, b) in enumerate(((ah, high), (al, low)))]
+    for c in stores:
+        c.start()
     gram[...] = gram_pack(ah[...], al[...])
-
-
-def apply_ghosts(part, held, lists, ghosts):
+    for c in stores:
+        c.wait()
+
+
+def apply_ghosts(pairs, part, held, ghosts):
     smem = pl.BlockSpec(memory_space=pltpu.SMEM)
     vmem = pl.BlockSpec(memory_space=pltpu.VMEM)
     anywhere = pl.BlockSpec(memory_space=pl.ANY)
+    hbm = pl.BlockSpec(memory_space=pltpu.HBM)
     _, ah, al, gram = pl.pallas_call(
         ghost_kernel,
         out_shape=[
             pltpu.VMEM((NBD * BS, K), F32),
-            pltpu.VMEM((NBD * BS, K), BF16),
-            pltpu.VMEM((NBD * BS, K), BF16),
+            pltpu.HBM((NBD * BS, K), BF16),
+            pltpu.HBM((NBD * BS, K), BF16),
             jax.ShapeDtypeStruct((2 * HALF, BS), F32),
         ],
-        in_specs=[smem] * 4 + [vmem] * 2 + [anywhere] * 4,
-        out_specs=[vmem] * 4,
+        in_specs=[smem] + [vmem] * 2 + [anywhere] * 4,
+        out_specs=[vmem, hbm, hbm, vmem],
         scratch_shapes=[
             pltpu.VMEM(((4 * GMAX + 1) * BS, K), BF16),
             pltpu.VMEM(((4 * GMAX + 1) * BS, K), BF16),
             pltpu.VMEM((4, GMAX, BS, K), F32),
+            pltpu.VMEM((NBD * BS, K), BF16),
+            pltpu.VMEM((NBD * BS, K), BF16),
             pltpu.SemaphoreType.DMA((4,)),
+            pltpu.SemaphoreType.DMA((2,)),
         ],
-        input_output_aliases={4: 0},
-        compiler_params=pltpu.CompilerParams(vmem_limit_bytes=16 * MB),
+        input_output_aliases={1: 0},
+        compiler_params=pltpu.CompilerParams(vmem_limit_bytes=12 * MB),
         cost_estimate=pl.CostEstimate(flops=3 * 10**9, bytes_accessed=25 * MB, transcendentals=0),
         name="apply_ghosts",
-    )(*lists, on_vmem(part), on_vmem(held), *ghosts)
+    )(pairs, on_vmem(part), on_vmem(held), *ghosts)
     return ah, al, gram
 
 
@@ -445,61 +447,84 @@
     return upper, lower
 
 
-def basis_kernel(low, high, ah, al, basis, upper, wh, wl, staged, sems):
+def basis_kernel(low, high, rows_high, rows_low, basis, upper, wh, wl, ah, al, staged, in_sems, sems):
+    pieces = NBD * BS // STORE
+
+    def piece(n):
+        return pl.ds(pl.multiple_of(n * STORE, STORE), STORE)
+
+    def load(n):
+        rows = piece(n)
+        return [
+            pltpu.make_async_copy(a.at[rows], b.at[rows], in_sems.at[k, n])
+            for k, (a, b) in enumerate(((rows_high, ah), (rows_low, al)))
+        ]
+
+    def store(n):
+        return pltpu.make_async_copy(staged.at[piece(n)], basis.at[piece(n)], sems.at[n])
+
+    def begin(n, _):
+        for c in load(n):
+            c.start()
+        return 0
+
+    lax.fori_loop(0, pieces, begin, 0)
     r, x = factor(low[...], high[...])
     upper[...] = r
     wh[...], wl[...] = split(x.T)
 
-    def store(n):
-        rows = pl.ds(pl.multiple_of(n * STORE, STORE), STORE)
-        return pltpu.make_async_copy(staged.at[rows], basis.at[rows], sems.at[n])
-
-    def chunk(n, _):
-        rows = pl.ds(pl.multiple_of(n * STORE, STORE), STORE)
+    def multiply(n, _):
+        for c in load(n):
+            c.wait()
+        rows = piece(n)
         h, l = ah[rows], al[rows]
         staged[rows] = dot(h, wh[...]) + dot(l, wh[...]) + dot(h, wl[...])
         store(n).start()
         return 0
 
-    lax.fori_loop(0, NBD * BS // STORE, chunk, 0)
-    for n in range(NBD * BS // STORE):
+    lax.fori_loop(0, pieces, multiply, 0)
+    for n in range(pieces):
         store(n).wait()
 
 
 def orthonormalize(low, high, ah, al):
     vmem = pl.BlockSpec(memory_space=pltpu.VMEM)
+    hbm = pl.BlockSpec(memory_space=pltpu.HBM)
     return pl.pallas_call(
         basis_kernel,
         out_shape=[
             jax.ShapeDtypeStruct((NBD * BS, K), F32),
             jax.ShapeDtypeStruct((K, K), F32),
         ],
-        in_specs=[vmem] * 4,
-        out_specs=[pl.BlockSpec(memory_space=pltpu.HBM), vmem],
+        in_specs=[vmem] * 2 + [hbm] * 2,
+        out_specs=[hbm, vmem],
         scratch_shapes=[
             pltpu.VMEM((K, K), BF16),
             pltpu.VMEM((K, K), BF16),
+            pltpu.VMEM((NBD * BS, K), BF16),
+            pltpu.VMEM((NBD * BS, K), BF16),
             pltpu.VMEM((NBD * BS, K), F32),
+            pltpu.SemaphoreType.DMA((2, NBD * BS // STORE)),
             pltpu.SemaphoreType.DMA((NBD * BS // STORE,)),
         ],
-        compiler_params=pltpu.CompilerParams(vmem_limit_bytes=16 * MB),
+        compiler_params=pltpu.CompilerParams(vmem_limit_bytes=12 * MB),
         cost_estimate=pl.CostEstimate(flops=10**9, bytes_accessed=7 * MB, transcendentals=0),
         name="factor_and_basis",
-    )(low, high, on_vmem(ah), on_vmem(al))
+    )(low, high, *[pltpu.with_memory_space_constraint(a, pltpu.HBM) for a in (ah, al)])
 
 
 def body(block_vectors, stiff_tiles, col_index, send_lists, send_counts, part_blocks):
     parity = jnp.stack([lax.axis_index("px") % 2, lax.axis_index("py") % 2]).astype(jnp.int32)
     tiles = stiff_tiles.reshape(NBD * TPR, BS, BS)
-    packed = pack_ghosts(parity, send_lists, send_counts, block_vectors)
-    ghosts = [
-        swapped(packed[0], "px", False),
-        swapped(packed[1], "px", True),
-        swapped(packed[2], "py", False),
-        swapped(packed[3], "py", True),
-    ]
-    part, held, *lists = apply_own(parity, col_index, part_blocks, block_vectors, tiles)
-    ah, al, gram = apply_ghosts(part, held, lists, ghosts)
+    (px_odd, px_even, py_odd, py_even), (own_pairs, ghost_pairs) = prepare(
+        parity, send_lists, send_counts, col_index.T, part_blocks, block_vectors
+    )
+    px_odd = swapped(px_odd, "px", True)
+    py_even = swapped(py_even, "py", False)
+    px_even = swapped(px_even, "px", False)
+    py_odd = swapped(py_odd, "py", True)
+    part, held = apply_own(own_pairs, block_vectors, tiles)
+    ah, al, gram = apply_ghosts(ghost_pairs, part, held, [px_even, px_odd, py_even, py_odd])
     low, high = sum_everywhere(gram)
     return tuple(orthonormalize(low, high, ah, al))
 

time: 81.4 us -> 79.1 us (0.972)
  local copies, waits for them, and re-layouts: 1.62 us -> 0.02 us
  starting transfers between devices: 31.5 us -> 30.5 us
    ppermute x1, starting transfers between devices: 3.17 us -> 1.27 us  [sum_everywhere(): total = mine + lax.ppermute(other, AXES, CORE_ROUTE)]
    pallas_call x1, Pallas kernels: 9.79 us -> 8.14 us  [apply_own(): pl.pallas_call(own_kernel, out_shape=[pltpu.VMEM((NBD * BS, K), F32), plt...]
    unnamed x9 -> x2, local copies, waits for them, and re-layouts: 1.61 us -> 0.01 us
    pallas_call x1, Pallas kernels: 3.74 us -> 5.03 us  [prepare(): pl.pallas_call(prepare_kernel, out_shape=[jax.ShapeDtypeStruct((GMAX, BS,...]
  transfers between devices with their start and end apart: 15 -> 15, of which waited for: 9 -> 9; matrix products, arithmetic and copies ran while one was open for 0% -> 0% of each run, Pallas kernels for 12% -> 10%
where the time goes in v4:
time: 79.1 us; the launch traced here: 78.9 us
  Pallas kernels  33 us (42%)
  starting transfers between devices  30.5 us (39%)
  waiting for transfers between devices  13.5 us (17%)
  between operations  1.72 us (2%)
    ppermute x9, starting transfers between devices, sum_everywhere(): near, wrap, far = [lax.ppermute(total, AXES, r) for r in routes]  16.3 us
    pallas_call x1, Pallas kernels, orthonormalize(): pl.pallas_call(basis_kernel, out_shape=[jax.ShapeDtypeStruct((NBD * BS, K...  12 us
    ppermute x9, waiting for transfers between devices, sum_everywhere(): near, wrap, far = [lax.ppermute(total, AXES, r) for r in routes]  11.6 us
    ppermute x4, starting transfers between devices, swapped(): return lax.ppermute(block, axis, pairs + [(j, i) for i, j in pairs])  8.5 us
    pallas_call x1, Pallas kernels, apply_own(): pl.pallas_call(own_kernel, out_shape=[pltpu.VMEM((NBD * BS, K), F32), plt...  8.14 us
    pallas_call x1, Pallas kernels, apply_ghosts(): pl.pallas_call(ghost_kernel, out_shape=[pltpu.VMEM((NBD * BS, K), F32), p...  7.87 us
    pallas_call x1, Pallas kernels, prepare(): pl.pallas_call(prepare_kernel, out_shape=[jax.ShapeDtypeStruct((GMAX, BS,...  5.03 us
    ppermute x1, starting transfers between devices, sum_everywhere(): theirs = lax.ppermute(total, AXES, CORE_ROUTE)  4.44 us
  transfers between devices with their start and end apart: 15, of which 9 were waited for; matrix products, arithmetic and copies ran while one was open for 0% of the time, Pallas kernels for 10%

profile of v4, /device:TPU:1, one launch (start us, length us, event | category | flops | bytes accessed | tf_op | source)
XLA Modules:
  0.0 78.9 jit_solution(7735000150926257691)
XLA Ops:
  0.6 0.0 copy-start
  1.5 0.1 pad_add_fusion.parity
  1.5 5.0 %prepare.1 = (f32[4,128,256]{2,1,0:T(8,128)}, f32[4,128,256]{2,1,0:T(8,128)}, f32[4,128,256]{2,1,0:T(8,128)}, f32[4,128,256]{2,1,0:T(8,128)}, s32[376]{0:T(512)S(1)}, /*index=5*/s32[376]{0:T(512)S(1)}) custom-call(s32[2]{0:T(128)S(1)} %pad_add_fusion.parity, s32[1]{0:T(128)S(6)} %copy.10.live, s32[1,4,4]{2,1,0:T(4,128)} %lists_in.1, s32[1,4]{1,0:T(1,128)} %counts_in.1, ...), custom_call_target="tpu_custom_call" | custom-call | bytes 4194304 | tf_op jit(solution)/shard_map/prepare/pallas_call | solution.py:179
  6.6 1.8 %collective-permute-start = (f32[4,128,256]{2,1,0:T(8,128)}, f32[4,128,256]{2,1,0:T(8,128)}, u32[]{:S(2)}, u32[]{:S(2)}) collective-permute-start(f32[4,128,256]{2,1,0:T(8,128)} %get-tuple-element.17), channel_id=1, source_target_pairs={{0,8},{16,24},{32,40},{48,56},{64,72},{80,88},{96,104},{112,120},{... | collective-permute-start | bytes 1572872 | tf_op jit(solution)/shard_map/ppermute | solution.py:73
  8.4 1.5 %collective-permute-start.1 = (f32[4,128,256]{2,1,0:T(8,128)}, f32[4,128,256]{2,1,0:T(8,128)}, u32[]{:S(2)}, u32[]{:S(2)}) collective-permute-start(f32[4,128,256]{2,1,0:T(8,128)} %get-tuple-element.18), channel_id=1, source_target_pairs={{8,16},{24,32},{40,48},{56,64},{72,80},{88,96},{104,112},{16,8},{3... | collective-permute-start | bytes 1572872 | tf_op jit(solution)/shard_map/ppermute | solution.py:73
  9.9 1.1 %collective-permute-start.2 = (f32[4,128,256]{2,1,0:T(8,128)}, f32[4,128,256]{2,1,0:T(8,128)}, u32[]{:S(2)}, u32[]{:S(2)}) collective-permute-start(f32[4,128,256]{2,1,0:T(8,128)} %get-tuple-element.19), channel_id=1, source_target_pairs={{0,1},{2,3},{4,5},{6,7},{1,0},{3,2},{5,4},{7,6},{8,9},{10,11},{12,... | collective-permute-start | bytes 1572872 | tf_op jit(solution)/shard_map/ppermute | solution.py:73
  11.0 4.1 %collective-permute-start.3 = (f32[4,128,256]{2,1,0:T(8,128)}, f32[4,128,256]{2,1,0:T(8,128)}, u32[]{:S(2)}, u32[]{:S(2)}) collective-permute-start(f32[4,128,256]{2,1,0:T(8,128)} %get-tuple-element.20), channel_id=1, source_target_pairs={{1,2},{3,4},{5,6},{2,1},{4,3},{6,5},{9,10},{11,12},{13,14},{10,9},... | collective-permute-start | bytes 1572872 | tf_op jit(solution)/shard_map/ppermute | solution.py:73
  15.1 8.1 %apply_own.1 = (f32[3072,256]{1,0:T(8,128)S(1)}, f32[288,128,128]{2,1,0:T(8,128)S(1)}) custom-call(s32[376]{0:T(512)S(1)} %get-tuple-element.14.pairs, f32[3072,256]{1,0:T(8,128)S(1)} %copy-done, f32[288,128,128]{2,1,0:T(8,128)} %bitcast.4), custom_call_target="tpu_custom_call" | custom-call | flops 4000000000 | bytes 26214400 | tf_op jit(solution)/shard_map/apply_own/pallas_call | solution.py:256
  23.2 0.0 collective-permute-done.g0
  23.3 0.0 collective-permute-done.3.g3
  23.3 7.9 %apply_ghosts.1 = (f32[3072,256]{1,0:T(8,128)S(1)}, bf16[3072,256]{1,0:T(8,128)(2,1)}, bf16[3072,256]{1,0:T(8,128)(2,1)}, f32[272,128]{1,0:T(8,128)S(1)}) custom-call(s32[376]{0:T(512)S(1)} %get-tuple-element.13.pairs, f32[3072,256]{1,0:T(8,128)S(1)} %get-tuple-element.15._, ...), custom_call_target="tpu_custom_call", output_to_operand_aliasing={{0}: (1, {})} | custom-call | flops 3000000000 | bytes 26214400 | tf_op jit(solution)/shard_map/apply_ghosts/pallas_call | solution.py:326
  31.2 1.3 %collective-permute-start.4 = (f32[136,128]{1,0:T(8,128)S(1)}, f32[136,128]{1,0:T(8,128)S(1)}, u32[]{:S(2)}, u32[]{:S(2)}) collective-permute-start(f32[136,128]{1,0:T(8,128)S(1)} %constant_dynamic-slice_fusion), channel_id=1, source_target_pairs={{0,1},{1,0},{2,3},{3,2},{4,5},{5,4},{6,7},{7,6},{32,33},{33,32},{3... | collective-permute-start | bytes 208904 | tf_op jit(solution)/shard_map/ppermute | solution.py:80
  32.5 0.9 %collective-permute-done.4 = f32[136,128]{1,0:T(8,128)S(1)} collective-permute-done((f32[136,128]{1,0:T(8,128)S(1)}, f32[136,128]{1,0:T(8,128)S(1)}, u32[]{:S(2)}, u32[]{:S(2)}) %collective-permute-start.4) | collective-permute-done | bytes 69664 | tf_op jit(solution)/shard_map/ppermute | solution.py:80
  33.4 2.1 %collective-permute-start.5 = (f32[136,128]{1,0:T(8,128)S(1)}, f32[136,128]{1,0:T(8,128)S(1)}, u32[]{:S(2)}, u32[]{:S(2)}) collective-permute-start(f32[136,128]{1,0:T(8,128)S(1)} %dynamic-slice_add_fusion), channel_id=1, source_target_pairs={{0,8},{1,9},{2,10},{3,11},{4,12},{5,13},{6,14},{7,15},{32,40},{33,... | collective-permute-start | bytes 208904 | tf_op jit(solution)/shard_map/ppermute | solution.py:83
  35.4 5.1 %collective-permute-start.6 = (f32[136,128]{1,0:T(8,128)S(1)}, f32[136,128]{1,0:T(8,128)S(1)}, u32[]{:S(2)}, u32[]{:S(2)}) collective-permute-start(f32[136,128]{1,0:T(8,128)S(1)} %dynamic-slice_add_fusion), channel_id=1, source_target_pairs={{0,24},{1,25},{2,26},{3,27},{4,28},{5,29},{6,30},{7,31},{32,56},{3... | collective-permute-start | bytes 208904 | tf_op jit(solution)/shard_map/ppermute | solution.py:83
  40.5 1.1 %collective-permute-start.7 = (f32[136,128]{1,0:T(8,128)S(1)}, f32[136,128]{1,0:T(8,128)S(1)}, u32[]{:S(2)}, u32[]{:S(2)}) collective-permute-start(f32[136,128]{1,0:T(8,128)S(1)} %dynamic-slice_add_fusion), channel_id=1, source_target_pairs={{0,16},{1,17},{2,18},{3,19},{4,20},{5,21},{6,22},{7,23},{32,48},{3... | collective-permute-start | bytes 208904 | tf_op jit(solution)/shard_map/ppermute | solution.py:83
  41.6 1.3 %collective-permute-done.6 = f32[136,128]{1,0:T(8,128)S(1)} collective-permute-done((f32[136,128]{1,0:T(8,128)S(1)}, f32[136,128]{1,0:T(8,128)S(1)}, u32[]{:S(2)}, u32[]{:S(2)}) %collective-permute-start.6) | collective-permute-done | bytes 69664 | tf_op jit(solution)/shard_map/ppermute | solution.py:83
  42.9 2.3 %collective-permute-done.7 = f32[136,128]{1,0:T(8,128)S(1)} collective-permute-done((f32[136,128]{1,0:T(8,128)S(1)}, f32[136,128]{1,0:T(8,128)S(1)}, u32[]{:S(2)}, u32[]{:S(2)}) %collective-permute-start.7) | collective-permute-done | bytes 69664 | tf_op jit(solution)/shard_map/ppermute | solution.py:83
  45.2 1.9 %collective-permute-start.10 = (f32[136,128]{1,0:T(8,128)S(1)}, f32[136,128]{1,0:T(8,128)S(1)}, u32[]{:S(2)}, u32[]{:S(2)}) collective-permute-start(f32[136,128]{1,0:T(8,128)S(1)} %add_add_fusion.2), channel_id=1, source_target_pairs={{0,64},{1,65},{2,66},{3,67},{4,68},{5,69},{6,70},{7,71},{32,96},{3... | collective-permute-start | bytes 208904 | tf_op jit(solution)/shard_map/ppermute | solution.py:83
  47.1 1.8 %collective-permute-start.8 = (f32[136,128]{1,0:T(8,128)S(1)}, f32[136,128]{1,0:T(8,128)S(1)}, u32[]{:S(2)}, u32[]{:S(2)}) collective-permute-start(f32[136,128]{1,0:T(8,128)S(1)} %add_add_fusion.2), channel_id=1, source_target_pairs={{0,32},{1,33},{2,34},{3,35},{4,36},{5,37},{6,38},{7,39},{32,0},{33... | collective-permute-start | bytes 208904 | tf_op jit(solution)/shard_map/ppermute | solution.py:83
  48.8 0.0 collective-permute-start.9
  48.9 1.1 %collective-permute-done.10 = f32[136,128]{1,0:T(8,128)S(1)} collective-permute-done((f32[136,128]{1,0:T(8,128)S(1)}, f32[136,128]{1,0:T(8,128)S(1)}, u32[]{:S(2)}, u32[]{:S(2)}) %collective-permute-start.10) | collective-permute-done | bytes 69664 | tf_op jit(solution)/shard_map/ppermute | solution.py:83
  49.9 1.9 %collective-permute-done.8 = f32[136,128]{1,0:T(8,128)S(1)} collective-permute-done((f32[136,128]{1,0:T(8,128)S(1)}, f32[136,128]{1,0:T(8,128)S(1)}, u32[]{:S(2)}, u32[]{:S(2)}) %collective-permute-start.8) | collective-permute-done | bytes 69664 | tf_op jit(solution)/shard_map/ppermute | solution.py:83
  51.8 1.4 %collective-permute-done.9 = f32[136,128]{1,0:T(8,128)S(1)} collective-permute-done((f32[136,128]{1,0:T(8,128)S(1)}, f32[136,128]{1,0:T(8,128)S(1)}, u32[]{:S(2)}, u32[]{:S(2)}) %collective-permute-start.9) | collective-permute-done | bytes 69664 | tf_op jit(solution)/shard_map/ppermute | solution.py:83
  53.2 1.4 %collective-permute-start.11 = (f32[136,128]{1,0:T(8,128)S(1)}, f32[136,128]{1,0:T(8,128)S(1)}, u32[]{:S(2)}, u32[]{:S(2)}) collective-permute-start(f32[136,128]{1,0:T(8,128)S(1)} %add_add_fusion.1), channel_id=1, source_target_pairs={{0,2},{1,3},{2,0},{3,1},{4,6},{5,7},{6,4},{7,5},{32,34},{33,35},{3... | collective-permute-start | bytes 208904 | tf_op jit(solution)/shard_map/ppermute | solution.py:83
  54.6 2.1 %collective-permute-start.12 = (f32[136,128]{1,0:T(8,128)S(1)}, f32[136,128]{1,0:T(8,128)S(1)}, u32[]{:S(2)}, u32[]{:S(2)}) collective-permute-start(f32[136,128]{1,0:T(8,128)S(1)} %add_add_fusion.1), channel_id=1, source_target_pairs={{0,6},{1,7},{2,4},{3,5},{4,2},{5,3},{6,0},{7,1},{32,38},{33,39},{3... | collective-permute-start | bytes 208904 | tf_op jit(solution)/shard_map/ppermute | solution.py:83
  56.7 1.0 %collective-permute-start.13 = (f32[136,128]{1,0:T(8,128)S(1)}, f32[136,128]{1,0:T(8,128)S(1)}, u32[]{:S(2)}, u32[]{:S(2)}) collective-permute-start(f32[136,128]{1,0:T(8,128)S(1)} %add_add_fusion.1), channel_id=1, source_target_pairs={{0,4},{1,5},{2,6},{3,7},{4,0},{5,1},{6,2},{7,3},{32,36},{33,37},{3... | collective-permute-start | bytes 208904 | tf_op jit(solution)/shard_map/ppermute | solution.py:83
  57.7 1.3 %collective-permute-done.12 = f32[136,128]{1,0:T(8,128)S(1)} collective-permute-done((f32[136,128]{1,0:T(8,128)S(1)}, f32[136,128]{1,0:T(8,128)S(1)}, u32[]{:S(2)}, u32[]{:S(2)}) %collective-permute-start.12) | collective-permute-done | bytes 69664 | tf_op jit(solution)/shard_map/ppermute | solution.py:83
  59.0 2.4 %collective-permute-done.13 = f32[136,128]{1,0:T(8,128)S(1)} collective-permute-done((f32[136,128]{1,0:T(8,128)S(1)}, f32[136,128]{1,0:T(8,128)S(1)}, u32[]{:S(2)}, u32[]{:S(2)}) %collective-permute-start.13) | collective-permute-done | bytes 69664 | tf_op jit(solution)/shard_map/ppermute | solution.py:83
  61.4 4.4 %collective-permute-start.14 = (f32[136,128]{1,0:T(8,128)S(1)}, f32[136,128]{1,0:T(8,128)S(1)}, u32[]{:S(2)}, u32[]{:S(2)}) collective-permute-start(f32[136,128]{1,0:T(8,128)S(1)} %add_add_fusion), channel_id=1, source_target_pairs={{0,1},{1,0},{2,3},{3,2},{4,5},{5,4},{6,7},{7,6},{32,33},{33,32},{3... | collective-permute-start | bytes 208904 | tf_op jit(solution)/shard_map/ppermute | solution.py:85
  65.8 0.9 %collective-permute-done.14 = f32[136,128]{1,0:T(8,128)S(1)} collective-permute-done((f32[136,128]{1,0:T(8,128)S(1)}, f32[136,128]{1,0:T(8,128)S(1)}, u32[]{:S(2)}, u32[]{:S(2)}) %collective-permute-start.14) | collective-permute-done | bytes 69664 | tf_op jit(solution)/shard_map/ppermute | solution.py:85
  66.8 12.0 %factor_and_basis.1 = (f32[3072,256]{1,0:T(8,128)}, f32[256,256]{1,0:T(8,128)}) custom-call(f32[136,128]{1,0:T(8,128)S(1)} %get-tuple-element.25.low, f32[136,128]{1,0:T(8,128)S(1)} %get-tuple-element.24.high, bf16[3072,256]{1,0:T(8,128)(2,1)} %get-tuple-element.22.rows_high, bf16[3072,256]{1,0:T(8,128)(2,1)} %get-tuple-element.23.rows_low), custom_call_target="tpu_custom_call" | custom-call | flops 1000000000 | bytes 7340032 | tf_op jit(solution)/shard_map/factor_and_basis/pallas_call | solution.py:493
  (11 shorter events, 0.1 us)
Async XLA Ops:
  0.6 14.5 %copy-start = (f32[3072,256]{1,0:T(8,128)S(1)}, f32[3072,256]{1,0:T(8,128)}, u32[]{:S(2)}) copy-start(f32[3072,256]{1,0:T(8,128)} %own.3) | copy-start | bytes 9437188
  6.6 16.7 %collective-permute-start = (f32[4,128,256]{2,1,0:T(8,128)}, f32[4,128,256]{2,1,0:T(8,128)}, u32[]{:S(2)}, u32[]{:S(2)}) collective-permute-start(f32[4,128,256]{2,1,0:T(8,128)} %get-tuple-element.17), channel_id=1, source_target_pairs={{0,8},{16,24},{32,40},{48,56},{64,72},{80,88},{96,104},{112,120},{... | collective-permute-start | bytes 1572872 | tf_op jit(solution)/shard_map/ppermute | solution.py:73
  8.4 14.8 %collective-permute-start.1 = (f32[4,128,256]{2,1,0:T(8,128)}, f32[4,128,256]{2,1,0:T(8,128)}, u32[]{:S(2)}, u32[]{:S(2)}) collective-permute-start(f32[4,128,256]{2,1,0:T(8,128)} %get-tuple-element.18), channel_id=1, source_target_pairs={{8,16},{24,32},{40,48},{56,64},{72,80},{88,96},{104,112},{16,8},{3... | collective-permute-start | bytes 1572872 | tf_op jit(solution)/shard_map/ppermute | solution.py:73
  9.9 13.4 %collective-permute-start.2 = (f32[4,128,256]{2,1,0:T(8,128)}, f32[4,128,256]{2,1,0:T(8,128)}, u32[]{:S(2)}, u32[]{:S(2)}) collective-permute-start(f32[4,128,256]{2,1,0:T(8,128)} %get-tuple-element.19), channel_id=1, source_target_pairs={{0,1},{2,3},{4,5},{6,7},{1,0},{3,2},{5,4},{7,6},{8,9},{10,11},{12,... | collective-permute-start | bytes 1572872 | tf_op jit(solution)/shard_map/ppermute | solution.py:73
  11.0 12.3 %collective-permute-start.3 = (f32[4,128,256]{2,1,0:T(8,128)}, f32[4,128,256]{2,1,0:T(8,128)}, u32[]{:S(2)}, u32[]{:S(2)}) collective-permute-start(f32[4,128,256]{2,1,0:T(8,128)} %get-tuple-element.20), channel_id=1, source_target_pairs={{1,2},{3,4},{5,6},{2,1},{4,3},{6,5},{9,10},{11,12},{13,14},{10,9},... | collective-permute-start | bytes 1572872 | tf_op jit(solution)/shard_map/ppermute | solution.py:73
  31.2 2.2 %collective-permute-start.4 = (f32[136,128]{1,0:T(8,128)S(1)}, f32[136,128]{1,0:T(8,128)S(1)}, u32[]{:S(2)}, u32[]{:S(2)}) collective-permute-start(f32[136,128]{1,0:T(8,128)S(1)} %constant_dynamic-slice_fusion), channel_id=1, source_target_pairs={{0,1},{1,0},{2,3},{3,2},{4,5},{5,4},{6,7},{7,6},{32,33},{33,32},{3... | collective-permute-start | bytes 208904 | tf_op jit(solution)/shard_map/ppermute | solution.py:80
  33.4 8.2 %collective-permute-start.5 = (f32[136,128]{1,0:T(8,128)S(1)}, f32[136,128]{1,0:T(8,128)S(1)}, u32[]{:S(2)}, u32[]{:S(2)}) collective-permute-start(f32[136,128]{1,0:T(8,128)S(1)} %dynamic-slice_add_fusion), channel_id=1, source_target_pairs={{0,8},{1,9},{2,10},{3,11},{4,12},{5,13},{6,14},{7,15},{32,40},{33,... | collective-permute-start | bytes 208904 | tf_op jit(solution)/shard_map/ppermute | solution.py:83
  35.4 7.5 %collective-permute-start.6 = (f32[136,128]{1,0:T(8,128)S(1)}, f32[136,128]{1,0:T(8,128)S(1)}, u32[]{:S(2)}, u32[]{:S(2)}) collective-permute-start(f32[136,128]{1,0:T(8,128)S(1)} %dynamic-slice_add_fusion), channel_id=1, source_target_pairs={{0,24},{1,25},{2,26},{3,27},{4,28},{5,29},{6,30},{7,31},{32,56},{3... | collective-permute-start | bytes 208904 | tf_op jit(solution)/shard_map/ppermute | solution.py:83
  40.5 4.7 %collective-permute-start.7 = (f32[136,128]{1,0:T(8,128)S(1)}, f32[136,128]{1,0:T(8,128)S(1)}, u32[]{:S(2)}, u32[]{:S(2)}) collective-permute-start(f32[136,128]{1,0:T(8,128)S(1)} %dynamic-slice_add_fusion), channel_id=1, source_target_pairs={{0,16},{1,17},{2,18},{3,19},{4,20},{5,21},{6,22},{7,23},{32,48},{3... | collective-permute-start | bytes 208904 | tf_op jit(solution)/shard_map/ppermute | solution.py:83
  45.2 4.7 %collective-permute-start.10 = (f32[136,128]{1,0:T(8,128)S(1)}, f32[136,128]{1,0:T(8,128)S(1)}, u32[]{:S(2)}, u32[]{:S(2)}) collective-permute-start(f32[136,128]{1,0:T(8,128)S(1)} %add_add_fusion.2), channel_id=1, source_target_pairs={{0,64},{1,65},{2,66},{3,67},{4,68},{5,69},{6,70},{7,71},{32,96},{3... | collective-permute-start | bytes 208904 | tf_op jit(solution)/shard_map/ppermute | solution.py:83
  47.1 4.7 %collective-permute-start.8 = (f32[136,128]{1,0:T(8,128)S(1)}, f32[136,128]{1,0:T(8,128)S(1)}, u32[]{:S(2)}, u32[]{:S(2)}) collective-permute-start(f32[136,128]{1,0:T(8,128)S(1)} %add_add_fusion.2), channel_id=1, source_target_pairs={{0,32},{1,33},{2,34},{3,35},{4,36},{5,37},{6,38},{7,39},{32,0},{33... | collective-permute-start | bytes 208904 | tf_op jit(solution)/shard_map/ppermute | solution.py:83
  48.8 4.4 %collective-permute-start.9 = (f32[136,128]{1,0:T(8,128)S(1)}, f32[136,128]{1,0:T(8,128)S(1)}, u32[]{:S(2)}, u32[]{:S(2)}) collective-permute-start(f32[136,128]{1,0:T(8,128)S(1)} %add_add_fusion.2), channel_id=1, source_target_pairs={{0,96},{1,97},{2,98},{3,99},{4,100},{5,101},{6,102},{7,103},{32,64... | collective-permute-start | bytes 208904 | tf_op jit(solution)/shard_map/ppermute | solution.py:83
  53.2 4.4 %collective-permute-start.11 = (f32[136,128]{1,0:T(8,128)S(1)}, f32[136,128]{1,0:T(8,128)S(1)}, u32[]{:S(2)}, u32[]{:S(2)}) collective-permute-start(f32[136,128]{1,0:T(8,128)S(1)} %add_add_fusion.1), channel_id=1, source_target_pairs={{0,2},{1,3},{2,0},{3,1},{4,6},{5,7},{6,4},{7,5},{32,34},{33,35},{3... | collective-permute-start | bytes 208904 | tf_op jit(solution)/shard_map/ppermute | solution.py:83
  54.6 4.4 %collective-permute-start.12 = (f32[136,128]{1,0:T(8,128)S(1)}, f32[136,128]{1,0:T(8,128)S(1)}, u32[]{:S(2)}, u32[]{:S(2)}) collective-permute-start(f32[136,128]{1,0:T(8,128)S(1)} %add_add_fusion.1), channel_id=1, source_target_pairs={{0,6},{1,7},{2,4},{3,5},{4,2},{5,3},{6,0},{7,1},{32,38},{33,39},{3... | collective-permute-start | bytes 208904 | tf_op jit(solution)/shard_map/ppermute | solution.py:83
  56.7 4.7 %collective-permute-start.13 = (f32[136,128]{1,0:T(8,128)S(1)}, f32[136,128]{1,0:T(8,128)S(1)}, u32[]{:S(2)}, u32[]{:S(2)}) collective-permute-start(f32[136,128]{1,0:T(8,128)S(1)} %add_add_fusion.1), channel_id=1, source_target_pairs={{0,4},{1,5},{2,6},{3,7},{4,0},{5,1},{6,2},{7,3},{32,36},{33,37},{3... | collective-permute-start | bytes 208904 | tf_op jit(solution)/shard_map/ppermute | solution.py:83
  61.4 5.3 %collective-permute-start.14 = (f32[136,128]{1,0:T(8,128)S(1)}, f32[136,128]{1,0:T(8,128)S(1)}, u32[]{:S(2)}, u32[]{:S(2)}) collective-permute-start(f32[136,128]{1,0:T(8,128)S(1)} %add_add_fusion), channel_id=1, source_target_pairs={{0,1},{1,0},{2,3},{3,2},{4,5},{5,4},{6,7},{7,6},{32,33},{33,32},{3... | collective-permute-start | bytes 208904 | tf_op jit(solution)/shard_map/ppermute | solution.py:85

commit v5 on v4

--- a/solution.py
+++ b/solution.py
@@ -79,9 +79,11 @@
     other = lax.dynamic_slice_in_dim(packed, (1 - core) * HALF, HALF, 0)
     total = mine + lax.ppermute(other, AXES, CORE_ROUTE)
     for dim in range(3):
-        routes = (pair_route(dim, False), pair_route(dim, True), far_route(dim))
-        near, wrap, far = [lax.ppermute(total, AXES, r) for r in routes]
-        total = (total + near) + (wrap + far)
+        routes = [pair_route(dim, False), pair_route(dim, True), far_route(dim)]
+        if dim == 1:
+            routes = routes[1:] + routes[:1]
+        first, second, third = [lax.ppermute(total, AXES, r) for r in routes]
+        total = (total + first) + (second + third)
     theirs = lax.ppermute(total, AXES, CORE_ROUTE)
     low = jnp.where(core == 0, total, theirs)
     high = jnp.where(core == 0, theirs, total)
@@ -282,8 +284,8 @@
     return jnp.concatenate([jnp.where(i <= j, first, second), gram[:BS, BS:], tail], axis=0)
 
 
-def ghost_kernel(pairs, _, held, g0, g1, g2, g3, total, high, low, gram, xh, xl, xv, ah, al, sems, out_sems):
-    arrivals = [pltpu.make_async_copy(g, xv.at[e], sems.at[e]) for e, g in enumerate((g0, g1, g2, g3))]
+def ghost_kernel(pairs, _, held, px_odd, py_even, px_even, py_odd, total, high, low, gram, xh, xl, xv, ah, al, sems, out_sems):
+    arrivals = [pltpu.make_async_copy(g, xv.at[e], sems.at[e]) for e, g in enumerate((px_even, px_odd, py_even, py_odd))]
     for c in arrivals:
         c.start()
     xh[4 * GMAX * BS :] = jnp.zeros((BS, K), BF16)
@@ -524,7 +526,7 @@
     px_even = swapped(px_even, "px", False)
     py_odd = swapped(py_odd, "py", True)
     part, held = apply_own(own_pairs, block_vectors, tiles)
-    ah, al, gram = apply_ghosts(ghost_pairs, part, held, [px_even, px_odd, py_even, py_odd])
+    ah, al, gram = apply_ghosts(ghost_pairs, part, held, [px_odd, py_even, px_even, py_odd])
     low, high = sum_everywhere(gram)
     return tuple(orthonormalize(low, high, ah, al))
 

time: 79.1 us -> 80.4 us (1.016)
  starting transfers between devices: 30.5 us -> 31.9 us
    ppermute x4, starting transfers between devices: 8.5 us -> 10.2 us  [swapped(): return lax.ppermute(block, axis, pairs + [(j, i) for i, j in pairs])]
    ppermute x9, starting transfers between devices: 16.3 us -> 14.7 us  [sum_everywhere(): first, second, third = [lax.ppermute(total, AXES, r) for r in routes]]
    ppermute x1, starting transfers between devices: 1.27 us -> 2.52 us  [sum_everywhere(): total = mine + lax.ppermute(other, AXES, CORE_ROUTE)]
    ppermute x4, waiting for transfers between devices: 0.01 us -> 1.01 us  [swapped(): return lax.ppermute(block, axis, pairs + [(j, i) for i, j in pairs])]
where the time goes in v5:
time: 80.4 us; the launch traced here: 80.3 us
  Pallas kernels  32.6 us (41%)
  starting transfers between devices  31.9 us (40%)
  waiting for transfers between devices  13.9 us (17%)
  between operations  1.71 us (2%)
    ppermute x9, starting transfers between devices, sum_everywhere(): first, second, third = [lax.ppermute(total, AXES, r) for r in routes]  14.7 us
    pallas_call x1, Pallas kernels, orthonormalize(): pl.pallas_call(basis_kernel, out_shape=[jax.ShapeDtypeStruct((NBD * BS, K...  12 us
    ppermute x9, waiting for transfers between devices, sum_everywhere(): first, second, third = [lax.ppermute(total, AXES, r) for r in routes]  11.1 us
    ppermute x4, starting transfers between devices, swapped(): return lax.ppermute(block, axis, pairs + [(j, i) for i, j in pairs])  10.2 us
    pallas_call x1, Pallas kernels, apply_own(): pl.pallas_call(own_kernel, out_shape=[pltpu.VMEM((NBD * BS, K), F32), plt...  7.91 us
    pallas_call x1, Pallas kernels, apply_ghosts(): pl.pallas_call(ghost_kernel, out_shape=[pltpu.VMEM((NBD * BS, K), F32), p...  7.87 us
    pallas_call x1, Pallas kernels, prepare(): pl.pallas_call(prepare_kernel, out_shape=[jax.ShapeDtypeStruct((GMAX, BS,...  4.9 us
    ppermute x1, starting transfers between devices, sum_everywhere(): theirs = lax.ppermute(total, AXES, CORE_ROUTE)  4.43 us
  transfers between devices with their start and end apart: 15, of which 9 were waited for; matrix products, arithmetic and copies ran while one was open for 0% of the time, Pallas kernels for 10%

profile of v5, /device:TPU:1, one launch (start us, length us, event | category | flops | bytes accessed | tf_op | source)
XLA Modules:
  0.0 80.3 jit_solution(13386070949903759715)
XLA Ops:
  0.6 0.0 copy-start
  1.5 0.1 pad_add_fusion.parity
  1.5 4.9 %prepare.1 = (f32[4,128,256]{2,1,0:T(8,128)}, f32[4,128,256]{2,1,0:T(8,128)}, f32[4,128,256]{2,1,0:T(8,128)}, f32[4,128,256]{2,1,0:T(8,128)}, s32[376]{0:T(512)S(1)}, /*index=5*/s32[376]{0:T(512)S(1)}) custom-call(s32[2]{0:T(128)S(1)} %pad_add_fusion.parity, s32[1]{0:T(128)S(6)} %copy.10.live, s32[1,4,4]{2,1,0:T(4,128)} %lists_in.1, s32[1,4]{1,0:T(1,128)} %counts_in.1, ...), custom_call_target="tpu_custom_call" | custom-call | bytes 4194304 | tf_op jit(solution)/shard_map/prepare/pallas_call | solution.py:181
  6.4 1.5 %collective-permute-start = (f32[4,128,256]{2,1,0:T(8,128)}, f32[4,128,256]{2,1,0:T(8,128)}, u32[]{:S(2)}, u32[]{:S(2)}) collective-permute-start(f32[4,128,256]{2,1,0:T(8,128)} %get-tuple-element.17), channel_id=1, source_target_pairs={{8,16},{24,32},{40,48},{56,64},{72,80},{88,96},{104,112},{16,8},{3... | collective-permute-start | bytes 1572872 | tf_op jit(solution)/shard_map/ppermute | solution.py:73
  7.9 2.1 %collective-permute-start.1 = (f32[4,128,256]{2,1,0:T(8,128)}, f32[4,128,256]{2,1,0:T(8,128)}, u32[]{:S(2)}, u32[]{:S(2)}) collective-permute-start(f32[4,128,256]{2,1,0:T(8,128)} %get-tuple-element.18), channel_id=1, source_target_pairs={{0,1},{2,3},{4,5},{6,7},{1,0},{3,2},{5,4},{7,6},{8,9},{10,11},{12,... | collective-permute-start | bytes 1572872 | tf_op jit(solution)/shard_map/ppermute | solution.py:73
  10.0 3.1 %collective-permute-start.2 = (f32[4,128,256]{2,1,0:T(8,128)}, f32[4,128,256]{2,1,0:T(8,128)}, u32[]{:S(2)}, u32[]{:S(2)}) collective-permute-start(f32[4,128,256]{2,1,0:T(8,128)} %get-tuple-element.19), channel_id=1, source_target_pairs={{0,8},{16,24},{32,40},{48,56},{64,72},{80,88},{96,104},{112,120},{... | collective-permute-start | bytes 1572872 | tf_op jit(solution)/shard_map/ppermute | solution.py:73
  13.1 3.5 %collective-permute-start.3 = (f32[4,128,256]{2,1,0:T(8,128)}, f32[4,128,256]{2,1,0:T(8,128)}, u32[]{:S(2)}, u32[]{:S(2)}) collective-permute-start(f32[4,128,256]{2,1,0:T(8,128)} %get-tuple-element.20), channel_id=1, source_target_pairs={{1,2},{3,4},{5,6},{2,1},{4,3},{6,5},{9,10},{11,12},{13,14},{10,9},... | collective-permute-start | bytes 1572872 | tf_op jit(solution)/shard_map/ppermute | solution.py:73
  16.7 7.9 %apply_own.1 = (f32[3072,256]{1,0:T(8,128)S(1)}, f32[288,128,128]{2,1,0:T(8,128)S(1)}) custom-call(s32[376]{0:T(512)S(1)} %get-tuple-element.14.pairs, f32[3072,256]{1,0:T(8,128)S(1)} %copy-done, f32[288,128,128]{2,1,0:T(8,128)} %bitcast.4), custom_call_target="tpu_custom_call" | custom-call | flops 4000000000 | bytes 26214400 | tf_op jit(solution)/shard_map/apply_own/pallas_call | solution.py:258
  24.6 0.0 collective-permute-done.1.py_even
  24.6 1.0 %collective-permute-done.2.px_even = f32[4,128,256]{2,1,0:T(8,128)} collective-permute-done((f32[4,128,256]{2,1,0:T(8,128)}, f32[4,128,256]{2,1,0:T(8,128)}, u32[]{:S(2)}, u32[]{:S(2)}) %collective-permute-start.2) | collective-permute-done | bytes 524320 | tf_op jit(solution)/shard_map/ppermute | solution.py:73
  25.6 0.0 collective-permute-done.3.py_odd
  25.6 7.9 %apply_ghosts.1 = (f32[3072,256]{1,0:T(8,128)S(1)}, bf16[3072,256]{1,0:T(8,128)(2,1)}, bf16[3072,256]{1,0:T(8,128)(2,1)}, f32[272,128]{1,0:T(8,128)S(1)}) custom-call(s32[376]{0:T(512)S(1)} %get-tuple-element.13.pairs, f32[3072,256]{1,0:T(8,128)S(1)} %get-tuple-element.15._, ...), custom_call_target="tpu_custom_call", output_to_operand_aliasing={{0}: (1, {})} | custom-call | flops 3000000000 | bytes 26214400 | tf_op jit(solution)/shard_map/apply_ghosts/pallas_call | solution.py:328
  33.5 2.5 %collective-permute-start.4 = (f32[136,128]{1,0:T(8,128)S(1)}, f32[136,128]{1,0:T(8,128)S(1)}, u32[]{:S(2)}, u32[]{:S(2)}) collective-permute-start(f32[136,128]{1,0:T(8,128)S(1)} %constant_dynamic-slice_fusion), channel_id=1, source_target_pairs={{0,1},{1,0},{2,3},{3,2},{4,5},{5,4},{6,7},{7,6},{32,33},{33,32},{3... | collective-permute-start | bytes 208904 | tf_op jit(solution)/shard_map/ppermute | solution.py:80
  36.0 0.9 %collective-permute-done.4 = f32[136,128]{1,0:T(8,128)S(1)} collective-permute-done((f32[136,128]{1,0:T(8,128)S(1)}, f32[136,128]{1,0:T(8,128)S(1)}, u32[]{:S(2)}, u32[]{:S(2)}) %collective-permute-start.4) | collective-permute-done | bytes 69664 | tf_op jit(solution)/shard_map/ppermute | solution.py:80
  36.9 0.7 collective-permute-start.5
  37.6 1.6 %collective-permute-start.6 = (f32[136,128]{1,0:T(8,128)S(1)}, f32[136,128]{1,0:T(8,128)S(1)}, u32[]{:S(2)}, u32[]{:S(2)}) collective-permute-start(f32[136,128]{1,0:T(8,128)S(1)} %dynamic-slice_add_fusion), channel_id=1, source_target_pairs={{0,24},{1,25},{2,26},{3,27},{4,28},{5,29},{6,30},{7,31},{32,56},{3... | collective-permute-start | bytes 208904 | tf_op jit(solution)/shard_map/ppermute | solution.py:85
  39.2 1.1 %collective-permute-start.7 = (f32[136,128]{1,0:T(8,128)S(1)}, f32[136,128]{1,0:T(8,128)S(1)}, u32[]{:S(2)}, u32[]{:S(2)}) collective-permute-start(f32[136,128]{1,0:T(8,128)S(1)} %dynamic-slice_add_fusion), channel_id=1, source_target_pairs={{0,16},{1,17},{2,18},{3,19},{4,20},{5,21},{6,22},{7,23},{32,48},{3... | collective-permute-start | bytes 208904 | tf_op jit(solution)/shard_map/ppermute | solution.py:85
  40.3 1.7 %collective-permute-done.6 = f32[136,128]{1,0:T(8,128)S(1)} collective-permute-done((f32[136,128]{1,0:T(8,128)S(1)}, f32[136,128]{1,0:T(8,128)S(1)}, u32[]{:S(2)}, u32[]{:S(2)}) %collective-permute-start.6) | collective-permute-done | bytes 69664 | tf_op jit(solution)/shard_map/ppermute | solution.py:85
  42.0 1.9 %collective-permute-done.7 = f32[136,128]{1,0:T(8,128)S(1)} collective-permute-done((f32[136,128]{1,0:T(8,128)S(1)}, f32[136,128]{1,0:T(8,128)S(1)}, u32[]{:S(2)}, u32[]{:S(2)}) %collective-permute-start.7) | collective-permute-done | bytes 69664 | tf_op jit(solution)/shard_map/ppermute | solution.py:85
  43.9 2.0 %collective-permute-start.10 = (f32[136,128]{1,0:T(8,128)S(1)}, f32[136,128]{1,0:T(8,128)S(1)}, u32[]{:S(2)}, u32[]{:S(2)}) collective-permute-start(f32[136,128]{1,0:T(8,128)S(1)} %add_add_fusion.2), channel_id=1, source_target_pairs={{0,32},{1,33},{2,34},{3,35},{4,36},{5,37},{6,38},{7,39},{32,0},{33... | collective-permute-start | bytes 208904 | tf_op jit(solution)/shard_map/ppermute | solution.py:85
  45.9 2.8 %collective-permute-start.8 = (f32[136,128]{1,0:T(8,128)S(1)}, f32[136,128]{1,0:T(8,128)S(1)}, u32[]{:S(2)}, u32[]{:S(2)}) collective-permute-start(f32[136,128]{1,0:T(8,128)S(1)} %add_add_fusion.2), channel_id=1, source_target_pairs={{0,96},{1,97},{2,98},{3,99},{4,100},{5,101},{6,102},{7,103},{32,64... | collective-permute-start | bytes 208904 | tf_op jit(solution)/shard_map/ppermute | solution.py:85
  48.8 1.1 %collective-permute-start.9 = (f32[136,128]{1,0:T(8,128)S(1)}, f32[136,128]{1,0:T(8,128)S(1)}, u32[]{:S(2)}, u32[]{:S(2)}) collective-permute-start(f32[136,128]{1,0:T(8,128)S(1)} %add_add_fusion.2), channel_id=1, source_target_pairs={{0,64},{1,65},{2,66},{3,67},{4,68},{5,69},{6,70},{7,71},{32,96},{3... | collective-permute-start | bytes 208904 | tf_op jit(solution)/shard_map/ppermute | solution.py:85
  49.9 0.6 collective-permute-done.8
  50.5 3.1 %collective-permute-done.9 = f32[136,128]{1,0:T(8,128)S(1)} collective-permute-done((f32[136,128]{1,0:T(8,128)S(1)}, f32[136,128]{1,0:T(8,128)S(1)}, u32[]{:S(2)}, u32[]{:S(2)}) %collective-permute-start.9) | collective-permute-done | bytes 69664 | tf_op jit(solution)/shard_map/ppermute | solution.py:85
  53.6 2.3 %collective-permute-start.11 = (f32[136,128]{1,0:T(8,128)S(1)}, f32[136,128]{1,0:T(8,128)S(1)}, u32[]{:S(2)}, u32[]{:S(2)}) collective-permute-start(f32[136,128]{1,0:T(8,128)S(1)} %add_add_fusion.1), channel_id=1, source_target_pairs={{0,2},{1,3},{2,0},{3,1},{4,6},{5,7},{6,4},{7,5},{32,34},{33,35},{3... | collective-permute-start | bytes 208904 | tf_op jit(solution)/shard_map/ppermute | solution.py:85
  55.9 2.2 %collective-permute-start.12 = (f32[136,128]{1,0:T(8,128)S(1)}, f32[136,128]{1,0:T(8,128)S(1)}, u32[]{:S(2)}, u32[]{:S(2)}) collective-permute-start(f32[136,128]{1,0:T(8,128)S(1)} %add_add_fusion.1), channel_id=1, source_target_pairs={{0,6},{1,7},{2,4},{3,5},{4,2},{5,3},{6,0},{7,1},{32,38},{33,39},{3... | collective-permute-start | bytes 208904 | tf_op jit(solution)/shard_map/ppermute | solution.py:85
  58.1 0.9 %collective-permute-start.13 = (f32[136,128]{1,0:T(8,128)S(1)}, f32[136,128]{1,0:T(8,128)S(1)}, u32[]{:S(2)}, u32[]{:S(2)}) collective-permute-start(f32[136,128]{1,0:T(8,128)S(1)} %add_add_fusion.1), channel_id=1, source_target_pairs={{0,4},{1,5},{2,6},{3,7},{4,0},{5,1},{6,2},{7,3},{32,36},{33,37},{3... | collective-permute-start | bytes 208904 | tf_op jit(solution)/shard_map/ppermute | solution.py:85
  59.0 1.3 %collective-permute-done.12 = f32[136,128]{1,0:T(8,128)S(1)} collective-permute-done((f32[136,128]{1,0:T(8,128)S(1)}, f32[136,128]{1,0:T(8,128)S(1)}, u32[]{:S(2)}, u32[]{:S(2)}) %collective-permute-start.12) | collective-permute-done | bytes 69664 | tf_op jit(solution)/shard_map/ppermute | solution.py:85
  60.3 2.5 %collective-permute-done.13 = f32[136,128]{1,0:T(8,128)S(1)} collective-permute-done((f32[136,128]{1,0:T(8,128)S(1)}, f32[136,128]{1,0:T(8,128)S(1)}, u32[]{:S(2)}, u32[]{:S(2)}) %collective-permute-start.13) | collective-permute-done | bytes 69664 | tf_op jit(solution)/shard_map/ppermute | solution.py:85
  62.8 4.4 %collective-permute-start.14 = (f32[136,128]{1,0:T(8,128)S(1)}, f32[136,128]{1,0:T(8,128)S(1)}, u32[]{:S(2)}, u32[]{:S(2)}) collective-permute-start(f32[136,128]{1,0:T(8,128)S(1)} %add_add_fusion), channel_id=1, source_target_pairs={{0,1},{1,0},{2,3},{3,2},{4,5},{5,4},{6,7},{7,6},{32,33},{33,32},{3... | collective-permute-start | bytes 208904 | tf_op jit(solution)/shard_map/ppermute | solution.py:87
  67.2 0.9 %collective-permute-done.14 = f32[136,128]{1,0:T(8,128)S(1)} collective-permute-done((f32[136,128]{1,0:T(8,128)S(1)}, f32[136,128]{1,0:T(8,128)S(1)}, u32[]{:S(2)}, u32[]{:S(2)}) %collective-permute-start.14) | collective-permute-done | bytes 69664 | tf_op jit(solution)/shard_map/ppermute | solution.py:87
  68.1 12.0 %factor_and_basis.1 = (f32[3072,256]{1,0:T(8,128)}, f32[256,256]{1,0:T(8,128)}) custom-call(f32[136,128]{1,0:T(8,128)S(1)} %get-tuple-element.25.low, f32[136,128]{1,0:T(8,128)S(1)} %get-tuple-element.24.high, bf16[3072,256]{1,0:T(8,128)(2,1)} %get-tuple-element.22.rows_high, bf16[3072,256]{1,0:T(8,128)(2,1)} %get-tuple-element.23.rows_low), custom_call_target="tpu_custom_call" | custom-call | flops 1000000000 | bytes 7340032 | tf_op jit(solution)/shard_map/factor_and_basis/pallas_call | solution.py:495
  (11 shorter events, 0.1 us)
Async XLA Ops:
  0.6 16.0 %copy-start = (f32[3072,256]{1,0:T(8,128)S(1)}, f32[3072,256]{1,0:T(8,128)}, u32[]{:S(2)}) copy-start(f32[3072,256]{1,0:T(8,128)} %own.3) | copy-start | bytes 9437188
  6.4 18.1 %collective-permute-start = (f32[4,128,256]{2,1,0:T(8,128)}, f32[4,128,256]{2,1,0:T(8,128)}, u32[]{:S(2)}, u32[]{:S(2)}) collective-permute-start(f32[4,128,256]{2,1,0:T(8,128)} %get-tuple-element.17), channel_id=1, source_target_pairs={{8,16},{24,32},{40,48},{56,64},{72,80},{88,96},{104,112},{16,8},{3... | collective-permute-start | bytes 1572872 | tf_op jit(solution)/shard_map/ppermute | solution.py:73
  7.9 16.7 %collective-permute-start.1 = (f32[4,128,256]{2,1,0:T(8,128)}, f32[4,128,256]{2,1,0:T(8,128)}, u32[]{:S(2)}, u32[]{:S(2)}) collective-permute-start(f32[4,128,256]{2,1,0:T(8,128)} %get-tuple-element.18), channel_id=1, source_target_pairs={{0,1},{2,3},{4,5},{6,7},{1,0},{3,2},{5,4},{7,6},{8,9},{10,11},{12,... | collective-permute-start | bytes 1572872 | tf_op jit(solution)/shard_map/ppermute | solution.py:73
  10.0 15.6 %collective-permute-start.2 = (f32[4,128,256]{2,1,0:T(8,128)}, f32[4,128,256]{2,1,0:T(8,128)}, u32[]{:S(2)}, u32[]{:S(2)}) collective-permute-start(f32[4,128,256]{2,1,0:T(8,128)} %get-tuple-element.19), channel_id=1, source_target_pairs={{0,8},{16,24},{32,40},{48,56},{64,72},{80,88},{96,104},{112,120},{... | collective-permute-start | bytes 1572872 | tf_op jit(solution)/shard_map/ppermute | solution.py:73
  13.1 12.5 %collective-permute-start.3 = (f32[4,128,256]{2,1,0:T(8,128)}, f32[4,128,256]{2,1,0:T(8,128)}, u32[]{:S(2)}, u32[]{:S(2)}) collective-permute-start(f32[4,128,256]{2,1,0:T(8,128)} %get-tuple-element.20), channel_id=1, source_target_pairs={{1,2},{3,4},{5,6},{2,1},{4,3},{6,5},{9,10},{11,12},{13,14},{10,9},... | collective-permute-start | bytes 1572872 | tf_op jit(solution)/shard_map/ppermute | solution.py:73
  33.5 3.4 %collective-permute-start.4 = (f32[136,128]{1,0:T(8,128)S(1)}, f32[136,128]{1,0:T(8,128)S(1)}, u32[]{:S(2)}, u32[]{:S(2)}) collective-permute-start(f32[136,128]{1,0:T(8,128)S(1)} %constant_dynamic-slice_fusion), channel_id=1, source_target_pairs={{0,1},{1,0},{2,3},{3,2},{4,5},{5,4},{6,7},{7,6},{32,33},{33,32},{3... | collective-permute-start | bytes 208904 | tf_op jit(solution)/shard_map/ppermute | solution.py:80
  36.9 3.4 %collective-permute-start.5 = (f32[136,128]{1,0:T(8,128)S(1)}, f32[136,128]{1,0:T(8,128)S(1)}, u32[]{:S(2)}, u32[]{:S(2)}) collective-permute-start(f32[136,128]{1,0:T(8,128)S(1)} %dynamic-slice_add_fusion), channel_id=1, source_target_pairs={{0,8},{1,9},{2,10},{3,11},{4,12},{5,13},{6,14},{7,15},{32,40},{33,... | collective-permute-start | bytes 208904 | tf_op jit(solution)/shard_map/ppermute | solution.py:85
  37.6 4.4 %collective-permute-start.6 = (f32[136,128]{1,0:T(8,128)S(1)}, f32[136,128]{1,0:T(8,128)S(1)}, u32[]{:S(2)}, u32[]{:S(2)}) collective-permute-start(f32[136,128]{1,0:T(8,128)S(1)} %dynamic-slice_add_fusion), channel_id=1, source_target_pairs={{0,24},{1,25},{2,26},{3,27},{4,28},{5,29},{6,30},{7,31},{32,56},{3... | collective-permute-start | bytes 208904 | tf_op jit(solution)/shard_map/ppermute | solution.py:85
  39.2 4.7 %collective-permute-start.7 = (f32[136,128]{1,0:T(8,128)S(1)}, f32[136,128]{1,0:T(8,128)S(1)}, u32[]{:S(2)}, u32[]{:S(2)}) collective-permute-start(f32[136,128]{1,0:T(8,128)S(1)} %dynamic-slice_add_fusion), channel_id=1, source_target_pairs={{0,16},{1,17},{2,18},{3,19},{4,20},{5,21},{6,22},{7,23},{32,48},{3... | collective-permute-start | bytes 208904 | tf_op jit(solution)/shard_map/ppermute | solution.py:85
  43.9 5.9 %collective-permute-start.10 = (f32[136,128]{1,0:T(8,128)S(1)}, f32[136,128]{1,0:T(8,128)S(1)}, u32[]{:S(2)}, u32[]{:S(2)}) collective-permute-start(f32[136,128]{1,0:T(8,128)S(1)} %add_add_fusion.2), channel_id=1, source_target_pairs={{0,32},{1,33},{2,34},{3,35},{4,36},{5,37},{6,38},{7,39},{32,0},{33... | collective-permute-start | bytes 208904 | tf_op jit(solution)/shard_map/ppermute | solution.py:85
  45.9 4.5 %collective-permute-start.8 = (f32[136,128]{1,0:T(8,128)S(1)}, f32[136,128]{1,0:T(8,128)S(1)}, u32[]{:S(2)}, u32[]{:S(2)}) collective-permute-start(f32[136,128]{1,0:T(8,128)S(1)} %add_add_fusion.2), channel_id=1, source_target_pairs={{0,96},{1,97},{2,98},{3,99},{4,100},{5,101},{6,102},{7,103},{32,64... | collective-permute-start | bytes 208904 | tf_op jit(solution)/shard_map/ppermute | solution.py:85
  48.8 4.8 %collective-permute-start.9 = (f32[136,128]{1,0:T(8,128)S(1)}, f32[136,128]{1,0:T(8,128)S(1)}, u32[]{:S(2)}, u32[]{:S(2)}) collective-permute-start(f32[136,128]{1,0:T(8,128)S(1)} %add_add_fusion.2), channel_id=1, source_target_pairs={{0,64},{1,65},{2,66},{3,67},{4,68},{5,69},{6,70},{7,71},{32,96},{3... | collective-permute-start | bytes 208904 | tf_op jit(solution)/shard_map/ppermute | solution.py:85
  53.6 5.4 %collective-permute-start.11 = (f32[136,128]{1,0:T(8,128)S(1)}, f32[136,128]{1,0:T(8,128)S(1)}, u32[]{:S(2)}, u32[]{:S(2)}) collective-permute-start(f32[136,128]{1,0:T(8,128)S(1)} %add_add_fusion.1), channel_id=1, source_target_pairs={{0,2},{1,3},{2,0},{3,1},{4,6},{5,7},{6,4},{7,5},{32,34},{33,35},{3... | collective-permute-start | bytes 208904 | tf_op jit(solution)/shard_map/ppermute | solution.py:85
  55.9 4.4 %collective-permute-start.12 = (f32[136,128]{1,0:T(8,128)S(1)}, f32[136,128]{1,0:T(8,128)S(1)}, u32[]{:S(2)}, u32[]{:S(2)}) collective-permute-start(f32[136,128]{1,0:T(8,128)S(1)} %add_add_fusion.1), channel_id=1, source_target_pairs={{0,6},{1,7},{2,4},{3,5},{4,2},{5,3},{6,0},{7,1},{32,38},{33,39},{3... | collective-permute-start | bytes 208904 | tf_op jit(solution)/shard_map/ppermute | solution.py:85
  58.1 4.7 %collective-permute-start.13 = (f32[136,128]{1,0:T(8,128)S(1)}, f32[136,128]{1,0:T(8,128)S(1)}, u32[]{:S(2)}, u32[]{:S(2)}) collective-permute-start(f32[136,128]{1,0:T(8,128)S(1)} %add_add_fusion.1), channel_id=1, source_target_pairs={{0,4},{1,5},{2,6},{3,7},{4,0},{5,1},{6,2},{7,3},{32,36},{33,37},{3... | collective-permute-start | bytes 208904 | tf_op jit(solution)/shard_map/ppermute | solution.py:85
  62.8 5.3 %collective-permute-start.14 = (f32[136,128]{1,0:T(8,128)S(1)}, f32[136,128]{1,0:T(8,128)S(1)}, u32[]{:S(2)}, u32[]{:S(2)}) collective-permute-start(f32[136,128]{1,0:T(8,128)S(1)} %add_add_fusion), channel_id=1, source_target_pairs={{0,1},{1,0},{2,3},{3,2},{4,5},{5,4},{6,7},{7,6},{32,33},{33,32},{3... | collective-permute-start | bytes 208904 | tf_op jit(solution)/shard_map/ppermute | solution.py:87

commit v6 on v4

--- a/solution.py
+++ b/solution.py
@@ -130,12 +130,12 @@
         out[0] = n >> 1
 
 
-def prepare_kernel(parity, live, lists_in, counts_in, cols_in, own, *refs):
-    outs, (own_list, ghost_list, lists, counts, cols, held) = refs[:4], refs[4:10]
-    small_sems, in_sems, out_sems = refs[10:]
+def prepare_kernel(parity, lists_in, counts_in, own, *refs):
+    outs, (lists, counts, held) = refs[:4], refs[4:7]
+    small_sems, in_sems, out_sems = refs[7:]
     small = [
         pltpu.make_async_copy(a, b, small_sems.at[n])
-        for n, (a, b) in enumerate(((lists_in, lists), (counts_in, counts), (cols_in, cols)))
+        for n, (a, b) in enumerate(((lists_in, lists), (counts_in, counts)))
     ]
     for c in small:
         c.start()
@@ -156,7 +156,6 @@
             fetch(n, s).start()
     for c in small[1:]:
         c.wait()
-    pair_lists(parity, cols, live, own_list, ghost_list)
     for n in range(4):
         for s in range(GMAX):
             fetch(n, s).wait()
@@ -171,29 +170,27 @@
             store(n, s).wait()
 
 
-def prepare(parity, lists, counts, cols, live, own):
+def prepare(parity, lists, counts, own):
     smem = pl.BlockSpec(memory_space=pltpu.SMEM)
     hbm = pl.BlockSpec(memory_space=pltpu.HBM)
     anywhere = pl.BlockSpec(memory_space=pl.ANY)
-    arrays = (lists, counts, cols, own)
-    outs = pl.pallas_call(
+    arrays = (lists, counts, own)
+    return pl.pallas_call(
         prepare_kernel,
-        out_shape=[jax.ShapeDtypeStruct((GMAX, BS, K), F32)] * 4
-        + [jax.ShapeDtypeStruct((LIST_SIZE,), jnp.int32)] * 2,
-        in_specs=[smem] * 2 + [hbm] * 4,
-        out_specs=[anywhere] * 4 + [smem] * 2,
+        out_shape=[jax.ShapeDtypeStruct((GMAX, BS, K), F32)] * 4,
+        in_specs=[smem] + [hbm] * 3,
+        out_specs=[anywhere] * 4,
         scratch_shapes=[
-            *[pltpu.SMEM(a.shape, jnp.int32) for a in arrays[:3]],
+            *[pltpu.SMEM(a.shape, jnp.int32) for a in arrays[:2]],
             pltpu.VMEM((4, GMAX, BS, K), F32),
-            pltpu.SemaphoreType.DMA((3,)),
+            pltpu.SemaphoreType.DMA((2,)),
             pltpu.SemaphoreType.DMA((4, GMAX)),
             pltpu.SemaphoreType.DMA((4, GMAX)),
         ],
         compiler_params=pltpu.CompilerParams(vmem_limit_bytes=4 * MB),
         cost_estimate=pl.CostEstimate(flops=0, bytes_accessed=4 * MB, transcendentals=0),
         name="prepare",
-    )(parity, live, *[pltpu.with_memory_space_constraint(a, pltpu.HBM) for a in arrays])
-    return outs[:4], outs[4:]
+    )(parity, *[pltpu.with_memory_space_constraint(a, pltpu.HBM) for a in arrays])
 
 
 def add_chunk(start, size, pairs, tiles, xh, xl, acc):
@@ -211,13 +208,14 @@
         acc[at] += dot(th, bh) + dot(tl, bh) + dot(th, bl)
 
 
-def own_kernel(pairs, own, tiles, part, held, xh, xl, sems):
+def own_kernel(parity, cols, live, own, tiles, part, held, ghost_pairs, xh, xl, pairs, sems):
     def fetch(row):
         rows = pl.ds(row * TPR, TPR)
         return pltpu.make_async_copy(tiles.at[rows], held.at[rows], sems.at[row])
 
     for row in range(AHEAD):
         fetch(row).start()
+    pair_lists(parity, cols, live, pairs, ghost_pairs)
     xh[NBD * BS :] = jnp.zeros((BS, K), BF16)
     xl[NBD * BS :] = jnp.zeros((BS, K), BF16)
 
@@ -251,22 +249,28 @@
     lax.fori_loop(ready, NBD, arrive, 0)
 
 
-def apply_own(pairs, own, tiles):
+def apply_own(parity, cols, live, own, tiles):
+    smem = pl.BlockSpec(memory_space=pltpu.SMEM)
     vmem = pl.BlockSpec(memory_space=pltpu.VMEM)
     return pl.pallas_call(
         own_kernel,
-        out_shape=[pltpu.VMEM((NBD * BS, K), F32), pltpu.VMEM((NBD * TPR, BS, BS), F32)],
-        in_specs=[pl.BlockSpec(memory_space=pltpu.SMEM), vmem, pl.BlockSpec(memory_space=pltpu.HBM)],
-        out_specs=[vmem] * 2,
+        out_shape=[
+            pltpu.VMEM((NBD * BS, K), F32),
+            pltpu.VMEM((NBD * TPR, BS, BS), F32),
+            jax.ShapeDtypeStruct((LIST_SIZE,), jnp.int32),
+        ],
+        in_specs=[smem] * 3 + [vmem, pl.BlockSpec(memory_space=pltpu.HBM)],
+        out_specs=[vmem, vmem, smem],
         scratch_shapes=[
             pltpu.VMEM(((NBD + 1) * BS, K), BF16),
             pltpu.VMEM(((NBD + 1) * BS, K), BF16),
+            pltpu.SMEM((LIST_SIZE,), jnp.int32),
             pltpu.SemaphoreType.DMA((NBD,)),
         ],
         compiler_params=pltpu.CompilerParams(vmem_limit_bytes=8 * MB),
         cost_estimate=pl.CostEstimate(flops=4 * 10**9, bytes_accessed=25 * MB, transcendentals=0),
         name="apply_own",
-    )(pairs, on_vmem(own), pltpu.with_memory_space_constraint(tiles, pltpu.HBM))
+    )(parity, cols, live, on_vmem(own), pltpu.with_memory_space_constraint(tiles, pltpu.HBM))
 
 
 def gram_pack(high, low):
@@ -516,14 +520,12 @@
 def body(block_vectors, stiff_tiles, col_index, send_lists, send_counts, part_blocks):
     parity = jnp.stack([lax.axis_index("px") % 2, lax.axis_index("py") % 2]).astype(jnp.int32)
     tiles = stiff_tiles.reshape(NBD * TPR, BS, BS)
-    (px_odd, px_even, py_odd, py_even), (own_pairs, ghost_pairs) = prepare(
-        parity, send_lists, send_counts, col_index.T, part_blocks, block_vectors
-    )
+    px_odd, px_even, py_odd, py_even = prepare(parity, send_lists, send_counts, block_vectors)
     px_odd = swapped(px_odd, "px", True)
     py_even = swapped(py_even, "py", False)
     px_even = swapped(px_even, "px", False)
     py_odd = swapped(py_odd, "py", True)
-    part, held = apply_own(own_pairs, block_vectors, tiles)
+    part, held, ghost_pairs = apply_own(parity, col_index.T, part_blocks, block_vectors, tiles)
     ah, al, gram = apply_ghosts(ghost_pairs, part, held, [px_even, px_odd, py_even, py_odd])
     low, high = sum_everywhere(gram)
     return tuple(orthonormalize(low, high, ah, al))

time: 79.1 us -> 79.8 us (level)
  Pallas kernels: 33 us -> 34.1 us
    pallas_call x1, Pallas kernels: 8.14 us -> 10.3 us  [apply_own(): pl.pallas_call(own_kernel, out_shape=[pltpu.VMEM((NBD * BS, K), F32), plt...]
    pallas_call x1, Pallas kernels: 5.03 us -> 3.95 us  [prepare(): pl.pallas_call(prepare_kernel, out_shape=[jax.ShapeDtypeStruct((GMAX, BS,...]
  transfers between devices with their start and end apart: 15 -> 15, of which waited for: 9 -> 9; matrix products, arithmetic and copies ran while one was open for 0% -> 0% of each run, Pallas kernels for 10% -> 13%
where the time goes in v6:
time: 79.8 us
  Pallas kernels  34.1 us (43%)
  starting transfers between devices  30.5 us (38%)
  waiting for transfers between devices  13.5 us (17%)
  between operations  1.59 us (2%)
    ppermute x9, starting transfers between devices, sum_everywhere(): near, wrap, far = [lax.ppermute(total, AXES, r) for r in routes]  15.8 us
    pallas_call x1, Pallas kernels, orthonormalize(): pl.pallas_call(basis_kernel, out_shape=[jax.ShapeDtypeStruct((NBD * BS, K...  12 us
    ppermute x9, waiting for transfers between devices, sum_everywhere(): near, wrap, far = [lax.ppermute(total, AXES, r) for r in routes]  11.6 us
    pallas_call x1, Pallas kernels, apply_own(): pl.pallas_call(own_kernel, out_shape=[pltpu.VMEM((NBD * BS, K), F32), plt...  10.3 us
    ppermute x4, starting transfers between devices, swapped(): return lax.ppermute(block, axis, pairs + [(j, i) for i, j in pairs])  8.37 us
    pallas_call x1, Pallas kernels, apply_ghosts(): pl.pallas_call(ghost_kernel, out_shape=[pltpu.VMEM((NBD * BS, K), F32), p...  7.86 us
    ppermute x1, starting transfers between devices, sum_everywhere(): theirs = lax.ppermute(total, AXES, CORE_ROUTE)  4.58 us
    pallas_call x1, Pallas kernels, prepare(): pl.pallas_call(prepare_kernel, out_shape=[jax.ShapeDtypeStruct((GMAX, BS,...  3.95 us
  transfers between devices with their start and end apart: 15, of which 9 were waited for; matrix products, arithmetic and copies ran while one was open for 0% of the time, Pallas kernels for 13%

profile of v6, /device:TPU:1, one launch (start us, length us, event | category | flops | bytes accessed | tf_op | source)
XLA Modules:
  0.0 79.8 jit_solution(5064900962992430570)
XLA Ops:
  0.6 0.0 copy-start
  0.7 0.1 pad_add_fusion.parity
  0.7 3.9 %prepare.1 = (f32[4,128,256]{2,1,0:T(8,128)}, f32[4,128,256]{2,1,0:T(8,128)}, f32[4,128,256]{2,1,0:T(8,128)}, f32[4,128,256]{2,1,0:T(8,128)}) custom-call(s32[2]{0:T(128)S(1)} %pad_add_fusion.parity, s32[1,4,4]{2,1,0:T(4,128)} %lists_in.1, s32[1,4]{1,0:T(1,128)} %counts_in.1, f32[3072,256]{1,0:T(8,128)} %own.3), custom_call_target="tpu_custom_call" | custom-call | bytes 4194304 | tf_op jit(solution)/shard_map/prepare/pallas_call | solution.py:178
  4.7 2.5 %collective-permute-start = (f32[4,128,256]{2,1,0:T(8,128)}, f32[4,128,256]{2,1,0:T(8,128)}, u32[]{:S(2)}, u32[]{:S(2)}) collective-permute-start(f32[4,128,256]{2,1,0:T(8,128)} %get-tuple-element.15), channel_id=1, source_target_pairs={{0,8},{16,24},{32,40},{48,56},{64,72},{80,88},{96,104},{112,120},{... | collective-permute-start | bytes 1572872 | tf_op jit(solution)/shard_map/ppermute | solution.py:73
  7.2 1.4 %collective-permute-start.1 = (f32[4,128,256]{2,1,0:T(8,128)}, f32[4,128,256]{2,1,0:T(8,128)}, u32[]{:S(2)}, u32[]{:S(2)}) collective-permute-start(f32[4,128,256]{2,1,0:T(8,128)} %get-tuple-element.16), channel_id=1, source_target_pairs={{8,16},{24,32},{40,48},{56,64},{72,80},{88,96},{104,112},{16,8},{3... | collective-permute-start | bytes 1572872 | tf_op jit(solution)/shard_map/ppermute | solution.py:73
  8.6 1.1 %collective-permute-start.2 = (f32[4,128,256]{2,1,0:T(8,128)}, f32[4,128,256]{2,1,0:T(8,128)}, u32[]{:S(2)}, u32[]{:S(2)}) collective-permute-start(f32[4,128,256]{2,1,0:T(8,128)} %get-tuple-element.17), channel_id=1, source_target_pairs={{0,1},{2,3},{4,5},{6,7},{1,0},{3,2},{5,4},{7,6},{8,9},{10,11},{12,... | collective-permute-start | bytes 1572872 | tf_op jit(solution)/shard_map/ppermute | solution.py:73
  9.7 3.3 %collective-permute-start.3 = (f32[4,128,256]{2,1,0:T(8,128)}, f32[4,128,256]{2,1,0:T(8,128)}, u32[]{:S(2)}, u32[]{:S(2)}) collective-permute-start(f32[4,128,256]{2,1,0:T(8,128)} %get-tuple-element.18), channel_id=1, source_target_pairs={{1,2},{3,4},{5,6},{2,1},{4,3},{6,5},{9,10},{11,12},{13,14},{10,9},... | collective-permute-start | bytes 1572872 | tf_op jit(solution)/shard_map/ppermute | solution.py:73
  13.8 10.3 %apply_own.1 = (f32[3072,256]{1,0:T(8,128)S(1)}, f32[288,128,128]{2,1,0:T(8,128)S(1)}, s32[376]{0:T(512)S(1)}) custom-call(s32[2]{0:T(128)S(1)} %pad_add_fusion.parity, s32[12,24]{1,0:T(8,128)S(1)} %bitcast.4, s32[1]{0:T(128)S(6)} %copy.10.live, f32[3072,256]{1,0:T(8,128)S(1)} %copy-done, f32[288,128,128]{2,1,0:T(8,128)} %bitcast.5), custom_call_target="tpu_custom_call" | custom-call | flops 4000000000 | bytes 26214400 | tf_op jit(solution)/shard_map/apply_own/pallas_call | solution.py:255
  24.1 0.0 collective-permute-done.1.g1
  24.1 7.9 %apply_ghosts.1 = (f32[3072,256]{1,0:T(8,128)S(1)}, bf16[3072,256]{1,0:T(8,128)(2,1)}, bf16[3072,256]{1,0:T(8,128)(2,1)}, f32[272,128]{1,0:T(8,128)S(1)}) custom-call(s32[376]{0:T(512)S(1)} %get-tuple-element.12.pairs, f32[3072,256]{1,0:T(8,128)S(1)} %get-tuple-element.13._, ...), custom_call_target="tpu_custom_call", output_to_operand_aliasing={{0}: (1, {})} | custom-call | flops 3000000000 | bytes 26214400 | tf_op jit(solution)/shard_map/apply_ghosts/pallas_call | solution.py:330
  32.0 1.7 %collective-permute-start.4 = (f32[136,128]{1,0:T(8,128)S(1)}, f32[136,128]{1,0:T(8,128)S(1)}, u32[]{:S(2)}, u32[]{:S(2)}) collective-permute-start(f32[136,128]{1,0:T(8,128)S(1)} %constant_dynamic-slice_fusion), channel_id=1, source_target_pairs={{0,1},{1,0},{2,3},{3,2},{4,5},{5,4},{6,7},{7,6},{32,33},{33,32},{3... | collective-permute-start | bytes 208904 | tf_op jit(solution)/shard_map/ppermute | solution.py:80
  33.8 0.9 %collective-permute-done.4 = f32[136,128]{1,0:T(8,128)S(1)} collective-permute-done((f32[136,128]{1,0:T(8,128)S(1)}, f32[136,128]{1,0:T(8,128)S(1)}, u32[]{:S(2)}, u32[]{:S(2)}) %collective-permute-start.4) | collective-permute-done | bytes 69664 | tf_op jit(solution)/shard_map/ppermute | solution.py:80
  34.7 2.1 %collective-permute-start.5 = (f32[136,128]{1,0:T(8,128)S(1)}, f32[136,128]{1,0:T(8,128)S(1)}, u32[]{:S(2)}, u32[]{:S(2)}) collective-permute-start(f32[136,128]{1,0:T(8,128)S(1)} %dynamic-slice_add_fusion), channel_id=1, source_target_pairs={{0,8},{1,9},{2,10},{3,11},{4,12},{5,13},{6,14},{7,15},{32,40},{33,... | collective-permute-start | bytes 208904 | tf_op jit(solution)/shard_map/ppermute | solution.py:83
  36.8 4.2 %collective-permute-start.6 = (f32[136,128]{1,0:T(8,128)S(1)}, f32[136,128]{1,0:T(8,128)S(1)}, u32[]{:S(2)}, u32[]{:S(2)}) collective-permute-start(f32[136,128]{1,0:T(8,128)S(1)} %dynamic-slice_add_fusion), channel_id=1, source_target_pairs={{0,24},{1,25},{2,26},{3,27},{4,28},{5,29},{6,30},{7,31},{32,56},{3... | collective-permute-start | bytes 208904 | tf_op jit(solution)/shard_map/ppermute | solution.py:83
  41.0 1.1 %collective-permute-start.7 = (f32[136,128]{1,0:T(8,128)S(1)}, f32[136,128]{1,0:T(8,128)S(1)}, u32[]{:S(2)}, u32[]{:S(2)}) collective-permute-start(f32[136,128]{1,0:T(8,128)S(1)} %dynamic-slice_add_fusion), channel_id=1, source_target_pairs={{0,16},{1,17},{2,18},{3,19},{4,20},{5,21},{6,22},{7,23},{32,48},{3... | collective-permute-start | bytes 208904 | tf_op jit(solution)/shard_map/ppermute | solution.py:83
  42.1 0.0 collective-permute-done.5
  42.1 1.3 %collective-permute-done.6 = f32[136,128]{1,0:T(8,128)S(1)} collective-permute-done((f32[136,128]{1,0:T(8,128)S(1)}, f32[136,128]{1,0:T(8,128)S(1)}, u32[]{:S(2)}, u32[]{:S(2)}) %collective-permute-start.6) | collective-permute-done | bytes 69664 | tf_op jit(solution)/shard_map/ppermute | solution.py:83
  43.4 2.3 %collective-permute-done.7 = f32[136,128]{1,0:T(8,128)S(1)} collective-permute-done((f32[136,128]{1,0:T(8,128)S(1)}, f32[136,128]{1,0:T(8,128)S(1)}, u32[]{:S(2)}, u32[]{:S(2)}) %collective-permute-start.7) | collective-permute-done | bytes 69664 | tf_op jit(solution)/shard_map/ppermute | solution.py:83
  45.7 3.4 %collective-permute-start.10 = (f32[136,128]{1,0:T(8,128)S(1)}, f32[136,128]{1,0:T(8,128)S(1)}, u32[]{:S(2)}, u32[]{:S(2)}) collective-permute-start(f32[136,128]{1,0:T(8,128)S(1)} %add_add_fusion.2), channel_id=1, source_target_pairs={{0,64},{1,65},{2,66},{3,67},{4,68},{5,69},{6,70},{7,71},{32,96},{3... | collective-permute-start | bytes 208904 | tf_op jit(solution)/shard_map/ppermute | solution.py:83
  49.0 0.8 collective-permute-start.8
  49.8 0.6 collective-permute-start.9
  50.4 0.3 collective-permute-done.10
  50.7 1.9 %collective-permute-done.8 = f32[136,128]{1,0:T(8,128)S(1)} collective-permute-done((f32[136,128]{1,0:T(8,128)S(1)}, f32[136,128]{1,0:T(8,128)S(1)}, u32[]{:S(2)}, u32[]{:S(2)}) %collective-permute-start.8) | collective-permute-done | bytes 69664 | tf_op jit(solution)/shard_map/ppermute | solution.py:83
  52.6 1.6 %collective-permute-done.9 = f32[136,128]{1,0:T(8,128)S(1)} collective-permute-done((f32[136,128]{1,0:T(8,128)S(1)}, f32[136,128]{1,0:T(8,128)S(1)}, u32[]{:S(2)}, u32[]{:S(2)}) %collective-permute-start.9) | collective-permute-done | bytes 69664 | tf_op jit(solution)/shard_map/ppermute | solution.py:83
  54.2 1.4 %collective-permute-start.11 = (f32[136,128]{1,0:T(8,128)S(1)}, f32[136,128]{1,0:T(8,128)S(1)}, u32[]{:S(2)}, u32[]{:S(2)}) collective-permute-start(f32[136,128]{1,0:T(8,128)S(1)} %add_add_fusion.1), channel_id=1, source_target_pairs={{0,2},{1,3},{2,0},{3,1},{4,6},{5,7},{6,4},{7,5},{32,34},{33,35},{3... | collective-permute-start | bytes 208904 | tf_op jit(solution)/shard_map/ppermute | solution.py:83
  55.6 1.6 %collective-permute-start.12 = (f32[136,128]{1,0:T(8,128)S(1)}, f32[136,128]{1,0:T(8,128)S(1)}, u32[]{:S(2)}, u32[]{:S(2)}) collective-permute-start(f32[136,128]{1,0:T(8,128)S(1)} %add_add_fusion.1), channel_id=1, source_target_pairs={{0,6},{1,7},{2,4},{3,5},{4,2},{5,3},{6,0},{7,1},{32,38},{33,39},{3... | collective-permute-start | bytes 208904 | tf_op jit(solution)/shard_map/ppermute | solution.py:83
  57.3 0.6 collective-permute-start.13
  57.8 2.1 %collective-permute-done.12 = f32[136,128]{1,0:T(8,128)S(1)} collective-permute-done((f32[136,128]{1,0:T(8,128)S(1)}, f32[136,128]{1,0:T(8,128)S(1)}, u32[]{:S(2)}, u32[]{:S(2)}) %collective-permute-start.12) | collective-permute-done | bytes 69664 | tf_op jit(solution)/shard_map/ppermute | solution.py:83
  60.0 2.1 %collective-permute-done.13 = f32[136,128]{1,0:T(8,128)S(1)} collective-permute-done((f32[136,128]{1,0:T(8,128)S(1)}, f32[136,128]{1,0:T(8,128)S(1)}, u32[]{:S(2)}, u32[]{:S(2)}) %collective-permute-start.13) | collective-permute-done | bytes 69664 | tf_op jit(solution)/shard_map/ppermute | solution.py:83
  62.2 4.6 %collective-permute-start.14 = (f32[136,128]{1,0:T(8,128)S(1)}, f32[136,128]{1,0:T(8,128)S(1)}, u32[]{:S(2)}, u32[]{:S(2)}) collective-permute-start(f32[136,128]{1,0:T(8,128)S(1)} %add_add_fusion), channel_id=1, source_target_pairs={{0,1},{1,0},{2,3},{3,2},{4,5},{5,4},{6,7},{7,6},{32,33},{33,32},{3... | collective-permute-start | bytes 208904 | tf_op jit(solution)/shard_map/ppermute | solution.py:85
  66.7 0.9 %collective-permute-done.14 = f32[136,128]{1,0:T(8,128)S(1)} collective-permute-done((f32[136,128]{1,0:T(8,128)S(1)}, f32[136,128]{1,0:T(8,128)S(1)}, u32[]{:S(2)}, u32[]{:S(2)}) %collective-permute-start.14) | collective-permute-done | bytes 69664 | tf_op jit(solution)/shard_map/ppermute | solution.py:85
  67.7 12.0 %factor_and_basis.1 = (f32[3072,256]{1,0:T(8,128)}, f32[256,256]{1,0:T(8,128)}) custom-call(f32[136,128]{1,0:T(8,128)S(1)} %get-tuple-element.23.low, f32[136,128]{1,0:T(8,128)S(1)} %get-tuple-element.22.high, bf16[3072,256]{1,0:T(8,128)(2,1)} %get-tuple-element.20.rows_high, bf16[3072,256]{1,0:T(8,128)(2,1)} %get-tuple-element.21.rows_low), custom_call_target="tpu_custom_call" | custom-call | flops 1000000000 | bytes 7340032 | tf_op jit(solution)/shard_map/factor_and_basis/pallas_call | solution.py:497
  (13 shorter events, 0.1 us)
Async XLA Ops:
  0.6 13.1 %copy-start = (f32[3072,256]{1,0:T(8,128)S(1)}, f32[3072,256]{1,0:T(8,128)}, u32[]{:S(2)}) copy-start(f32[3072,256]{1,0:T(8,128)} %own.3) | copy-start | bytes 9437188
  0.6 13.1 %copy-start.1 = (s32[24,12]{0,1:T(8,128)S(1)}, s32[24,12]{0,1:T(8,128)}, u32[]{:S(2)}) copy-start(s32[24,12]{0,1:T(8,128)} %param.8) | copy-start | bytes 3460
  4.7 19.4 %collective-permute-start = (f32[4,128,256]{2,1,0:T(8,128)}, f32[4,128,256]{2,1,0:T(8,128)}, u32[]{:S(2)}, u32[]{:S(2)}) collective-permute-start(f32[4,128,256]{2,1,0:T(8,128)} %get-tuple-element.15), channel_id=1, source_target_pairs={{0,8},{16,24},{32,40},{48,56},{64,72},{80,88},{96,104},{112,120},{... | collective-permute-start | bytes 1572872 | tf_op jit(solution)/shard_map/ppermute | solution.py:73
  7.2 16.9 %collective-permute-start.1 = (f32[4,128,256]{2,1,0:T(8,128)}, f32[4,128,256]{2,1,0:T(8,128)}, u32[]{:S(2)}, u32[]{:S(2)}) collective-permute-start(f32[4,128,256]{2,1,0:T(8,128)} %get-tuple-element.16), channel_id=1, source_target_pairs={{8,16},{24,32},{40,48},{56,64},{72,80},{88,96},{104,112},{16,8},{3... | collective-permute-start | bytes 1572872 | tf_op jit(solution)/shard_map/ppermute | solution.py:73
  8.6 15.5 %collective-permute-start.2 = (f32[4,128,256]{2,1,0:T(8,128)}, f32[4,128,256]{2,1,0:T(8,128)}, u32[]{:S(2)}, u32[]{:S(2)}) collective-permute-start(f32[4,128,256]{2,1,0:T(8,128)} %get-tuple-element.17), channel_id=1, source_target_pairs={{0,1},{2,3},{4,5},{6,7},{1,0},{3,2},{5,4},{7,6},{8,9},{10,11},{12,... | collective-permute-start | bytes 1572872 | tf_op jit(solution)/shard_map/ppermute | solution.py:73
  9.7 14.4 %collective-permute-start.3 = (f32[4,128,256]{2,1,0:T(8,128)}, f32[4,128,256]{2,1,0:T(8,128)}, u32[]{:S(2)}, u32[]{:S(2)}) collective-permute-start(f32[4,128,256]{2,1,0:T(8,128)} %get-tuple-element.18), channel_id=1, source_target_pairs={{1,2},{3,4},{5,6},{2,1},{4,3},{6,5},{9,10},{11,12},{13,14},{10,9},... | collective-permute-start | bytes 1572872 | tf_op jit(solution)/shard_map/ppermute | solution.py:73
  32.0 2.7 %collective-permute-start.4 = (f32[136,128]{1,0:T(8,128)S(1)}, f32[136,128]{1,0:T(8,128)S(1)}, u32[]{:S(2)}, u32[]{:S(2)}) collective-permute-start(f32[136,128]{1,0:T(8,128)S(1)} %constant_dynamic-slice_fusion), channel_id=1, source_target_pairs={{0,1},{1,0},{2,3},{3,2},{4,5},{5,4},{6,7},{7,6},{32,33},{33,32},{3... | collective-permute-start | bytes 208904 | tf_op jit(solution)/shard_map/ppermute | solution.py:80
  34.7 7.4 %collective-permute-start.5 = (f32[136,128]{1,0:T(8,128)S(1)}, f32[136,128]{1,0:T(8,128)S(1)}, u32[]{:S(2)}, u32[]{:S(2)}) collective-permute-start(f32[136,128]{1,0:T(8,128)S(1)} %dynamic-slice_add_fusion), channel_id=1, source_target_pairs={{0,8},{1,9},{2,10},{3,11},{4,12},{5,13},{6,14},{7,15},{32,40},{33,... | collective-permute-start | bytes 208904 | tf_op jit(solution)/shard_map/ppermute | solution.py:83
  36.8 6.6 %collective-permute-start.6 = (f32[136,128]{1,0:T(8,128)S(1)}, f32[136,128]{1,0:T(8,128)S(1)}, u32[]{:S(2)}, u32[]{:S(2)}) collective-permute-start(f32[136,128]{1,0:T(8,128)S(1)} %dynamic-slice_add_fusion), channel_id=1, source_target_pairs={{0,24},{1,25},{2,26},{3,27},{4,28},{5,29},{6,30},{7,31},{32,56},{3... | collective-permute-start | bytes 208904 | tf_op jit(solution)/shard_map/ppermute | solution.py:83
  41.0 4.7 %collective-permute-start.7 = (f32[136,128]{1,0:T(8,128)S(1)}, f32[136,128]{1,0:T(8,128)S(1)}, u32[]{:S(2)}, u32[]{:S(2)}) collective-permute-start(f32[136,128]{1,0:T(8,128)S(1)} %dynamic-slice_add_fusion), channel_id=1, source_target_pairs={{0,16},{1,17},{2,18},{3,19},{4,20},{5,21},{6,22},{7,23},{32,48},{3... | collective-permute-start | bytes 208904 | tf_op jit(solution)/shard_map/ppermute | solution.py:83
  45.7 5.1 %collective-permute-start.10 = (f32[136,128]{1,0:T(8,128)S(1)}, f32[136,128]{1,0:T(8,128)S(1)}, u32[]{:S(2)}, u32[]{:S(2)}) collective-permute-start(f32[136,128]{1,0:T(8,128)S(1)} %add_add_fusion.2), channel_id=1, source_target_pairs={{0,64},{1,65},{2,66},{3,67},{4,68},{5,69},{6,70},{7,71},{32,96},{3... | collective-permute-start | bytes 208904 | tf_op jit(solution)/shard_map/ppermute | solution.py:83
  49.0 3.6 %collective-permute-start.8 = (f32[136,128]{1,0:T(8,128)S(1)}, f32[136,128]{1,0:T(8,128)S(1)}, u32[]{:S(2)}, u32[]{:S(2)}) collective-permute-start(f32[136,128]{1,0:T(8,128)S(1)} %add_add_fusion.2), channel_id=1, source_target_pairs={{0,32},{1,33},{2,34},{3,35},{4,36},{5,37},{6,38},{7,39},{32,0},{33... | collective-permute-start | bytes 208904 | tf_op jit(solution)/shard_map/ppermute | solution.py:83
  49.8 4.4 %collective-permute-start.9 = (f32[136,128]{1,0:T(8,128)S(1)}, f32[136,128]{1,0:T(8,128)S(1)}, u32[]{:S(2)}, u32[]{:S(2)}) collective-permute-start(f32[136,128]{1,0:T(8,128)S(1)} %add_add_fusion.2), channel_id=1, source_target_pairs={{0,96},{1,97},{2,98},{3,99},{4,100},{5,101},{6,102},{7,103},{32,64... | collective-permute-start | bytes 208904 | tf_op jit(solution)/shard_map/ppermute | solution.py:83
  54.2 3.7 %collective-permute-start.11 = (f32[136,128]{1,0:T(8,128)S(1)}, f32[136,128]{1,0:T(8,128)S(1)}, u32[]{:S(2)}, u32[]{:S(2)}) collective-permute-start(f32[136,128]{1,0:T(8,128)S(1)} %add_add_fusion.1), channel_id=1, source_target_pairs={{0,2},{1,3},{2,0},{3,1},{4,6},{5,7},{6,4},{7,5},{32,34},{33,35},{3... | collective-permute-start | bytes 208904 | tf_op jit(solution)/shard_map/ppermute | solution.py:83
  55.6 4.4 %collective-permute-start.12 = (f32[136,128]{1,0:T(8,128)S(1)}, f32[136,128]{1,0:T(8,128)S(1)}, u32[]{:S(2)}, u32[]{:S(2)}) collective-permute-start(f32[136,128]{1,0:T(8,128)S(1)} %add_add_fusion.1), channel_id=1, source_target_pairs={{0,6},{1,7},{2,4},{3,5},{4,2},{5,3},{6,0},{7,1},{32,38},{33,39},{3... | collective-permute-start | bytes 208904 | tf_op jit(solution)/shard_map/ppermute | solution.py:83
  57.3 4.9 %collective-permute-start.13 = (f32[136,128]{1,0:T(8,128)S(1)}, f32[136,128]{1,0:T(8,128)S(1)}, u32[]{:S(2)}, u32[]{:S(2)}) collective-permute-start(f32[136,128]{1,0:T(8,128)S(1)} %add_add_fusion.1), channel_id=1, source_target_pairs={{0,4},{1,5},{2,6},{3,7},{4,0},{5,1},{6,2},{7,3},{32,36},{33,37},{3... | collective-permute-start | bytes 208904 | tf_op jit(solution)/shard_map/ppermute | solution.py:83
  62.2 5.5 %collective-permute-start.14 = (f32[136,128]{1,0:T(8,128)S(1)}, f32[136,128]{1,0:T(8,128)S(1)}, u32[]{:S(2)}, u32[]{:S(2)}) collective-permute-start(f32[136,128]{1,0:T(8,128)S(1)} %add_add_fusion), channel_id=1, source_target_pairs={{0,1},{1,0},{2,3},{3,2},{4,5},{5,4},{6,7},{7,6},{32,33},{33,32},{3... | collective-permute-start | bytes 208904 | tf_op jit(solution)/shard_map/ppermute | solution.py:85
